TPU v7x, 32 devices: a whole 2x2x4 slice. The times are simulated.
32 devices in a mesh: gx: 8 (over z, x), gy: 4 (over y, core).
Axes of the slice: x: 2, y: 2, z: 4, core: 2. Of those that a mesh axis runs over, the one named last changes fastest.
Arguments:
- vel0: bfloat16 [2, 2048, 1024], P(None, 'gx', 'gy'), may hold values from -6 to 6
- visc: float32 [2048, 1024], P('gx', 'gy'), may hold values from 0.1 to 1
- fric: float32 [2048, 1024], P('gx', 'gy'), may hold values from 0.5 to 5
- drive: bfloat16 [2, 2048, 1024], P(None, 'gx', 'gy'), may hold values from -6 to 6
- scene_obs: bfloat16 [4, 128, 2, 128, 128], P('gy', 'gx'), may hold values from -6 to 6
- scene_weight: bfloat16 [4, 128], P('gy', 'gx'), may hold values from 0.5 to 4
- scene_owner: int32 [4, 128, 1], P('gy', 'gx'), may hold values from 0 to 7; in each aligned block of 16 rows (0 to 15, 16 to 31, ..., all dimensions but the last counted through in order) at most 2 rows name the same one
- scene_slot: int32 [4, 128], P('gy', 'gx'), may hold values from 0 to 3
- ice_mask: int32 [16, 8], P('gx', 'gy'), may hold values 0 or 1
Outputs:
- grad_fric: float32 [2048, 1024], P('gx', 'gy')
Inputs may be any that keep to these rules, and one draw needn't show every extreme that they name: `scene_owner`: among one device's 16 scenes at most 2 name the same owner, and in some device one owner is named exactly 2 times.
All inputs are finite; a program needn't handle non-finite values. No bound on the sum of `ice_mask` on one device may be relied on, other than what follows from the above.
Results may differ from a plain program's by a relative error of at most 0.0003.
Values may be sent and summed in bfloat16 or wider, within the bound.
No kernel may reach another device: no remote copies, remote signals or barrier semaphores. Data moves between devices by JAX's collectives and lax.ppermute only.
A program may use at most 64 MiB of HBM per device.

v0:
```python
import jax
import jax.numpy as jnp
from jax import lax
from jax.sharding import PartitionSpec as P

CAP = 2


OMEGA = 0.6


def from_behind(value, axis, steps):
    count = lax.axis_size(axis)
    first, last = (max(0, -steps), min(count, count - steps))
    return lax.ppermute(value, axis, [(source, source + steps) for source in range(first, last)])


def stress_image(field, visc):
    above_x = from_behind(field[:, :1, :], "gx", -1)
    above_y = from_behind(field[:, :, :1], "gy", -1)
    along_x = jnp.concatenate([field[:, 1:, :], above_x], axis=1) - field
    along_y = jnp.concatenate([field[:, :, 1:], above_y], axis=2) - field
    sxx = visc * (4.0 * along_x[0] + 2.0 * along_y[1])
    syy = visc * (4.0 * along_y[1] + 2.0 * along_x[0])
    sxy = visc * (along_y[0] + along_x[1])
    below_x = from_behind(jnp.stack([sxx[-1], sxy[-1]]), "gx", 1)
    below_y = from_behind(jnp.stack([sxy[:, -1], syy[:, -1]]), "gy", 1)
    push_u = (
        jnp.concatenate([below_x[0:1], sxx[:-1]], axis=0)
        - sxx
        + jnp.concatenate([below_y[0][:, None], sxy[:, :-1]], axis=1)
        - sxy
    )
    push_v = (
        jnp.concatenate([below_x[1:2], sxy[:-1]], axis=0)
        - sxy
        + jnp.concatenate([below_y[1][:, None], syy[:, :-1]], axis=1)
        - syy
    )
    return jnp.stack([push_u, push_v])


def spread_tiles(values, tiles_x, tiles_y, tile):
    wide = jnp.broadcast_to(values.reshape(tiles_x, 1, tiles_y, 1), (tiles_x, tile, tiles_y, tile))
    return wide.reshape(tiles_x * tile, tiles_y * tile)


def body(vel0, visc, fric, drive, scene_obs, scene_weight, scene_owner, scene_slot, ice_mask):
    cells_x, cells_y = visc.shape
    tile = scene_obs.shape[-1]
    tiles_x = cells_x // tile
    tiles_y = cells_y // tile
    slot_count = tiles_x * tiles_y
    visc_row = from_behind(visc[-1:, :], "gx", 1)
    visc_col = from_behind(visc[:, -1:], "gy", 1)
    visc_x = jnp.concatenate([visc_row, visc[:-1]], axis=0)
    visc_y = jnp.concatenate([visc_col, visc[:, :-1]], axis=1)
    diag = jnp.stack([5.0 * visc + 4.0 * visc_x + visc_y, 5.0 * visc + visc_x + 4.0 * visc_y])
    relax = 1.0 / (diag + fric)
    owners = scene_owner[0, :, 0]
    slots = scene_slot[0]
    weights = scene_weight[0]
    observed = scene_obs[0]
    count = owners.shape[0]
    groups = lax.axis_size("gx")
    places = groups * CAP
    order = jnp.arange(count, dtype=jnp.int32)
    same_owner = owners[:, None] == owners[None, :]
    earlier = order[None, :] < order[:, None]
    rank = jnp.sum(jnp.logical_and(same_owner, earlier), axis=1)
    target = owners * CAP + rank
    place_mask = target[None, :] == jnp.arange(places, dtype=jnp.int32)[:, None]
    place_table = place_mask.astype(jnp.bfloat16)
    obs_buffer = jnp.dot(
        place_table, observed.reshape(count, -1), preferred_element_type=jnp.float32
    )
    obs_buffer = obs_buffer.astype(jnp.bfloat16)
    weight_buffer = jnp.dot(place_table, weights[:, None], preferred_element_type=jnp.float32)[
        :, 0
    ].astype(jnp.bfloat16)
    slot_buffer = jnp.sum(jnp.where(place_mask, slots[None, :], 0), axis=1)
    slot_range = jnp.arange(slot_count, dtype=jnp.int32)
    start = vel0.astype(jnp.float32)
    force = drive.astype(jnp.float32)
    first_res = force - stress_image(start, visc) - fric * start
    first = start + OMEGA * relax * first_res
    second_res = force - stress_image(first, visc) - fric * first
    second = first + OMEGA * relax * second_res
    got_obs, got_weight, got_slot = (
        lax.all_to_all(
            obs_buffer.reshape(places, 2, tile, tile), "gx", split_axis=0, concat_axis=0, tiled=True
        ),
        lax.all_to_all(weight_buffer, "gx", split_axis=0, concat_axis=0, tiled=True),
        lax.all_to_all(slot_buffer, "gx", split_axis=0, concat_axis=0, tiled=True),
    )
    picker = jnp.where(
        got_slot[:, None] == slot_range[None, :], got_weight[:, None], jnp.zeros((), jnp.bfloat16)
    )
    summed = jnp.dot(
        picker.T, got_obs.reshape(got_obs.shape[0], -1), preferred_element_type=jnp.float32
    )
    tile_weight = jnp.sum(picker.astype(jnp.float32), axis=0)
    obs_sum = (
        summed.reshape(tiles_x, tiles_y, 2, tile, tile)
        .transpose(2, 0, 3, 1, 4)
        .reshape(2, cells_x, cells_y)
    )
    weight_cell = spread_tiles(tile_weight, tiles_x, tiles_y, tile)
    ice = spread_tiles(ice_mask.astype(jnp.float32), tiles_x, tiles_y, tile)
    misfit_grad = ice * (weight_cell * second - obs_sum)
    lift_two = OMEGA * relax * misfit_grad
    back = misfit_grad - stress_image(lift_two, visc) - fric * lift_two
    lift_one = OMEGA * relax * back
    part_one = jnp.sum(lift_one * (relax * first_res + start), axis=0)
    part_two = jnp.sum(lift_two * (relax * second_res + first), axis=0)
    return -ice * (part_one + part_two)


def solution(mesh):
    placed = (
        P(None, "gx", "gy"),
        P("gx", "gy"),
        P("gx", "gy"),
        P(None, "gx", "gy"),
        P("gy", "gx", None, None, None),
        P("gy", "gx"),
        P("gy", "gx", None),
        P("gy", "gx"),
        P("gx", "gy"),
    )
    return jax.shard_map(body, mesh=mesh, in_specs=placed, out_specs=P("gx", "gy"), check_vma=False)
```

profile of v0, /device:TPU:24, one launch (start us, length us, event | category | flops | bytes accessed | tf_op | source)
XLA Modules:
  0.0 119.3 jit_solution(7240960893506759124)
XLA Ops:
  0.0 0.9 convert_reduce_fusion
  0.9 0.7 multiply_add_fusion.2
  1.8 0.7 copy.31
  2.5 6.0 %all-to-all-start.1 = ((bf16[8,2,1]{1,2,0:T(2,128)(2,1)}), bf16[8,2,1]{1,2,0:T(2,128)(2,1)S(1)}, u32[]{:S(2)}, u32[]{:S(2)}) async-start(bf16[8,2,1]{1,2,0:T(2,128)(2,1)} %copy.31), calls=%async_computation.1 | async-start | bytes 8192 | tf_op jit(solution)/shard_map/all_to_all | solution.py:93
  8.5 1.3 %slice.198 = f32[1,256]{1,0:T(1,128)} slice(f32[256,256]{1,0:T(8,128)} %param.10), slice={[255:256], [0:256]} | slice | bytes 2048 | tf_op jit(solution)/shard_map/slice | solution.py:54
  9.8 3.4 %collective-permute-start = (f32[1,256]{1,0:T(1,128)}, f32[1,256]{1,0:T(1,128)}, u32[]{:S(2)}, u32[]{:S(2)}) collective-permute-start(f32[1,256]{1,0:T(1,128)} %slice.198), channel_id=1, source_target_pairs={{0,4},{4,8},{8,12},{12,16},{16,20},{20,24},{24,28},{1,5},{5,9},{9,... | collective-permute-start | bytes 3080 | tf_op jit(solution)/shard_map/ppermute | solution.py:15
  13.2 1.3 %slice.263 = f32[2,1,256]{2,1,0:T(1,128)} slice(bf16[2,256,256]{2,1,0:T(8,128)(2,1)} %param.9), slice={[0:2], [0:1], [0:256]} | slice | bytes 4096 | tf_op jit(solution)/shard_map/slice | solution.py:19
  14.5 3.4 %collective-permute-start.2 = (f32[2,1,256]{2,1,0:T(1,128)}, f32[2,1,256]{2,1,0:T(1,128)}, u32[]{:S(2)}, u32[]{:S(2)}) collective-permute-start(f32[2,1,256]{2,1,0:T(1,128)} %slice.263), channel_id=1, source_target_pairs={{4,0},{8,4},{12,8},{16,12},{20,16},{24,20},{28,24},{5,1},{9,5},{13... | collective-permute-start | bytes 6152 | tf_op jit(solution)/shard_map/ppermute | solution.py:15
  17.9 1.7 %slice.200 = f32[256,1]{1,0:T(8,128)} slice(f32[256,256]{1,0:T(8,128)} %param.10), slice={[0:256], [255:256]} | slice | bytes 2048 | tf_op jit(solution)/shard_map/slice | solution.py:55
  19.5 1.3 %collective-permute-start.1 = (f32[256,1]{1,0:T(8,128)}, f32[256,1]{1,0:T(8,128)S(1)}, u32[]{:S(2)}, u32[]{:S(2)}) collective-permute-start(f32[256,1]{1,0:T(8,128)} %slice.200), channel_id=1, source_target_pairs={{0,1},{1,2},{2,3},{4,5},{5,6},{6,7},{8,9},{9,10},{10,11},{12,13},{... | collective-permute-start | bytes 3080 | tf_op jit(solution)/shard_map/ppermute | solution.py:15
  20.8 0.9 slice.266
  21.7 1.3 %collective-permute-start.3 = (f32[2,256,1]{2,1,0:T(8,128)S(1)}, f32[2,256,1]{2,1,0:T(8,128)S(1)}, u32[]{:S(2)}, u32[]{:S(2)}) collective-permute-start(f32[2,256,1]{2,1,0:T(8,128)S(1)} %slice.266), channel_id=1, source_target_pairs={{1,0},{2,1},{3,2},{5,4},{6,5},{7,6},{9,8},{10,9},{11,10},{13,12},{... | collective-permute-start | bytes 6152 | tf_op jit(solution)/shard_map/ppermute | solution.py:15
  23.0 0.6 multiply_add_fusion.1
  23.8 0.9 slice.262
  24.8 0.7 all_to_all.13
  25.5 0.5 reshape_squeeze.3
  25.9 0.4 fusion
  26.4 1.2 %copy.45 = bf16[2,8,256,128]{3,2,1,0:T(8,128)(2,1)} copy(bf16[2,8,256,128]{3,1,2,0:T(8,128)(2,1)S(1)} %fusion) | data formatting | bytes 2097152
  27.6 5.7 %all-to-all-start = ((s32[8,2,1]{1,2,0:T(1,128)}), s32[8,2,1]{1,2,0:T(1,128)S(1)}, u32[]{:S(2)}, u32[]{:S(2)}) async-start(s32[8,2,1]{1,2,0:T(1,128)} %bitcast.4), calls=%async_computation | async-start | bytes 8192 | tf_op jit(solution)/shard_map/all_to_all | solution.py:94
  33.4 3.1 %all-to-all-done = s32[8,2,1]{1,2,0:T(1,128)S(1)} async-done(((s32[8,2,1]{1,2,0:T(1,128)}), s32[8,2,1]{1,2,0:T(1,128)S(1)}, u32[]{:S(2)}, u32[]{:S(2)}) %all-to-all-start) | async-done | bytes 96 | tf_op jit(solution)/shard_map/all_to_all | solution.py:94
  36.4 6.9 %all-to-all-start.2 = ((bf16[16,2,128,128]{3,2,1,0:T(8,128)(2,1)}), bf16[16,2,128,128]{3,2,1,0:T(8,128)(2,1)S(1)}, u32[]{:S(2)}, u32[]{:S(2)}) async-start(bf16[16,2,128,128]{3,2,1,0:T(8,128)(2,1)} %bitcast.54), calls=%async_computation.2 | async-start | bytes 2097152 | tf_op jit(solution)/shard_map/all_to_all | solution.py:90
  43.3 0.6 broadcast.128
  43.9 0.7 reduce.16
  44.8 0.5 copy-done.23
  45.3 0.9 convert_subtract_fusion.3
  46.3 0.9 add_bitcast_fusion.1
  47.2 0.2 slice_reduce_fusion.4
  47.4 3.1 %collective-permute-start.5 = (f32[2,256]{1,0:T(2,128)S(1)}, f32[2,256]{1,0:T(2,128)S(1)}, u32[]{:S(2)}, u32[]{:S(2)}) collective-permute-start(f32[2,256]{1,0:T(2,128)S(1)} %pad_maximum_fusion.3), channel_id=1, source_target_pairs={{0,1},{1,2},{2,3},{4,5},{5,6},{6,7},{8,9},{9,10},{10,11},{12,13},{... | collective-permute-start | bytes 6152 | tf_op jit(solution)/shard_map/ppermute | solution.py:15
  50.5 3.4 %collective-permute-start.4 = (f32[2,256]{1,0:T(2,128)S(1)}, f32[2,256]{1,0:T(2,128)S(1)}, u32[]{:S(2)}, u32[]{:S(2)}) collective-permute-start(f32[2,256]{1,0:T(2,128)S(1)} %pad_maximum_fusion.2), channel_id=1, source_target_pairs={{0,4},{4,8},{8,12},{12,16},{16,20},{20,24},{24,28},{1,5},{5,9},{9,... | collective-permute-start | bytes 6152 | tf_op jit(solution)/shard_map/ppermute | solution.py:15
  54.2 6.0 %collective-permute-done.4 = f32[2,256]{1,0:T(2,128)S(1)} collective-permute-done((f32[2,256]{1,0:T(2,128)S(1)}, f32[2,256]{1,0:T(2,128)S(1)}, u32[]{:S(2)}, u32[]{:S(2)}) %collective-permute-start.4) | collective-permute-done | bytes 2080 | tf_op jit(solution)/shard_map/ppermute | solution.py:15
  60.3 0.2 fusion.19
  60.5 0.7 copy-done.9
  61.5 1.9 %collective-permute-start.6 = (f32[2,1,256]{2,1,0:T(1,128)S(1)}, f32[2,1,256]{2,1,0:T(1,128)S(1)}, u32[]{:S(2)}, u32[]{:S(2)}) collective-permute-start(f32[2,1,256]{2,1,0:T(1,128)S(1)} %slice.283), channel_id=1, source_target_pairs={{4,0},{8,4},{12,8},{16,12},{20,16},{24,20},{28,24},{5,1},{9,5},{13... | collective-permute-start | bytes 6152 | tf_op jit(solution)/shard_map/ppermute | solution.py:15
  63.5 1.3 %collective-permute-start.7 = (f32[2,256,1]{2,1,0:T(8,128)S(1)}, f32[2,256,1]{2,1,0:T(8,128)S(1)}, u32[]{:S(2)}, u32[]{:S(2)}) collective-permute-start(f32[2,256,1]{2,1,0:T(8,128)S(1)} %slice.286), channel_id=1, source_target_pairs={{1,0},{2,1},{3,2},{5,4},{6,5},{7,6},{9,8},{10,9},{11,10},{13,12},{... | collective-permute-start | bytes 6152 | tf_op jit(solution)/shard_map/ppermute | solution.py:15
  65.1 0.9 copy_bitcast_fusion
  65.9 0.2 slice.285
  66.2 0.8 collective-permute-done.6
  67.5 0.2 slice_reduce_fusion.2
  67.7 6.2 %collective-permute-start.9 = (f32[2,256]{1,0:T(2,128)S(1)}, f32[2,256]{1,0:T(2,128)S(1)}, u32[]{:S(2)}, u32[]{:S(2)}) collective-permute-start(f32[2,256]{1,0:T(2,128)S(1)} %pad_maximum_fusion.5), channel_id=1, source_target_pairs={{0,1},{1,2},{2,3},{4,5},{5,6},{6,7},{8,9},{9,10},{10,11},{12,13},{... | collective-permute-start | bytes 6152 | tf_op jit(solution)/shard_map/ppermute | solution.py:15
  73.9 0.6 pad_maximum_fusion.4
  74.5 3.6 %collective-permute-start.8 = (f32[2,256]{1,0:T(2,128)}, f32[2,256]{1,0:T(2,128)}, u32[]{:S(2)}, u32[]{:S(2)}) collective-permute-start(f32[2,256]{1,0:T(2,128)} %pad_maximum_fusion.4), channel_id=1, source_target_pairs={{0,4},{4,8},{8,12},{12,16},{16,20},{20,24},{24,28},{1,5},{5,9},{9,... | collective-permute-start | bytes 6152 | tf_op jit(solution)/shard_map/ppermute | solution.py:15
  78.3 0.8 copy.35
  79.1 9.6 %collective-permute-done.8 = f32[2,256]{1,0:T(2,128)} collective-permute-done((f32[2,256]{1,0:T(2,128)}, f32[2,256]{1,0:T(2,128)}, u32[]{:S(2)}, u32[]{:S(2)}) %collective-permute-start.8) | collective-permute-done | bytes 2080 | tf_op jit(solution)/shard_map/ppermute | solution.py:15
  88.7 0.8 fusion.50
  89.4 1.9 %fusion.25 = (f32[1,256,256]{2,1,0:T(8,128)}, f32[1,256,256]{2,1,0:T(8,128)}) fusion(f32[256,256]{1,0:T(8,128)S(1)} %get-tuple-element.12, f32[256,256]{1,0:T(8,128)S(1)} %get-tuple-element.10, f32[255,256]{1,0:T(8,128)S(1)} %bitcast.141, f32[1,256]{1,0:T(1,128)S(1)} %get-tuple-element.39, f32[256,255]{1,0:T(8,128)S(1)} %bitcast.131, f32[256,1]{1,0:T(8,128)S(1)} %copy.34, ...), kind=kLoop, calls=%fused_computation.53 | loop fusion | flops 655360 | bytes 2359296 | tf_op jit(solution)/shard_map/stack | solution.py:40
  91.4 0.7 copy.59
  92.1 0.2 copy.47
  92.3 0.4 copy-done.24
  92.7 0.7 convolution_bitcast_fusion
  93.5 0.4 reshape.126
  94.0 0.4 copy-done.10
  94.6 2.2 %multiply_reduce_fusion = (f32[256,256]{1,0:T(8,128)}, f32[2,256,256]{2,1,0:T(8,128)S(1)}) fusion(f32[2,256,256]{2,1,0:T(8,128)S(1)} %convert_add_fusion.1, f32[1,256,256]{2,1,0:T(8,128)} %get-tuple-element.25, f32[1,256,256]{2,1,0:T(8,128)S(1)} %copy-done.15, bf16[2,256,256]{2,1,0:T(8,128)(2,1)S(1)} %copy-done.13, f32[256,256]{1,0:T(8,128)S(1)} %copy-done.10, ...), kind=kLoop, calls=%fused_computation.26 | loop fusion | flops 2424832 | bytes 3932160 | tf_op jit(solution)/shard_map/reduce_sum | solution.py:115
  96.8 3.9 %collective-permute-start.10 = (f32[2,1,256]{2,1,0:T(1,128)S(1)}, f32[2,1,256]{2,1,0:T(1,128)S(1)}, u32[]{:S(2)}, u32[]{:S(2)}) collective-permute-start(f32[2,1,256]{2,1,0:T(1,128)S(1)} %slice.303), channel_id=1, source_target_pairs={{4,0},{8,4},{12,8},{16,12},{20,16},{24,20},{28,24},{5,1},{9,5},{13... | collective-permute-start | bytes 6152 | tf_op jit(solution)/shard_map/ppermute | solution.py:15
  100.7 1.3 %collective-permute-start.11 = (f32[2,256,1]{2,1,0:T(8,128)S(1)}, f32[2,256,1]{2,1,0:T(8,128)S(1)}, u32[]{:S(2)}, u32[]{:S(2)}) collective-permute-start(f32[2,256,1]{2,1,0:T(8,128)S(1)} %slice.306), channel_id=1, source_target_pairs={{1,0},{2,1},{3,2},{5,4},{6,5},{7,6},{9,8},{10,9},{11,10},{13,12},{... | collective-permute-start | bytes 6152 | tf_op jit(solution)/shard_map/ppermute | solution.py:15
  102.0 0.2 slice.305
  102.3 1.9 %collective-permute-done.11 = f32[2,256,1]{2,1,0:T(8,128)S(1)} collective-permute-done((f32[2,256,1]{2,1,0:T(8,128)S(1)}, f32[2,256,1]{2,1,0:T(8,128)S(1)}, u32[]{:S(2)}, u32[]{:S(2)}) %collective-permute-start.11) | collective-permute-done | bytes 2080 | tf_op jit(solution)/shard_map/ppermute | solution.py:15
  104.8 4.8 %collective-permute-start.13 = (f32[2,256]{1,0:T(2,128)S(1)}, f32[2,256]{1,0:T(2,128)S(1)}, u32[]{:S(2)}, u32[]{:S(2)}) collective-permute-start(f32[2,256]{1,0:T(2,128)S(1)} %pad_maximum_fusion.7), channel_id=1, source_target_pairs={{0,1},{1,2},{2,3},{4,5},{5,6},{6,7},{8,9},{9,10},{10,11},{12,13},{... | collective-permute-start | bytes 6152 | tf_op jit(solution)/shard_map/ppermute | solution.py:15
  109.6 2.2 %collective-permute-start.12 = (f32[2,256]{1,0:T(2,128)S(1)}, f32[2,256]{1,0:T(2,128)S(1)}, u32[]{:S(2)}, u32[]{:S(2)}) collective-permute-start(f32[2,256]{1,0:T(2,128)S(1)} %pad_maximum_fusion.6), channel_id=1, source_target_pairs={{0,4},{4,8},{8,12},{12,16},{16,20},{20,24},{24,28},{1,5},{5,9},{9,... | collective-permute-start | bytes 6152 | tf_op jit(solution)/shard_map/ppermute | solution.py:15
  111.9 0.8 copy.39
  112.7 3.2 %collective-permute-done.12 = f32[2,256]{1,0:T(2,128)S(1)} collective-permute-done((f32[2,256]{1,0:T(2,128)S(1)}, f32[2,256]{1,0:T(2,128)S(1)}, u32[]{:S(2)}, u32[]{:S(2)}) %collective-permute-start.12) | collective-permute-done | bytes 2080 | tf_op jit(solution)/shard_map/ppermute | solution.py:15
  116.0 1.3 %fusion.31 = (f32[1,256,256]{2,1,0:T(8,128)S(1)}, f32[1,256,256]{2,1,0:T(8,128)S(1)}) fusion(f32[256,256]{1,0:T(8,128)S(1)} %get-tuple-element.9, f32[256,256]{1,0:T(8,128)S(1)} %get-tuple-element.7, f32[255,256]{1,0:T(8,128)S(1)} %bitcast.142, f32[1,256]{1,0:T(1,128)S(1)} %get-tuple-element.35, f32[256,255]{1,0:T(8,128)S(1)} %bitcast.133, ...), kind=kLoop, calls=%fused_computation.61 | loop fusion | flops 655360 | bytes 2359296 | tf_op jit(solution)/shard_map/stack | solution.py:40
  117.5 0.5 fusion.5
  118.1 0.4 copy-done.8
  118.5 0.8 add_multiply_fusion
  (111 shorter events, 3.8 us)
Async XLA Ops:
  0.0 1.7 %copy-start = (bf16[1,16]{1,0:T(2,128)(2,1)S(1)}, bf16[1,16]{1,0:T(2,128)(2,1)}, u32[]{:S(2)}) copy-start(bf16[1,16]{1,0:T(2,128)(2,1)} %param.14) | copy-start | bytes 100
  0.0 23.6 %copy-start.1 = (bf16[2,256,256]{2,1,0:T(8,128)(2,1)S(1)}, bf16[2,256,256]{2,1,0:T(8,128)(2,1)}, u32[]{:S(2)}) copy-start(bf16[2,256,256]{2,1,0:T(8,128)(2,1)} %param.9) | copy-start | bytes 786436
  2.5 25.1 %all-to-all-start.1 = ((bf16[8,2,1]{1,2,0:T(2,128)(2,1)}), bf16[8,2,1]{1,2,0:T(2,128)(2,1)S(1)}, u32[]{:S(2)}, u32[]{:S(2)}) async-start(bf16[8,2,1]{1,2,0:T(2,128)(2,1)} %copy.31), calls=%async_computation.1 | async-start | bytes 8192 | tf_op jit(solution)/shard_map/all_to_all | solution.py:93
  9.8 36.4 %collective-permute-start = (f32[1,256]{1,0:T(1,128)}, f32[1,256]{1,0:T(1,128)}, u32[]{:S(2)}, u32[]{:S(2)}) collective-permute-start(f32[1,256]{1,0:T(1,128)} %slice.198), channel_id=1, source_target_pairs={{0,4},{4,8},{8,12},{12,16},{16,20},{20,24},{24,28},{1,5},{5,9},{9,... | collective-permute-start | bytes 3080 | tf_op jit(solution)/shard_map/ppermute | solution.py:15
  14.5 30.8 %collective-permute-start.2 = (f32[2,1,256]{2,1,0:T(1,128)}, f32[2,1,256]{2,1,0:T(1,128)}, u32[]{:S(2)}, u32[]{:S(2)}) collective-permute-start(f32[2,1,256]{2,1,0:T(1,128)} %slice.263), channel_id=1, source_target_pairs={{4,0},{8,4},{12,8},{16,12},{20,16},{24,20},{28,24},{5,1},{9,5},{13... | collective-permute-start | bytes 6152 | tf_op jit(solution)/shard_map/ppermute | solution.py:15
  19.5 26.7 %collective-permute-start.1 = (f32[256,1]{1,0:T(8,128)}, f32[256,1]{1,0:T(8,128)S(1)}, u32[]{:S(2)}, u32[]{:S(2)}) collective-permute-start(f32[256,1]{1,0:T(8,128)} %slice.200), channel_id=1, source_target_pairs={{0,1},{1,2},{2,3},{4,5},{5,6},{6,7},{8,9},{9,10},{10,11},{12,13},{... | collective-permute-start | bytes 3080 | tf_op jit(solution)/shard_map/ppermute | solution.py:15
  21.7 23.6 %collective-permute-start.3 = (f32[2,256,1]{2,1,0:T(8,128)S(1)}, f32[2,256,1]{2,1,0:T(8,128)S(1)}, u32[]{:S(2)}, u32[]{:S(2)}) collective-permute-start(f32[2,256,1]{2,1,0:T(8,128)S(1)} %slice.266), channel_id=1, source_target_pairs={{1,0},{2,1},{3,2},{5,4},{6,5},{7,6},{9,8},{10,9},{11,10},{13,12},{... | collective-permute-start | bytes 6152 | tf_op jit(solution)/shard_map/ppermute | solution.py:15
  23.6 1.0 copy-start.27
  23.7 1.1 copy-start.26
  23.7 1.8 %copy-start.21 = (bf16[1,16,2,128,128]{4,3,2,1,0:T(8,128)(2,1)S(1)}, bf16[1,16,2,128,128]{4,3,2,1,0:T(8,128)(2,1)}, u32[]{:S(2)}) copy-start(bf16[1,16,2,128,128]{4,3,2,1,0:T(8,128)(2,1)} %param.13) | copy-start | bytes 3145732
  27.6 8.9 %all-to-all-start = ((s32[8,2,1]{1,2,0:T(1,128)}), s32[8,2,1]{1,2,0:T(1,128)S(1)}, u32[]{:S(2)}, u32[]{:S(2)}) async-start(s32[8,2,1]{1,2,0:T(1,128)} %bitcast.4), calls=%async_computation | async-start | bytes 8192 | tf_op jit(solution)/shard_map/all_to_all | solution.py:94
  36.4 8.9 %copy-start.20 = (f32[2,255,256]{2,1,0:T(8,128)S(1)}, f32[2,255,256]{2,1,0:T(8,128)}, u32[]{:S(2)}) copy-start(f32[2,255,256]{2,1,0:T(8,128)} %slice.262) | copy-start | bytes 1566724
  36.4 54.9 %all-to-all-start.2 = ((bf16[16,2,128,128]{3,2,1,0:T(8,128)(2,1)}), bf16[16,2,128,128]{3,2,1,0:T(8,128)(2,1)S(1)}, u32[]{:S(2)}, u32[]{:S(2)}) async-start(bf16[16,2,128,128]{3,2,1,0:T(8,128)(2,1)} %bitcast.54), calls=%async_computation.2 | async-start | bytes 2097152 | tf_op jit(solution)/shard_map/all_to_all | solution.py:90
  44.7 0.6 copy-start.23
  45.3 1.0 copy-start.2
  47.4 6.5 %collective-permute-start.5 = (f32[2,256]{1,0:T(2,128)S(1)}, f32[2,256]{1,0:T(2,128)S(1)}, u32[]{:S(2)}, u32[]{:S(2)}) collective-permute-start(f32[2,256]{1,0:T(2,128)S(1)} %pad_maximum_fusion.3), channel_id=1, source_target_pairs={{0,1},{1,2},{2,3},{4,5},{5,6},{6,7},{8,9},{9,10},{10,11},{12,13},{... | collective-permute-start | bytes 6152 | tf_op jit(solution)/shard_map/ppermute | solution.py:15
  50.5 9.7 %collective-permute-start.4 = (f32[2,256]{1,0:T(2,128)S(1)}, f32[2,256]{1,0:T(2,128)S(1)}, u32[]{:S(2)}, u32[]{:S(2)}) collective-permute-start(f32[2,256]{1,0:T(2,128)S(1)} %pad_maximum_fusion.2), channel_id=1, source_target_pairs={{0,4},{4,8},{8,12},{12,16},{16,20},{20,24},{24,28},{1,5},{5,9},{9,... | collective-permute-start | bytes 6152 | tf_op jit(solution)/shard_map/ppermute | solution.py:15
  60.3 1.0 copy-start.9
  60.3 1.0 copy-start.12
  60.5 1.0 copy-start.3
  60.5 1.0 copy-start.5
  61.5 5.5 %collective-permute-start.6 = (f32[2,1,256]{2,1,0:T(1,128)S(1)}, f32[2,1,256]{2,1,0:T(1,128)S(1)}, u32[]{:S(2)}, u32[]{:S(2)}) collective-permute-start(f32[2,1,256]{2,1,0:T(1,128)S(1)} %slice.283), channel_id=1, source_target_pairs={{4,0},{8,4},{12,8},{16,12},{20,16},{24,20},{28,24},{5,1},{9,5},{13... | collective-permute-start | bytes 6152 | tf_op jit(solution)/shard_map/ppermute | solution.py:15
  63.5 3.6 %collective-permute-start.7 = (f32[2,256,1]{2,1,0:T(8,128)S(1)}, f32[2,256,1]{2,1,0:T(8,128)S(1)}, u32[]{:S(2)}, u32[]{:S(2)}) collective-permute-start(f32[2,256,1]{2,1,0:T(8,128)S(1)} %slice.286), channel_id=1, source_target_pairs={{1,0},{2,1},{3,2},{5,4},{6,5},{7,6},{9,8},{10,9},{11,10},{13,12},{... | collective-permute-start | bytes 6152 | tf_op jit(solution)/shard_map/ppermute | solution.py:15
  65.0 1.1 copy-start.7
  67.7 10.4 %collective-permute-start.9 = (f32[2,256]{1,0:T(2,128)S(1)}, f32[2,256]{1,0:T(2,128)S(1)}, u32[]{:S(2)}, u32[]{:S(2)}) collective-permute-start(f32[2,256]{1,0:T(2,128)S(1)} %pad_maximum_fusion.5), channel_id=1, source_target_pairs={{0,1},{1,2},{2,3},{4,5},{5,6},{6,7},{8,9},{9,10},{10,11},{12,13},{... | collective-permute-start | bytes 6152 | tf_op jit(solution)/shard_map/ppermute | solution.py:15
  74.5 14.2 %collective-permute-start.8 = (f32[2,256]{1,0:T(2,128)}, f32[2,256]{1,0:T(2,128)}, u32[]{:S(2)}, u32[]{:S(2)}) collective-permute-start(f32[2,256]{1,0:T(2,128)} %pad_maximum_fusion.4), channel_id=1, source_target_pairs={{0,4},{4,8},{8,12},{12,16},{16,20},{20,24},{24,28},{1,5},{5,9},{9,... | collective-permute-start | bytes 6152 | tf_op jit(solution)/shard_map/ppermute | solution.py:15
  92.0 0.7 copy-start.24
  92.1 0.7 copy-start.25
  93.4 1.0 copy-start.10
  93.5 1.0 copy-start.13
  93.5 1.1 copy-start.15
  96.8 5.5 %collective-permute-start.10 = (f32[2,1,256]{2,1,0:T(1,128)S(1)}, f32[2,1,256]{2,1,0:T(1,128)S(1)}, u32[]{:S(2)}, u32[]{:S(2)}) collective-permute-start(f32[2,1,256]{2,1,0:T(1,128)S(1)} %slice.303), channel_id=1, source_target_pairs={{4,0},{8,4},{12,8},{16,12},{20,16},{24,20},{28,24},{5,1},{9,5},{13... | collective-permute-start | bytes 6152 | tf_op jit(solution)/shard_map/ppermute | solution.py:15
  100.7 3.4 %collective-permute-start.11 = (f32[2,256,1]{2,1,0:T(8,128)S(1)}, f32[2,256,1]{2,1,0:T(8,128)S(1)}, u32[]{:S(2)}, u32[]{:S(2)}) collective-permute-start(f32[2,256,1]{2,1,0:T(8,128)S(1)} %slice.306), channel_id=1, source_target_pairs={{1,0},{2,1},{3,2},{5,4},{6,5},{7,6},{9,8},{10,9},{11,10},{13,12},{... | collective-permute-start | bytes 6152 | tf_op jit(solution)/shard_map/ppermute | solution.py:15
  104.8 7.0 %collective-permute-start.13 = (f32[2,256]{1,0:T(2,128)S(1)}, f32[2,256]{1,0:T(2,128)S(1)}, u32[]{:S(2)}, u32[]{:S(2)}) collective-permute-start(f32[2,256]{1,0:T(2,128)S(1)} %pad_maximum_fusion.7), channel_id=1, source_target_pairs={{0,1},{1,2},{2,3},{4,5},{5,6},{6,7},{8,9},{9,10},{10,11},{12,13},{... | collective-permute-start | bytes 6152 | tf_op jit(solution)/shard_map/ppermute | solution.py:15
  109.6 6.4 %collective-permute-start.12 = (f32[2,256]{1,0:T(2,128)S(1)}, f32[2,256]{1,0:T(2,128)S(1)}, u32[]{:S(2)}, u32[]{:S(2)}) collective-permute-start(f32[2,256]{1,0:T(2,128)S(1)} %pad_maximum_fusion.6), channel_id=1, source_target_pairs={{0,4},{4,8},{8,12},{12,16},{16,20},{20,24},{24,28},{1,5},{5,9},{9,... | collective-permute-start | bytes 6152 | tf_op jit(solution)/shard_map/ppermute | solution.py:15
  115.9 1.3 %copy-start.4 = (f32[1,256,256]{2,1,0:T(8,128)S(1)}, f32[1,256,256]{2,1,0:T(8,128)}, u32[]{:S(2)}) copy-start(f32[1,256,256]{2,1,0:T(8,128)} %copy-done.3) | copy-start | bytes 786436
  115.9 1.3 %copy-start.6 = (f32[1,256,256]{2,1,0:T(8,128)S(1)}, f32[1,256,256]{2,1,0:T(8,128)}, u32[]{:S(2)}) copy-start(f32[1,256,256]{2,1,0:T(8,128)} %copy-done.5) | copy-start | bytes 786436
  115.9 1.4 %copy-start.11 = (f32[256,256]{1,0:T(8,128)S(1)}, f32[256,256]{1,0:T(8,128)}, u32[]{:S(2)}) copy-start(f32[256,256]{1,0:T(8,128)} %param.11) | copy-start | bytes 786436
  116.0 1.4 %copy-start.14 = (bf16[2,256,256]{2,1,0:T(8,128)(2,1)S(1)}, bf16[2,256,256]{2,1,0:T(8,128)(2,1)}, u32[]{:S(2)}) copy-start(bf16[2,256,256]{2,1,0:T(8,128)(2,1)} %param.12) | copy-start | bytes 786436
  116.0 1.3 %copy-start.16 = (f32[1,256,256]{2,1,0:T(8,128)S(1)}, f32[1,256,256]{2,1,0:T(8,128)}, u32[]{:S(2)}) copy-start(f32[1,256,256]{2,1,0:T(8,128)} %get-tuple-element.24) | copy-start | bytes 786436
  116.0 1.4 %copy-start.17 = (f32[1,256,256]{2,1,0:T(8,128)S(1)}, f32[1,256,256]{2,1,0:T(8,128)}, u32[]{:S(2)}) copy-start(f32[1,256,256]{2,1,0:T(8,128)} %get-tuple-element.25) | copy-start | bytes 786436
  116.0 1.4 %copy-start.18 = (f32[256,256]{1,0:T(8,128)S(1)}, f32[256,256]{1,0:T(8,128)}, u32[]{:S(2)}) copy-start(f32[256,256]{1,0:T(8,128)} %get-tuple-element.47) | copy-start | bytes 786436
  116.0 1.5 %copy-start.19 = (f32[256,256]{1,0:T(8,128)S(1)}, f32[256,256]{1,0:T(8,128)}, u32[]{:S(2)}) copy-start(f32[256,256]{1,0:T(8,128)} %get-tuple-element.48) | copy-start | bytes 786436
  117.5 0.9 copy-start.8
  117.5 1.0 copy-start.22
where the time goes:
time: 120 us; the launch traced here: 119 us
  starting transfers between devices  59.5 us (50%)
  waiting for transfers between devices  24.7 us (21%)
  local copies, waits for them, and re-layouts  20 us (17%)
  other arithmetic  13.1 us (11%)
  matrix products  1.25 us (1%)
    ppermute x14, starting transfers between devices, from_behind(): lax.ppermute(value, axis, [(source, source + steps) for source in range(f...  41 us
    ppermute x14, waiting for transfers between devices, from_behind(): lax.ppermute(value, axis, [(source, source + steps) for source in range(f...  21.6 us
    all_to_all x1, starting transfers between devices, body(): lax.all_to_all(obs_buffer.reshape(places, 2, tile, tile), 'gx', split_axi...  6.89 us
    all_to_all x1, starting transfers between devices, body(): lax.all_to_all(weight_buffer, 'gx', split_axis=0, concat_axis=0, tiled=True)  6.03 us
    all_to_all x1, starting transfers between devices, body(): lax.all_to_all(slot_buffer, 'gx', split_axis=0, concat_axis=0, tiled=True)  5.67 us
    unnamed x59, local copies, waits for them, and re-layouts  5.19 us
    another operation x3, other arithmetic, stress_image(): return jnp.stack([push_u, push_v])  3.41 us
    all_to_all x1, waiting for transfers between devices, body(): lax.all_to_all(slot_buffer, 'gx', split_axis=0, concat_axis=0, tiled=True)  3.09 us
  transfers between devices with their start and end apart: 17, of which 6 were waited for; matrix products, arithmetic and copies ran while one was open for 17% of the time, Pallas kernels for 0%

commit v1 on v0

v1 whole, which is shorter than its diff:
```python
import functools

import jax
import jax.numpy as jnp
from jax import lax
from jax.experimental import pallas as pl
from jax.experimental.pallas import tpu as pltpu
from jax.sharding import PartitionSpec as P

CAP = 2
OMEGA = 0.6
LANE = 128
PAD = 16
PACK = 16
FIELDS = ((0, 3), (3, 3), (6, 3), (9, 2), (11, 2), (13, 2), (15, 1))
U, V, VISC, FRIC, DRIVE_U, DRIVE_V, ICE = range(7)

VMEM = pl.BlockSpec(memory_space=pltpu.VMEM)
SMEM = pl.BlockSpec(memory_space=pltpu.SMEM)
ANY = pl.BlockSpec(memory_space=pl.ANY)


def partner(me, step, count):
    if count & (count - 1) == 0:
        return me ^ step
    return (me + step) % count


def from_behind(value, axis, steps):
    count = lax.axis_size(axis)
    first, last = (max(0, -steps), min(count, count - steps))
    return lax.ppermute(value, axis, [(source, source + steps) for source in range(first, last)])


def own_field(index, vel, visc, fric, drive, rows):
    if index in (U, V):
        return vel[index, rows, :].astype(jnp.float32)
    if index == VISC:
        return visc[rows, :]
    if index == FRIC:
        return fric[rows, :]
    return drive[index - DRIVE_U, rows, :].astype(jnp.float32)


def ice_row(ice, tile_row, shape, tile):
    lane = lax.broadcasted_iota(jnp.int32, shape, 1)
    row = jnp.zeros(shape, jnp.float32)
    for column in range(shape[1] // tile):
        row = jnp.where(lane // tile == column, ice[tile_row, column].astype(jnp.float32), row)
    return row


def send_kernel(groups, count, tile, *refs):
    owner, slot, weight, ice, obs, vel, visc, fric, drive = refs[:9]
    pays = refs[9 : 9 + groups]
    to_low, to_high = refs[9 + groups : 11 + groups]
    place, filled, edges, extra, scene_sem, edge_sem, extra_sem = refs[11 + groups :]
    blocks = tile // PACK
    me = lax.axis_index("gx")
    edge_copies = [
        pltpu.make_async_copy(obs.at[:, at], edges.at[number], edge_sem.at[number])
        for number, at in enumerate((0, blocks, blocks - 1, 2 * blocks - 1))
    ]
    for copy in edge_copies:
        copy.start()
    for index in range((groups + 2) * CAP):
        place[index] = -1
    for index in range(groups):
        filled[index] = 0
    for scene in range(count):
        who = owner[scene]
        rank = filled[who]
        place[(who + 1) * CAP + rank] = scene
        filled[who] = rank + 1
    copies = []
    for step in range(groups):
        to = partner(me, step, groups)
        for rank in range(CAP):
            scene = jnp.maximum(place[(to + 1) * CAP + rank], 0)
            copy = pltpu.make_async_copy(
                obs.at[scene],
                pays[step].at[pl.ds(rank * 2 * blocks, 2 * blocks)],
                scene_sem.at[step * CAP + rank],
            )
            copy.start()
            copies.append(copy)
    cells = visc.shape[0]
    for index, (at, depth) in enumerate(FIELDS[:-1]):
        to_low[at : at + depth, :] = own_field(index, vel, visc, fric, drive, slice(0, depth))
        to_high[at : at + depth, :] = own_field(index, vel, visc, fric, drive, slice(cells - depth, cells))
    at = FIELDS[ICE][0]
    to_low[at : at + 1, :] = ice_row(ice, 0, (1, visc.shape[1]), tile)
    to_high[at : at + 1, :] = ice_row(ice, cells // tile - 1, (1, visc.shape[1]), tile)
    for copy in edge_copies:
        copy.wait()
    row = lax.broadcasted_iota(jnp.int32, (PACK, LANE), 0)
    lane = lax.broadcasted_iota(jnp.int32, (PACK, LANE), 1)
    for step in range(groups):
        to = partner(me, step, groups)
        block = jnp.zeros((PACK, LANE), jnp.float32)
        for side in range(2):
            for rank in range(CAP):
                spot = place[(to + (2 if side == 0 else 0)) * CAP + rank]
                scene = jnp.maximum(spot, 0)
                amount = jnp.where(spot >= 0, weight[scene], 0.0)
                where = slot[scene]
                for part in range(2):
                    line = edges[side * 2 + part, scene].astype(jnp.float32)
                    line = line[0:1] if side == 0 else line[PACK - 1 : PACK]
                    block = jnp.where(row == (side * CAP + rank) * 2 + part, line, block)
                    value = jnp.where(where == side * 2 + part, amount, 0.0)
                    block = jnp.where((row == 8) & (lane == 8 + (side * CAP + rank) * 2 + part), value, block)
        for rank in range(CAP):
            spot = place[(to + 1) * CAP + rank]
            scene = jnp.maximum(spot, 0)
            amount = jnp.where(spot >= 0, weight[scene], 0.0)
            for position in range(4):
                value = jnp.where(slot[scene] == position, amount, 0.0)
                block = jnp.where((row == 8) & (lane == rank * 4 + position), value, block)
        extra[step] = block.astype(jnp.bfloat16)
        copy = pltpu.make_async_copy(
            extra.at[pl.ds(step, 1)], pays[step].at[pl.ds(CAP * 2 * blocks, 1)], extra_sem.at[step]
        )
        copy.start()
        copies.append(copy)
    for copy in copies:
        copy.wait()


def columns_of(block, first):
    picked = lax.broadcasted_iota(jnp.int32, (8, LANE), 0) + first
    pick = (picked == lax.broadcasted_iota(jnp.int32, (8, LANE), 1)).astype(jnp.float32)
    return lax.dot_general(
        pick, block, (((1,), (1,)), ((), ())),
        precision=lax.Precision.HIGHEST, preferred_element_type=jnp.float32,
    )


def widen_kernel(tile, ice, vel, visc, fric, drive, low, high, ext, to_low, to_high):
    cells = visc.shape[0]
    rows = ext.shape[1]
    own = slice(PAD, PAD + cells)
    to_low[...] = jnp.zeros_like(to_low)
    to_high[...] = jnp.zeros_like(to_high)
    for index, (at, depth) in enumerate(FIELDS):
        ext[index, 0:PAD, :] = jnp.zeros((PAD, ext.shape[2]), jnp.float32)
        ext[index, PAD + cells :, :] = jnp.zeros((PAD, ext.shape[2]), jnp.float32)
        if index == ICE:
            for tile_row in range(cells // tile):
                ext[index, PAD + tile_row * tile : PAD + (tile_row + 1) * tile, :] = ice_row(
                    ice, tile_row, (tile, ext.shape[2]), tile
                )
        else:
            ext[index, own, :] = own_field(index, vel, visc, fric, drive, slice(None))
        ext[index, PAD - depth : PAD, :] = low[at : at + depth, :]
        ext[index, PAD + cells : PAD + cells + depth, :] = high[at : at + depth, :]
        if index != ICE:
            first = columns_of(ext[index, :, 0:LANE], 0)
            last = columns_of(ext[index, :, ext.shape[2] - LANE :], LANE - depth)
            to_low[at : at + depth, 0:rows] = first[0:depth]
            to_high[at : at + depth, 0:rows] = last[0:depth]


def stress_block(u, v, visc, low, rows, wide):
    here, after = pl.ds(low, rows), pl.ds(low + 1, rows)
    vel_u, vel_v = u[here, :], v[here, :]
    a_x = u[after, :] - vel_u
    b_x = v[after, :] - vel_v
    a_y = pltpu.roll(vel_u, wide - 1, 1) - vel_u
    b_y = pltpu.roll(vel_v, wide - 1, 1) - vel_v
    nu = visc[here, :]
    return nu * (4.0 * a_x + 2.0 * b_y), nu * (4.0 * b_y + 2.0 * a_x), nu * (a_y + b_x)


def image_block(sxx, syy, sxy, low, rows):
    here, before = pl.ds(low, rows), pl.ds(low - 1, rows)
    mid = sxy[here, :]
    push_u = sxx[before, :] - sxx[here, :] + pltpu.roll(mid, 1, 1) - mid
    side = syy[here, :]
    push_v = sxy[before, :] - mid + pltpu.roll(side, 1, 1) - side
    return push_u, push_v


def sweep_kernel(ext, left, right, second, ease, lead, trail, wide_visc, *scratch):
    rows, cells_y = ext.shape[1], ext.shape[2]
    wide = cells_y + LANE
    u, v, fric, drive_u, drive_v, next_u, next_v, relax_u, relax_v, sxx, syy, sxy, turned = scratch
    turned[...] = jnp.zeros_like(turned)
    turned[0:PACK, :] = right[...]
    turned[PACK : 2 * PACK, :] = left[...]
    upright = jnp.transpose(turned[...])[0:rows]
    lane = lax.broadcasted_iota(jnp.int32, (rows, LANE), 1)
    fields = (u, v, wide_visc, fric, drive_u, drive_v)
    for index, field in enumerate(fields):
        at, depth = FIELDS[index]
        field[:, 0:cells_y] = ext[index]
        after = pltpu.roll(upright, (LANE - at) % LANE, 1)
        before = pltpu.roll(upright, (LANE - depth - PACK - at) % LANE, 1)
        field[:, cells_y:wide] = jnp.where(
            lane < depth, after, jnp.where(lane >= LANE - depth, before, 0.0)
        )
    blocks = range(8, rows - 8, 8)
    own = range(PAD, rows - PAD, 8)
    for low in blocks:
        here = pl.ds(low, 8)
        nu, drag = wide_visc[here, :], fric[here, :]
        nu_x = wide_visc[pl.ds(low - 1, 8), :]
        nu_y = pltpu.roll(nu, 1, 1)
        inside = drag > 0.0
        for out, diag in ((relax_u, 5.0 * nu + 4.0 * nu_x + nu_y), (relax_v, 5.0 * nu + nu_x + 4.0 * nu_y)):
            out[here, :] = jnp.where(inside, 1.0 / jnp.where(inside, diag + drag, 1.0), 0.0)
    for low in blocks:
        here = pl.ds(low, 8)
        sxx[here, :], syy[here, :], sxy[here, :] = stress_block(u, v, wide_visc, low, 8, wide)
    for low in blocks:
        here = pl.ds(low, 8)
        pushes = image_block(sxx, syy, sxy, low, 8)
        for part, (push, vel, force, relax, after) in enumerate(
            zip(pushes, (u, v), (drive_u, drive_v), (relax_u, relax_v), (next_u, next_v))
        ):
            now, soft = vel[here, :], relax[here, :]
            move = soft * (force[here, :] - push - fric[here, :] * now)
            after[here, :] = now + OMEGA * move
            slack = OMEGA * soft
            ease[part, here, :] = slack[:, 0:cells_y]
            if low in own:
                lead[part, pl.ds(low - PAD, 8), :] = (slack * (move + now))[:, 0:cells_y]
    for low in blocks:
        here = pl.ds(low, 8)
        sxx[here, :], syy[here, :], sxy[here, :] = stress_block(next_u, next_v, wide_visc, low, 8, wide)
    for low in blocks:
        here = pl.ds(low, 8)
        pushes = image_block(sxx, syy, sxy, low, 8)
        for part, (push, vel, force, relax) in enumerate(
            zip(pushes, (next_u, next_v), (drive_u, drive_v), (relax_u, relax_v))
        ):
            now = vel[here, :]
            move = relax[here, :] * (force[here, :] - push - fric[here, :] * now)
            second[part, here, :] = (now + OMEGA * move)[:, 0:cells_y]
            if low in own:
                trail[part, pl.ds(low - PAD, 8), :] = (move + now)[:, 0:cells_y]


def misfit_kernel(groups, tile, *refs):
    pays = refs[:groups]
    second, ease, ext, misfit, lift, to_low, to_high, table, total = refs[groups:]
    rows, cells_y = second.shape[1], second.shape[2]
    cells = rows - 2 * PAD
    blocks = tile // PACK
    tiles_y = cells_y // tile
    slots = cells // tile * tiles_y
    places = groups * CAP
    total[...] = jnp.zeros_like(total)
    ring = [[[jnp.zeros((1, LANE), jnp.float32) for _ in range(2)] for _ in range(2)] for _ in range(2)]
    ring_weight = [[jnp.zeros((1, LANE), jnp.float32) for _ in range(2)] for _ in range(2)]
    for group in range(groups):
        block = pays[group][CAP * 2 * blocks].astype(jnp.float32)
        meta = block[8:9]
        for index in range(CAP * slots):
            line = jnp.broadcast_to(meta[:, index : index + 1], (1, LANE))
            table[pl.ds(group * CAP * slots + index, 1), :] = line
            total[pl.ds(index % slots, 1), :] += line
        for side in range(2):
            for rank in range(CAP):
                for column in range(2):
                    index = 8 + (side * CAP + rank) * 2 + column
                    line = jnp.broadcast_to(meta[:, index : index + 1], (1, LANE))
                    ring_weight[side][column] += line
                    for part in range(2):
                        at = (side * CAP + rank) * 2 + part
                        ring[side][part][column] += line * block[at : at + 1]
    lift[:, 0:PAD, :] = jnp.zeros((2, PAD, cells_y), jnp.float32)
    lift[:, PAD + cells :, :] = jnp.zeros((2, PAD, cells_y), jnp.float32)
    for side, at in enumerate((PAD + cells, PAD - 1)):
        for column in range(2):
            lanes = slice(column * tile, (column + 1) * tile)
            for part in range(2):
                cold = ext[ICE, at : at + 1, lanes]
                gap = cold * (ring_weight[side][column] * second[part, at : at + 1, lanes] - ring[side][part][column])
                lift[part, at : at + 1, lanes] = ease[part, at : at + 1, lanes] * gap

    def step(index, carry):
        part, chunk = index // blocks, index % blocks
        sums = [jnp.zeros((PACK, LANE), jnp.float32) for _ in range(slots)]
        for spot in range(places):
            got = pays[spot // CAP][(spot % CAP) * 2 * blocks + index].astype(jnp.float32)
            for position in range(slots):
                sums[position] += table[pl.ds(spot * slots + position, 1), :] * got
        for position in range(slots):
            lanes = slice((position % tiles_y) * tile, (position % tiles_y + 1) * tile)
            at = pl.multiple_of((position // tiles_y) * tile + chunk * PACK, PACK)
            wide_at = pl.multiple_of(at + PAD, PACK)
            cold = ext[ICE, pl.ds(wide_at, PACK), lanes]
            gap = cold * (
                total[pl.ds(position, 1), :] * second[part, pl.ds(wide_at, PACK), lanes] - sums[position]
            )
            misfit[part, pl.ds(at, PACK), lanes] = gap
            lift[part, pl.ds(wide_at, PACK), lanes] = ease[part, pl.ds(wide_at, PACK), lanes] * gap
        return carry

    lax.fori_loop(0, 2 * blocks, step, 0)
    to_low[...] = jnp.zeros_like(to_low)
    to_high[...] = jnp.zeros_like(to_high)
    for part in range(2):
        to_low[part : part + 1, 0:rows] = columns_of(lift[part, :, 0:LANE], 0)[0:1]
        to_high[part : part + 1, 0:rows] = columns_of(lift[part, :, cells_y - LANE :], LANE - 1)[0:1]


def grad_kernel(lift, misfit, left, right, ext, visc, lead, trail, grad, u, v, sxx, syy, sxy, turned):
    rows, cells_y = lift.shape[1], lift.shape[2]
    wide = cells_y + LANE
    turned[...] = jnp.zeros_like(turned)
    turned[0:8, :] = right[...]
    turned[8:16, :] = left[...]
    upright = jnp.transpose(turned[...])[0:rows]
    lane = lax.broadcasted_iota(jnp.int32, (rows, LANE), 1)
    for part, field in enumerate((u, v)):
        field[:, 0:cells_y] = lift[part]
        after = pltpu.roll(upright, (LANE - part) % LANE, 1)
        before = pltpu.roll(upright, LANE - 1 - 8 - part, 1)
        field[:, cells_y:wide] = jnp.where(lane == 0, after, jnp.where(lane == LANE - 1, before, 0.0))
    for low in range(8, rows - PAD, 8):
        here = pl.ds(low, 8)
        sxx[here, :], syy[here, :], sxy[here, :] = stress_block(u, v, visc, low, 8, wide)
    for low in range(PAD, rows - PAD, 8):
        own = pl.ds(low - PAD, 8)
        here = pl.ds(low, 8)
        drag = ext[FRIC, here, :]
        sums = jnp.zeros((8, cells_y), jnp.float32)
        for part, push in enumerate(image_block(sxx, syy, sxy, low, 8)):
            now = lift[part, here, :]
            back = misfit[part, own, :] - push[:, 0:cells_y] - drag * now
            sums += back * lead[part, own, :] + now * trail[part, own, :]
        grad[own, :] = -ext[ICE, here, :] * sums


def body(vel0, visc, fric, drive, scene_obs, scene_weight, scene_owner, scene_slot, ice_mask):
    cells_x, cells_y = visc.shape
    tile = scene_obs.shape[-1]
    count = scene_obs.shape[1]
    groups = lax.axis_size("gx")
    blocks = tile // PACK
    rows, wide = cells_x + 2 * PAD, cells_y + LANE
    long = -(-rows // LANE) * LANE
    f32 = jnp.float32
    obs = scene_obs.reshape(count, 2 * blocks, PACK, LANE)
    limit = 32 << 20

    def shape(*dims, dtype=f32):
        return jax.ShapeDtypeStruct(dims, dtype)

    pay = shape(CAP * 2 * blocks + 1, PACK, LANE, dtype=jnp.bfloat16)
    *pays, x_low, x_high = pl.pallas_call(
        functools.partial(send_kernel, groups, count, tile),
        out_shape=[pay] * groups + [shape(PACK, cells_y)] * 2,
        in_specs=[SMEM] * 4 + [ANY] + [VMEM] * 4,
        out_specs=[ANY] * groups + [VMEM] * 2,
        scratch_shapes=[
            pltpu.SMEM(((groups + 2) * CAP,), jnp.int32),
            pltpu.SMEM((groups,), jnp.int32),
            pltpu.VMEM((4, count, PACK, LANE), jnp.bfloat16),
            pltpu.VMEM((groups, PACK, LANE), jnp.bfloat16),
            pltpu.SemaphoreType.DMA((groups * CAP,)),
            pltpu.SemaphoreType.DMA((4,)),
            pltpu.SemaphoreType.DMA((groups,)),
        ],
        compiler_params=pltpu.CompilerParams(vmem_limit_bytes=limit),
        name="send",
    )(
        scene_owner.reshape(count), scene_slot.reshape(count), scene_weight.reshape(count).astype(f32),
        ice_mask, obs, vel0, visc, fric, drive,
    )
    from_high = from_behind(x_low, "gx", -1)
    from_low = from_behind(x_high, "gx", 1)
    got = [pays[0]]
    for step in range(1, groups):
        pairs = [(me, partner(me, step, groups)) for me in range(groups)]
        got.append(lax.ppermute(pays[step], "gx", pairs))
    ext, y_low, y_high = pl.pallas_call(
        functools.partial(widen_kernel, tile),
        out_shape=[shape(len(FIELDS), rows, cells_y), shape(PACK, long), shape(PACK, long)],
        in_specs=[SMEM] + [VMEM] * 6,
        out_specs=[VMEM] * 3,
        compiler_params=pltpu.CompilerParams(vmem_limit_bytes=limit),
        name="widen",
    )(ice_mask, vel0, visc, fric, drive, from_low, from_high)
    y_right = from_behind(y_low, "gy", -1)
    y_left = from_behind(y_high, "gy", 1)
    second, ease, lead, trail, wide_visc = pl.pallas_call(
        sweep_kernel,
        out_shape=[
            shape(2, rows, cells_y), shape(2, rows, cells_y), shape(2, cells_x, cells_y),
            shape(2, cells_x, cells_y), shape(rows, wide),
        ],
        in_specs=[VMEM] * 3,
        out_specs=[VMEM] * 5,
        scratch_shapes=[pltpu.VMEM((rows, wide), f32)] * 12 + [pltpu.VMEM((LANE, long), f32)],
        compiler_params=pltpu.CompilerParams(vmem_limit_bytes=limit),
        name="sweep",
    )(ext, y_left, y_right)
    misfit, lift, lift_low, lift_high = pl.pallas_call(
        functools.partial(misfit_kernel, groups, tile),
        out_shape=[shape(2, cells_x, cells_y), shape(2, rows, cells_y), shape(8, long), shape(8, long)],
        in_specs=[VMEM] * (groups + 3),
        out_specs=[VMEM] * 4,
        scratch_shapes=[pltpu.VMEM((groups * CAP * 4, LANE), f32), pltpu.VMEM((8, LANE), f32)],
        compiler_params=pltpu.CompilerParams(vmem_limit_bytes=limit),
        name="misfit",
    )(*got, second, ease, ext)
    lift_right = from_behind(lift_low, "gy", -1)
    lift_left = from_behind(lift_high, "gy", 1)
    return pl.pallas_call(
        grad_kernel,
        out_shape=shape(cells_x, cells_y),
        in_specs=[VMEM] * 8,
        out_specs=VMEM,
        scratch_shapes=[pltpu.VMEM((rows, wide), f32)] * 5 + [pltpu.VMEM((LANE, long), f32)],
        compiler_params=pltpu.CompilerParams(vmem_limit_bytes=limit),
        name="grad",
    )(lift, misfit, lift_left, lift_right, ext, wide_visc, lead, trail)


def solution(mesh):
    placed = (
        P(None, "gx", "gy"),
        P("gx", "gy"),
        P("gx", "gy"),
        P(None, "gx", "gy"),
        P("gy", "gx", None, None, None),
        P("gy", "gx"),
        P("gy", "gx", None),
        P("gy", "gx"),
        P("gx", "gy"),
    )
    return jax.shard_map(body, mesh=mesh, in_specs=placed, out_specs=P("gx", "gy"), check_vma=False)
```

time: 120 us -> 70.8 us (0.59)
  the two profiles are of different devices: /device:TPU:24 before, /device:TPU:11 now
where the time goes in v1:
time: 70.8 us; the launch traced here: 70.4 us
  waiting for transfers between devices  27.5 us (39%)
  starting transfers between devices  23.6 us (33%)
  Pallas kernels  11.4 us (16%)
  local copies, waits for them, and re-layouts  7.01 us (10%)
    ppermute x6, starting transfers between devices, from_behind(): lax.ppermute(value, axis, [(source, source + steps) for source in range(f...  21.2 us
    ppermute x7, waiting for transfers between devices, body(): got.append(lax.ppermute(pays[step], 'gx', pairs))  18.2 us
    ppermute x6, waiting for transfers between devices, from_behind(): lax.ppermute(value, axis, [(source, source + steps) for source in range(f...  9.34 us
    unnamed x18, local copies, waits for them, and re-layouts  7.01 us
    pallas_call x1, Pallas kernels, body(): pl.pallas_call(sweep_kernel, out_shape=[shape(2, rows, cells_y), shape(2,...  2.86 us
    pallas_call x1, Pallas kernels, body(): pl.pallas_call(functools.partial(send_kernel, groups, count, tile), out_s...  2.79 us
    ppermute x7, starting transfers between devices, body(): got.append(lax.ppermute(pays[step], 'gx', pairs))  2.38 us
    pallas_call x1, Pallas kernels, body(): pl.pallas_call(functools.partial(widen_kernel, tile), out_shape=[shape(le...  2.22 us
  transfers between devices with their start and end apart: 13, of which 7 were waited for; matrix products, arithmetic and copies ran while one was open for 0% of the time, Pallas kernels for 7%

profile of v1, /device:TPU:11, one launch (start us, length us, event | category | flops | bytes accessed | tf_op | source)
XLA Modules:
  0.0 70.4 jit_solution(12627333442912644554)
XLA Ops:
  0.0 0.7 bitcast_convert_fusion.refs_2_
  0.7 0.0 copy-start
  0.7 1.2 %copy-done = bf16[1,16,2,128,128]{4,3,2,1,0:T(8,128)(2,1)S(1)} copy-done((bf16[1,16,2,128,128]{4,3,2,1,0:T(8,128)(2,1)S(1)}, bf16[1,16,2,128,128]{4,3,2,1,0:T(8,128)(2,1)}, u32[]{:S(2)}) %copy-start) | copy-done | bytes 1048600
  1.9 0.0 copy-start.1
  1.9 0.9 %copy-done.1 = bf16[2,256,256]{2,1,0:T(8,128)(2,1)S(1)} copy-done((bf16[2,256,256]{2,1,0:T(8,128)(2,1)S(1)}, bf16[2,256,256]{2,1,0:T(8,128)(2,1)}, u32[]{:S(2)}) %copy-start.1) | copy-done | bytes 262168
  2.8 0.0 copy-start.3
  2.8 0.9 %copy-done.3 = f32[256,256]{1,0:T(8,128)S(1)} copy-done((f32[256,256]{1,0:T(8,128)S(1)}, f32[256,256]{1,0:T(8,128)}, u32[]{:S(2)}) %copy-start.3) | copy-done | bytes 262168
  3.8 0.0 copy-start.4
  3.8 0.9 %copy-done.4 = f32[256,256]{1,0:T(8,128)S(1)} copy-done((f32[256,256]{1,0:T(8,128)S(1)}, f32[256,256]{1,0:T(8,128)}, u32[]{:S(2)}) %copy-start.4) | copy-done | bytes 262168
  4.7 0.0 copy-start.5
  4.7 0.9 %copy-done.5 = bf16[2,256,256]{2,1,0:T(8,128)(2,1)S(1)} copy-done((bf16[2,256,256]{2,1,0:T(8,128)(2,1)S(1)}, bf16[2,256,256]{2,1,0:T(8,128)(2,1)}, u32[]{:S(2)}) %copy-start.5) | copy-done | bytes 262168
  5.7 0.0 copy-start.6
  5.7 0.7 copy-done.6
  6.4 0.0 copy-start.7
  6.4 0.7 copy-done.7
  7.0 0.0 copy-start.8
  7.0 0.7 copy-done.8
  7.7 0.0 copy-start.2
  7.7 2.8 %send.1 = (bf16[33,16,128]{2,1,0:T(8,128)(2,1)S(1)}, bf16[33,16,128]{2,1,0:T(8,128)(2,1)S(1)}, bf16[33,16,128]{2,1,0:T(8,128)(2,1)S(1)}, bf16[33,16,128]{2,1,0:T...) custom-call(s32[16]{0:T(128)S(1)} %bitcast.7, ...), custom_call_target="tpu_custom_call" | custom-call | tf_op jit(solution)/shard_map/send/pallas_call | solution.py:353
  10.5 0.3 collective-permute-start
  10.8 0.0 collective-permute-start.1
  10.8 5.4 %collective-permute-start.7 = (f32[16,256]{1,0:T(8,128)S(1)}, f32[16,256]{1,0:T(8,128)S(1)}, u32[]{:S(2)}, u32[]{:S(2)}) collective-permute-start(f32[16,256]{1,0:T(8,128)S(1)} %get-tuple-element.35), channel_id=1, source_target_pairs={{0,4},{4,8},{8,12},{12,16},{16,20},{20,24},{24,28},{1,5},{5,9},{9,... | collective-permute-start | bytes 49160 | tf_op jit(solution)/shard_map/ppermute | solution.py:32
  16.2 1.9 %collective-permute-start.8 = (f32[16,256]{1,0:T(8,128)S(1)}, f32[16,256]{1,0:T(8,128)S(1)}, u32[]{:S(2)}, u32[]{:S(2)}) collective-permute-start(f32[16,256]{1,0:T(8,128)S(1)} %get-tuple-element.36), channel_id=1, source_target_pairs={{4,0},{8,4},{12,8},{16,12},{20,16},{24,20},{28,24},{5,1},{9,5},{13... | collective-permute-start | bytes 49160 | tf_op jit(solution)/shard_map/ppermute | solution.py:32
  18.1 0.0 collective-permute-done.7.low
  18.2 3.4 %collective-permute-done.8.high = f32[16,256]{1,0:T(8,128)S(1)} collective-permute-done((f32[16,256]{1,0:T(8,128)S(1)}, f32[16,256]{1,0:T(8,128)S(1)}, u32[]{:S(2)}, u32[]{:S(2)}) %collective-permute-start.8) | collective-permute-done | bytes 16416 | tf_op jit(solution)/shard_map/ppermute | solution.py:32
  21.6 0.0 copy-done.2
  21.6 2.2 %widen.1 = (f32[7,288,256]{2,1,0:T(8,128)S(1)}, f32[16,384]{1,0:T(8,128)S(1)}, f32[16,384]{1,0:T(8,128)S(1)}) custom-call(s32[2,2]{1,0:T(2,128)S(1)} %copy-done.6, bf16[2,256,256]{2,1,0:T(8,128)(2,1)S(1)} %copy-done.2, f32[256,256]{1,0:T(8,128)S(1)} %copy-done.3, f32[256,256]{1,0:T(8,128)S(1)} %copy-done.4, bf16[2,256,256]{2,1,0:T(8,128)(2,1)S(1)} %copy-done.5, ...), custom_call_target="tpu_custom_call" | custom-call | tf_op jit(solution)/shard_map/widen/pallas_call | solution.py:379
  23.8 5.7 %collective-permute-start.9 = (f32[16,384]{1,0:T(8,128)S(1)}, f32[16,384]{1,0:T(8,128)S(1)}, u32[]{:S(2)}, u32[]{:S(2)}) collective-permute-start(f32[16,384]{1,0:T(8,128)S(1)} %get-tuple-element.38), channel_id=1, source_target_pairs={{0,1},{1,2},{2,3},{4,5},{5,6},{6,7},{8,9},{9,10},{10,11},{12,13},{... | collective-permute-start | bytes 73736 | tf_op jit(solution)/shard_map/ppermute | solution.py:32
  29.5 1.9 %collective-permute-start.10 = (f32[16,384]{1,0:T(8,128)S(1)}, f32[16,384]{1,0:T(8,128)S(1)}, u32[]{:S(2)}, u32[]{:S(2)}) collective-permute-start(f32[16,384]{1,0:T(8,128)S(1)} %get-tuple-element.39), channel_id=1, source_target_pairs={{1,0},{2,1},{3,2},{5,4},{6,5},{7,6},{9,8},{10,9},{11,10},{13,12},{... | collective-permute-start | bytes 73736 | tf_op jit(solution)/shard_map/ppermute | solution.py:32
  31.5 0.1 collective-permute-start.2
  31.5 0.0 collective-permute-done.9.left
  31.6 0.6 collective-permute-start.3
  32.2 2.8 %collective-permute-done.10.right = f32[16,384]{1,0:T(8,128)S(1)} collective-permute-done((f32[16,384]{1,0:T(8,128)S(1)}, f32[16,384]{1,0:T(8,128)S(1)}, u32[]{:S(2)}, u32[]{:S(2)}) %collective-permute-start.10) | collective-permute-done | bytes 24608 | tf_op jit(solution)/shard_map/ppermute | solution.py:32
  35.0 0.0 collective-permute-start.4
  35.0 0.0 collective-permute-done.refs_1_
  35.0 0.2 collective-permute-start.5
  35.2 0.0 collective-permute-done.1.refs_2_
  35.2 1.2 %collective-permute-start.6 = (bf16[33,16,128]{2,1,0:T(8,128)(2,1)S(1)}, bf16[33,16,128]{2,1,0:T(8,128)(2,1)S(1)}, u32[]{:S(2)}, u32[]{:S(2)}) collective-permute-start(bf16[33,16,128]{2,1,0:T(8,128)(2,1)S(1)} %get-tuple-element.34), channel_id=1, source_target_pairs={{0,28},{4,24},{8,20},{12,16},{16,12},{20,8},{24,4},{28,0},{1,29},{... | collective-permute-start | bytes 405512 | tf_op jit(solution)/shard_map/ppermute | solution.py:378
  36.4 2.9 %sweep.1 = (f32[2,288,256]{2,1,0:T(8,128)S(1)}, f32[2,288,256]{2,1,0:T(8,128)S(1)}, f32[2,256,256]{2,1,0:T(8,128)S(1)}, f32[2,256,256]{2,1,0:T(8,128)S(1)}, f32[288,384]{1,0:T(8,128)S(1)}) custom-call(f32[7,288,256]{2,1,0:T(8,128)S(1)} %get-tuple-element.37.ext.refs_10_, f32[16,384]{1,0:T(8,128)S(1)} %collective-permute-done.9.left, ...), custom_call_target="tpu_custom_call" | custom-call | tf_op jit(solution)/shard_map/sweep/pallas_call | solution.py:389
  39.2 0.0 collective-permute-done.2.refs_3_
  39.2 7.0 %collective-permute-done.3.refs_4_ = bf16[33,16,128]{2,1,0:T(8,128)(2,1)S(1)} collective-permute-done((bf16[33,16,128]{2,1,0:T(8,128)(2,1)S(1)}, bf16[33,16,128]{2,1,0:T(8,128)(2,1)S(1)}, u32[]{:S(2)}, u32[]{:S(2)}) %collective-permute-start.3) | collective-permute-done | bytes 135200 | tf_op jit(solution)/shard_map/ppermute | solution.py:378
  46.3 2.9 %collective-permute-done.4.refs_5_ = bf16[33,16,128]{2,1,0:T(8,128)(2,1)S(1)} collective-permute-done((bf16[33,16,128]{2,1,0:T(8,128)(2,1)S(1)}, bf16[33,16,128]{2,1,0:T(8,128)(2,1)S(1)}, u32[]{:S(2)}, u32[]{:S(2)}) %collective-permute-start.4) | collective-permute-done | bytes 135200 | tf_op jit(solution)/shard_map/ppermute | solution.py:378
  49.2 4.4 %collective-permute-done.5.refs_6_ = bf16[33,16,128]{2,1,0:T(8,128)(2,1)S(1)} collective-permute-done((bf16[33,16,128]{2,1,0:T(8,128)(2,1)S(1)}, bf16[33,16,128]{2,1,0:T(8,128)(2,1)S(1)}, u32[]{:S(2)}, u32[]{:S(2)}) %collective-permute-start.5) | collective-permute-done | bytes 135200 | tf_op jit(solution)/shard_map/ppermute | solution.py:378
  53.6 3.9 %collective-permute-done.6.refs_7_ = bf16[33,16,128]{2,1,0:T(8,128)(2,1)S(1)} collective-permute-done((bf16[33,16,128]{2,1,0:T(8,128)(2,1)S(1)}, bf16[33,16,128]{2,1,0:T(8,128)(2,1)S(1)}, u32[]{:S(2)}, u32[]{:S(2)}) %collective-permute-start.6) | collective-permute-done | bytes 135200 | tf_op jit(solution)/shard_map/ppermute | solution.py:378
  57.4 1.7 %misfit.1 = (f32[2,256,256]{2,1,0:T(8,128)S(1)}, f32[2,288,256]{2,1,0:T(8,128)S(1)}, f32[8,384]{1,0:T(8,128)S(1)}, f32[8,384]{1,0:T(8,128)S(1)}) custom-call(bf16[33,16,128]{2,1,0:T(8,128)(2,1)S(1)} %get-tuple-element.27.refs_0_, bf16[33,16,128]{2,1,0:T(8,128)(2,1)S(1)} %collective-permute-done.refs_1_, ...), custom_call_target="tpu_custom_call" | custom-call | tf_op jit(solution)/shard_map/misfit/pallas_call | solution.py:401
  59.2 4.4 %collective-permute-start.11 = (f32[8,384]{1,0:T(8,128)S(1)}, f32[8,384]{1,0:T(8,128)S(1)}, u32[]{:S(2)}, u32[]{:S(2)}) collective-permute-start(f32[8,384]{1,0:T(8,128)S(1)} %get-tuple-element.44), channel_id=1, source_target_pairs={{0,1},{1,2},{2,3},{4,5},{5,6},{6,7},{8,9},{9,10},{10,11},{12,13},{... | collective-permute-start | bytes 36872 | tf_op jit(solution)/shard_map/ppermute | solution.py:32
  63.6 1.9 %collective-permute-start.12 = (f32[8,384]{1,0:T(8,128)S(1)}, f32[8,384]{1,0:T(8,128)S(1)}, u32[]{:S(2)}, u32[]{:S(2)}) collective-permute-start(f32[8,384]{1,0:T(8,128)S(1)} %get-tuple-element.45), channel_id=1, source_target_pairs={{1,0},{2,1},{3,2},{5,4},{6,5},{7,6},{9,8},{10,9},{11,10},{13,12},{... | collective-permute-start | bytes 36872 | tf_op jit(solution)/shard_map/ppermute | solution.py:32
  65.5 0.0 collective-permute-done.11.left
  65.5 3.1 %collective-permute-done.12.right = f32[8,384]{1,0:T(8,128)S(1)} collective-permute-done((f32[8,384]{1,0:T(8,128)S(1)}, f32[8,384]{1,0:T(8,128)S(1)}, u32[]{:S(2)}, u32[]{:S(2)}) %collective-permute-start.12) | collective-permute-done | bytes 12320 | tf_op jit(solution)/shard_map/ppermute | solution.py:32
  68.6 1.8 %grad.1 = f32[256,256]{1,0:T(8,128)} custom-call(f32[2,288,256]{2,1,0:T(8,128)S(1)} %get-tuple-element.42.lift, f32[2,256,256]{2,1,0:T(8,128)S(1)} %get-tuple-element.43.misfit, f32[8,384]{1,0:T(8,128)S(1)} %collective-permute-done.11.left, f32[8,384]{1,0:T(8,128)S(1)} %collective-permute-done.12.right, f32[7,288,256]{2,1,0:T(8,128)S(1)} %get-tuple-element.37.ext.refs_10_, ...), custom_call_target="tpu_custom_call" | custom-call | tf_op jit(solution)/shard_map/grad/pallas_call | solution.py:412
Async XLA Ops:
  0.7 1.2 %copy-start = (bf16[1,16,2,128,128]{4,3,2,1,0:T(8,128)(2,1)S(1)}, bf16[1,16,2,128,128]{4,3,2,1,0:T(8,128)(2,1)}, u32[]{:S(2)}) copy-start(bf16[1,16,2,128,128]{4,3,2,1,0:T(8,128)(2,1)} %param.13) | copy-start | bytes 3145732
  1.9 0.9 %copy-start.1 = (bf16[2,256,256]{2,1,0:T(8,128)(2,1)S(1)}, bf16[2,256,256]{2,1,0:T(8,128)(2,1)}, u32[]{:S(2)}) copy-start(bf16[2,256,256]{2,1,0:T(8,128)(2,1)} %vel.1) | copy-start | bytes 786436
  2.8 0.9 %copy-start.3 = (f32[256,256]{1,0:T(8,128)S(1)}, f32[256,256]{1,0:T(8,128)}, u32[]{:S(2)}) copy-start(f32[256,256]{1,0:T(8,128)} %visc.1) | copy-start | bytes 786436
  3.8 0.9 %copy-start.4 = (f32[256,256]{1,0:T(8,128)S(1)}, f32[256,256]{1,0:T(8,128)}, u32[]{:S(2)}) copy-start(f32[256,256]{1,0:T(8,128)} %fric.1) | copy-start | bytes 786436
  4.7 0.9 %copy-start.5 = (bf16[2,256,256]{2,1,0:T(8,128)(2,1)S(1)}, bf16[2,256,256]{2,1,0:T(8,128)(2,1)}, u32[]{:S(2)}) copy-start(bf16[2,256,256]{2,1,0:T(8,128)(2,1)} %drive.1) | copy-start | bytes 786436
  5.7 0.7 copy-start.6
  6.4 0.7 copy-start.7
  7.0 0.7 copy-start.8
  7.7 13.9 %copy-start.2 = (bf16[2,256,256]{2,1,0:T(8,128)(2,1)S(1)}, bf16[2,256,256]{2,1,0:T(8,128)(2,1)}, u32[]{:S(2)}) copy-start(bf16[2,256,256]{2,1,0:T(8,128)(2,1)} %vel.1) | copy-start | bytes 786436
  10.5 24.5 %collective-permute-start = (bf16[33,16,128]{2,1,0:T(8,128)(2,1)S(1)}, bf16[33,16,128]{2,1,0:T(8,128)(2,1)S(1)}, u32[]{:S(2)}, u32[]{:S(2)}) collective-permute-start(bf16[33,16,128]{2,1,0:T(8,128)(2,1)S(1)} %get-tuple-element.28), channel_id=1, source_target_pairs={{0,4},{4,0},{8,12},{12,8},{16,20},{20,16},{24,28},{28,24},{1,5},{5... | collective-permute-start | bytes 405512 | tf_op jit(solution)/shard_map/ppermute | solution.py:378
  10.8 24.4 %collective-permute-start.1 = (bf16[33,16,128]{2,1,0:T(8,128)(2,1)S(1)}, bf16[33,16,128]{2,1,0:T(8,128)(2,1)S(1)}, u32[]{:S(2)}, u32[]{:S(2)}) collective-permute-start(bf16[33,16,128]{2,1,0:T(8,128)(2,1)S(1)} %get-tuple-element.29), channel_id=1, source_target_pairs={{0,8},{4,12},{8,0},{12,4},{16,24},{20,28},{24,16},{28,20},{1,9},{5... | collective-permute-start | bytes 405512 | tf_op jit(solution)/shard_map/ppermute | solution.py:378
  10.8 7.4 %collective-permute-start.7 = (f32[16,256]{1,0:T(8,128)S(1)}, f32[16,256]{1,0:T(8,128)S(1)}, u32[]{:S(2)}, u32[]{:S(2)}) collective-permute-start(f32[16,256]{1,0:T(8,128)S(1)} %get-tuple-element.35), channel_id=1, source_target_pairs={{0,4},{4,8},{8,12},{12,16},{16,20},{20,24},{24,28},{1,5},{5,9},{9,... | collective-permute-start | bytes 49160 | tf_op jit(solution)/shard_map/ppermute | solution.py:32
  16.2 5.4 %collective-permute-start.8 = (f32[16,256]{1,0:T(8,128)S(1)}, f32[16,256]{1,0:T(8,128)S(1)}, u32[]{:S(2)}, u32[]{:S(2)}) collective-permute-start(f32[16,256]{1,0:T(8,128)S(1)} %get-tuple-element.36), channel_id=1, source_target_pairs={{4,0},{8,4},{12,8},{16,12},{20,16},{24,20},{28,24},{5,1},{9,5},{13... | collective-permute-start | bytes 49160 | tf_op jit(solution)/shard_map/ppermute | solution.py:32
  23.8 7.7 %collective-permute-start.9 = (f32[16,384]{1,0:T(8,128)S(1)}, f32[16,384]{1,0:T(8,128)S(1)}, u32[]{:S(2)}, u32[]{:S(2)}) collective-permute-start(f32[16,384]{1,0:T(8,128)S(1)} %get-tuple-element.38), channel_id=1, source_target_pairs={{0,1},{1,2},{2,3},{4,5},{5,6},{6,7},{8,9},{9,10},{10,11},{12,13},{... | collective-permute-start | bytes 73736 | tf_op jit(solution)/shard_map/ppermute | solution.py:32
  29.5 5.4 %collective-permute-start.10 = (f32[16,384]{1,0:T(8,128)S(1)}, f32[16,384]{1,0:T(8,128)S(1)}, u32[]{:S(2)}, u32[]{:S(2)}) collective-permute-start(f32[16,384]{1,0:T(8,128)S(1)} %get-tuple-element.39), channel_id=1, source_target_pairs={{1,0},{2,1},{3,2},{5,4},{6,5},{7,6},{9,8},{10,9},{11,10},{13,12},{... | collective-permute-start | bytes 73736 | tf_op jit(solution)/shard_map/ppermute | solution.py:32
  31.5 7.8 %collective-permute-start.2 = (bf16[33,16,128]{2,1,0:T(8,128)(2,1)S(1)}, bf16[33,16,128]{2,1,0:T(8,128)(2,1)S(1)}, u32[]{:S(2)}, u32[]{:S(2)}) collective-permute-start(bf16[33,16,128]{2,1,0:T(8,128)(2,1)S(1)} %get-tuple-element.30), channel_id=1, source_target_pairs={{0,12},{4,8},{8,4},{12,0},{16,28},{20,24},{24,20},{28,16},{1,13},{... | collective-permute-start | bytes 405512 | tf_op jit(solution)/shard_map/ppermute | solution.py:378
  31.6 14.7 %collective-permute-start.3 = (bf16[33,16,128]{2,1,0:T(8,128)(2,1)S(1)}, bf16[33,16,128]{2,1,0:T(8,128)(2,1)S(1)}, u32[]{:S(2)}, u32[]{:S(2)}) collective-permute-start(bf16[33,16,128]{2,1,0:T(8,128)(2,1)S(1)} %get-tuple-element.31), channel_id=1, source_target_pairs={{0,16},{4,20},{8,24},{12,28},{16,0},{20,4},{24,8},{28,12},{1,17},{... | collective-permute-start | bytes 405512 | tf_op jit(solution)/shard_map/ppermute | solution.py:378
  35.0 14.2 %collective-permute-start.4 = (bf16[33,16,128]{2,1,0:T(8,128)(2,1)S(1)}, bf16[33,16,128]{2,1,0:T(8,128)(2,1)S(1)}, u32[]{:S(2)}, u32[]{:S(2)}) collective-permute-start(bf16[33,16,128]{2,1,0:T(8,128)(2,1)S(1)} %get-tuple-element.32), channel_id=1, source_target_pairs={{0,20},{4,16},{8,28},{12,24},{16,4},{20,0},{24,12},{28,8},{1,21},{... | collective-permute-start | bytes 405512 | tf_op jit(solution)/shard_map/ppermute | solution.py:378
  35.0 18.6 %collective-permute-start.5 = (bf16[33,16,128]{2,1,0:T(8,128)(2,1)S(1)}, bf16[33,16,128]{2,1,0:T(8,128)(2,1)S(1)}, u32[]{:S(2)}, u32[]{:S(2)}) collective-permute-start(bf16[33,16,128]{2,1,0:T(8,128)(2,1)S(1)} %get-tuple-element.33), channel_id=1, source_target_pairs={{0,24},{4,28},{8,16},{12,20},{16,8},{20,12},{24,0},{28,4},{1,25},{... | collective-permute-start | bytes 405512 | tf_op jit(solution)/shard_map/ppermute | solution.py:378
  35.2 22.3 %collective-permute-start.6 = (bf16[33,16,128]{2,1,0:T(8,128)(2,1)S(1)}, bf16[33,16,128]{2,1,0:T(8,128)(2,1)S(1)}, u32[]{:S(2)}, u32[]{:S(2)}) collective-permute-start(bf16[33,16,128]{2,1,0:T(8,128)(2,1)S(1)} %get-tuple-element.34), channel_id=1, source_target_pairs={{0,28},{4,24},{8,20},{12,16},{16,12},{20,8},{24,4},{28,0},{1,29},{... | collective-permute-start | bytes 405512 | tf_op jit(solution)/shard_map/ppermute | solution.py:378
  59.2 6.3 %collective-permute-start.11 = (f32[8,384]{1,0:T(8,128)S(1)}, f32[8,384]{1,0:T(8,128)S(1)}, u32[]{:S(2)}, u32[]{:S(2)}) collective-permute-start(f32[8,384]{1,0:T(8,128)S(1)} %get-tuple-element.44), channel_id=1, source_target_pairs={{0,1},{1,2},{2,3},{4,5},{5,6},{6,7},{8,9},{9,10},{10,11},{12,13},{... | collective-permute-start | bytes 36872 | tf_op jit(solution)/shard_map/ppermute | solution.py:32
  63.6 5.0 %collective-permute-start.12 = (f32[8,384]{1,0:T(8,128)S(1)}, f32[8,384]{1,0:T(8,128)S(1)}, u32[]{:S(2)}, u32[]{:S(2)}) collective-permute-start(f32[8,384]{1,0:T(8,128)S(1)} %get-tuple-element.45), channel_id=1, source_target_pairs={{1,0},{2,1},{3,2},{5,4},{6,5},{7,6},{9,8},{10,9},{11,10},{13,12},{... | collective-permute-start | bytes 36872 | tf_op jit(solution)/shard_map/ppermute | solution.py:32

commit v2 on v0

v2 whole, which is shorter than its diff:
```python
import functools

import jax
import jax.numpy as jnp
from jax import lax
from jax.experimental import pallas as pl
from jax.experimental.pallas import tpu as pltpu
from jax.sharding import PartitionSpec as P

CAP = 2
OMEGA = 0.6
LANE = 128
PAD = 16
PACK = 16
FIELDS = ((0, 3), (3, 3), (6, 3), (9, 2), (11, 2), (13, 2), (15, 1))
U, V, VISC, FRIC, DRIVE_U, DRIVE_V, ICE = range(7)
SCENES = PACK

VMEM = pl.BlockSpec(memory_space=pltpu.VMEM)
HBM = pl.BlockSpec(memory_space=pltpu.HBM)
F32 = jnp.float32


def partner(me, step, count):
    if count & (count - 1) == 0:
        return me ^ step
    return (me + step) % count


def from_behind(value, axis, steps):
    count = lax.axis_size(axis)
    first, last = (max(0, -steps), min(count, count - steps))
    return lax.ppermute(value, axis, [(source, source + steps) for source in range(first, last)])


def after(value, *others):
    return lax.optimization_barrier((value, *others))[0]


def in_place(*values):
    return [pltpu.with_memory_space_constraint(value, pltpu.HBM) for value in values]


def copy_all(pairs, sems, first=0):
    copies = [
        pltpu.make_async_copy(source, target, sems.at[first + number])
        for number, (source, target) in enumerate(pairs)
    ]
    for copy in copies:
        copy.start()
    return copies


def wait_all(copies):
    for copy in copies:
        copy.wait()


def ice_line(values, shape, tile):
    lane = lax.broadcasted_iota(jnp.int32, shape, 1)
    line = jnp.zeros(shape, F32)
    for number, value in enumerate(values):
        line = jnp.where(lane // tile == number, value.astype(F32), line)
    return line


def fill_places(place, filled, groups, count, owner_of):
    for index in range((groups + 2) * CAP):
        place[index] = -1
    for index in range(groups):
        filled[index] = 0
    for scene in range(count):
        who = owner_of(scene)
        rank = filled[who]
        place[(who + 1) * CAP + rank] = scene
        filled[who] = rank + 1


def columns_of(pick, block, precision):
    return lax.dot_general(
        pick, block, (((1,), (1,)), ((), ())), precision=precision, preferred_element_type=F32
    )


def load_scalars(owner, slot, weight, owner_s, slot_s, weight_b, weight_v, weight_s, sems):
    loads = copy_all([(owner, owner_s), (slot, slot_s), (weight, weight_b)], sems)
    loads[2].wait()
    weight_v[...] = weight_b[...].astype(F32)
    loads[2] = pltpu.make_async_copy(weight_v, weight_s, sems.at[2])
    loads[2].start()
    return loads


def easting_block(to, place, slot_s, weight_s, edge):
    row = lax.broadcasted_iota(jnp.int32, (PACK, LANE), 0)
    lane = lax.broadcasted_iota(jnp.int32, (PACK, LANE), 1)
    block = jnp.zeros((PACK, LANE), F32)
    for side in range(2):
        for rank in range(CAP):
            spot = place[(to + (2 if side == 0 else 0)) * CAP + rank]
            scene = jnp.maximum(spot, 0)
            amount = jnp.where(spot >= 0, weight_s[0, scene], 0.0)
            where = slot_s[0, scene]
            for part in range(2):
                line = edge(scene, part, side).astype(F32)
                line = line[0:1] if side == 0 else line[PACK - 1 : PACK]
                block = jnp.where(row == (side * CAP + rank) * 2 + part, line, block)
                value = jnp.where(where == side * 2 + part, amount, 0.0)
                block = jnp.where((row == 8) & (lane == 8 + (side * CAP + rank) * 2 + part), value, block)
    for rank in range(CAP):
        spot = place[(to + 1) * CAP + rank]
        scene = jnp.maximum(spot, 0)
        amount = jnp.where(spot >= 0, weight_s[0, scene], 0.0)
        for position in range(4):
            value = jnp.where(slot_s[0, scene] == position, amount, 0.0)
            block = jnp.where((row == 8) & (lane == rank * 4 + position), value, block)
    return block.astype(jnp.bfloat16)


def gather_scenes(obs, pays, steps, place, groups, blocks, me, sems):
    copies = []
    for number, step in enumerate(steps):
        to = partner(me, step, groups)
        for rank in range(CAP):
            scene = jnp.maximum(place[(to + 1) * CAP + rank], 0)
            target = pays[number].at[pl.ds(rank * 2 * blocks, 2 * blocks)]
            copies += copy_all([(obs.at[scene], target)], sems, number * CAP + rank)
    return copies


def send_kernel(groups, count, tile, steps, *refs):
    owner, slot, weight, obs = refs[:4]
    pays = refs[4 : 4 + len(steps)]
    owner_s, slot_s, weight_b, weight_v, weight_s, edges, place, filled, scalar_sem, edge_sem, scene_sem = refs[
        4 + len(steps) :
    ]
    blocks = tile // PACK
    me = lax.axis_index("gx")
    loads = copy_all(
        [(obs.at[:, at], edges.at[number]) for number, at in enumerate((0, blocks, blocks - 1, 2 * blocks - 1))], edge_sem
    )
    scalars = load_scalars(owner, slot, weight, owner_s, slot_s, weight_b, weight_v, weight_s, scalar_sem)
    scalars[0].wait()
    fill_places(place, filled, groups, count, lambda scene: owner_s[0, scene])
    copies = gather_scenes(obs, pays, steps, place, groups, blocks, me, scene_sem)
    wait_all(scalars[1:] + loads)
    for number, step in enumerate(steps):
        to = partner(me, step, groups)
        pays[number][CAP * 2 * blocks] = easting_block(
            to, place, slot_s, weight_s, lambda scene, part, side: edges[side * 2 + part, scene]
        )
    wait_all(copies)


def pack_kernel(groups, count, tile, steps, *refs):
    owner, slot, weight, ice, obs_h, vel_h, visc_h, fric_h, drive_h = refs[:9]
    pays = refs[9 : 9 + len(steps)]
    to_low, to_high = refs[9 + len(steps) : 11 + len(steps)]
    (
        owner_s, slot_s, weight_b, weight_v, weight_s, ice_s, owner_v, slot_v, obs, vel, visc, fric, drive,
        place, filled, scalar_sem, more_sem, load_sem, scene_sem,
    ) = refs[11 + len(steps) :]
    blocks = tile // PACK
    me = lax.axis_index("gx")
    loads = copy_all([(vel_h, vel), (drive_h, drive), (visc_h, visc), (fric_h, fric), (obs_h, obs)], load_sem)
    more = copy_all([(ice, ice_s), (owner, owner_v), (slot, slot_v)], more_sem)
    scalars = load_scalars(owner, slot, weight, owner_s, slot_s, weight_b, weight_v, weight_s, scalar_sem)
    scalars[0].wait()
    fill_places(place, filled, groups, count, lambda scene: owner_s[0, scene])
    copies = gather_scenes(obs_h, pays, steps, place, groups, blocks, me, scene_sem)
    picked = lax.broadcasted_iota(jnp.int32, (8, LANE), 0)
    across = lax.broadcasted_iota(jnp.int32, (8, LANE), 1)
    cells_y = visc.shape[1]

    def pick(first, kind):
        return (across == picked + first).astype(kind)

    wait_all(loads[:4])
    for index, (at, depth) in enumerate(FIELDS[:-1]):
        for target, low, first in ((to_low, 0, 0), (to_high, cells_y - LANE, LANE - depth)):
            lanes = slice(low, low + LANE)
            if index in (VISC, FRIC):
                field = (visc if index == VISC else fric)[:, lanes]
                rows = columns_of(pick(first, F32), field, lax.Precision.HIGHEST)
            else:
                field = vel[index, :, lanes] if index in (U, V) else drive[index - DRIVE_U, :, lanes]
                rows = columns_of(pick(first, jnp.bfloat16), field, None)
            target[at : at + depth, :] = rows[0:depth]
    loads[4].wait()
    both = (across == jnp.where(picked == 0, 0, LANE - 1)).astype(jnp.bfloat16)
    for scene in range(count):
        rows = columns_of(both, obs[scene].reshape(2 * tile, LANE), None)
        to_low[SCENES + scene : SCENES + scene + 1, :] = rows[0:1]
        to_high[SCENES + scene : SCENES + scene + 1, :] = rows[1:2]
    wait_all(scalars[1:] + more)
    for target, at in ((to_low, 0), (to_high, ice_s.shape[1] - 1)):
        target[SCENES + count :, :] = jnp.zeros((8, target.shape[1]), F32)
        for number, values in enumerate((owner_v, slot_v, weight_v)):
            target[SCENES + count + number : SCENES + count + number + 1, 0:count] = values[...].astype(F32)
        row = FIELDS[ICE][0]
        target[row : row + 1, :] = ice_line(
            [ice_s[number, at] for number in range(ice_s.shape[0])], (1, target.shape[1]), tile
        )
    for number, step in enumerate(steps):
        to = partner(me, step, groups)
        pays[number][CAP * 2 * blocks] = easting_block(
            to, place, slot_s, weight_s,
            lambda scene, part, side: obs[scene, part * blocks + (0 if side == 0 else blocks - 1)],
        )
    wait_all(copies)


def side_tiles(right, left, turned):
    turned[...] = jnp.zeros_like(turned)
    turned[0:PACK, :] = right[0:PACK, :]
    turned[PACK : 2 * PACK, :] = left[0:PACK, :]
    return jnp.transpose(turned[...])


def side_tile(upright, index):
    at, depth = FIELDS[index]
    lane = lax.broadcasted_iota(jnp.int32, upright.shape, 1)
    after = pltpu.roll(upright, (LANE - at) % LANE, 1)
    before = pltpu.roll(upright, LANE - depth - PACK - at, 1)
    return jnp.where(lane < depth, after, jnp.where(lane >= LANE - depth, before, 0.0))


def widen_kernel(groups, count, tile, early, late, *refs):
    ice, vel, visc, fric, drive, right, left = refs[:7]
    pays = refs[7 + len(late) : 7 + 2 * len(late)]
    apart = refs[7 + 2 * len(late) : 7 + 2 * len(late) + len(early)]
    to_low, to_high = refs[7 + 2 * len(late) + len(early) : 9 + 2 * len(late) + len(early)]
    ice_s, notes, first_b, last_b, first_f, last_f, turned, place, filled, sems = refs[
        9 + 2 * len(late) + len(early) :
    ]
    cells = visc.shape[0]
    cells_y = visc.shape[1]
    blocks = tile // PACK
    me = lax.axis_index("gx")
    tail = pl.ds(SCENES + count, 8)
    loads = copy_all(
        [
            (right.at[tail], notes.at[0]), (left.at[tail], notes.at[1]), (ice, ice_s),
            (vel.at[:, 0:16], first_b.at[0:2]), (drive.at[:, 0:16], first_b.at[2:4]),
            (vel.at[:, cells - 16 : cells], last_b.at[0:2]), (drive.at[:, cells - 16 : cells], last_b.at[2:4]),
            (visc.at[0:8], first_f.at[0]), (fric.at[0:8], first_f.at[1]),
            (visc.at[cells - 8 : cells], last_f.at[0]), (fric.at[cells - 8 : cells], last_f.at[1]),
        ],
        sems,
    )
    upright = side_tiles(right, left, turned)
    wait_all(loads)
    for index, (at, depth) in enumerate(FIELDS):
        if index == ICE:
            first, last = (
                ice_line([ice_s[number, column] for column in range(ice_s.shape[1])], (1, cells_y), tile)
                for number in (0, ice_s.shape[0] - 1)
            )
        elif index in (VISC, FRIC):
            first, last = first_f[index - VISC], last_f[index - VISC]
        else:
            number = index if index in (U, V) else index - DRIVE_U + 2
            first, last = first_b[number].astype(F32), last_b[number].astype(F32)
        to_low[at : at + depth, 0:cells_y] = first[0:depth]
        to_high[at : at + depth, 0:cells_y] = last[last.shape[0] - depth :]
        to_low[at : at + depth, cells_y:] = side_tile(upright[0:8], index)[0:depth]
        to_high[at : at + depth, cells_y:] = side_tile(upright[cells - 8 :], index)[8 - depth : 8]
    packs = (right, left)
    for side in range(2):
        fill_places(place.at[side], filled, groups, count, lambda scene: notes[side, 0, scene].astype(jnp.int32))
    row = lax.broadcasted_iota(jnp.int32, (PACK, LANE), 0)
    lane = lax.broadcasted_iota(jnp.int32, (PACK, LANE), 1)
    for number, step in enumerate(late + early):
        to = partner(me, step, groups)
        block = jnp.zeros((PACK, LANE), F32)
        for side in range(2):
            for rank in range(CAP):
                spot = place[side, (to + 1) * CAP + rank]
                scene = jnp.maximum(spot, 0)
                amount = jnp.where(spot >= 0, notes[side, 2, scene], 0.0)
                where = notes[side, 1, scene].astype(jnp.int32)
                line = packs[side][pl.ds(SCENES + scene, 1), :]
                for part in range(2):
                    block = jnp.where(
                        row == (side * CAP + rank) * 2 + part, line[:, part * LANE : (part + 1) * LANE], block
                    )
                    value = jnp.where(where == part * 2 + side, amount, 0.0)
                    block = jnp.where((row == 8) & (lane == (side * CAP + rank) * 2 + part), value, block)
                spot = place[side, (to + (0 if side == 0 else 2)) * CAP + rank]
                scene = jnp.maximum(spot, 0)
                amount = jnp.where(spot >= 0, notes[side, 2, scene], 0.0)
                where = notes[side, 1, scene].astype(jnp.int32)
                line = packs[side][pl.ds(SCENES + scene, 1), :]
                at = tile - 1 if side == 0 else 0
                base = 8 + side * 6 + rank * 3
                for part in range(2):
                    value = jnp.broadcast_to(line[:, part * LANE + at : part * LANE + at + 1], (1, LANE))
                    block = jnp.where((row == 8) & (lane == base + part), value, block)
                value = jnp.where(where == (2 if side == 0 else 1), amount, 0.0)
                block = jnp.where((row == 8) & (lane == base + 2), value, block)
        if number < len(late):
            pays[number][CAP * 2 * blocks + 1] = block.astype(jnp.bfloat16)
        else:
            apart[number - len(late)][0] = block.astype(jnp.bfloat16)


def stress_block(u, v, visc, low, rows, wide):
    here, after = pl.ds(low, rows), pl.ds(low + 1, rows)
    vel_u, vel_v = u[here, :], v[here, :]
    a_x = u[after, :] - vel_u
    b_x = v[after, :] - vel_v
    a_y = pltpu.roll(vel_u, wide - 1, 1) - vel_u
    b_y = pltpu.roll(vel_v, wide - 1, 1) - vel_v
    nu = visc[here, :]
    return nu * (4.0 * a_x + 2.0 * b_y), nu * (4.0 * b_y + 2.0 * a_x), nu * (a_y + b_x)


def image_block(sxx, syy, sxy, low, rows):
    here, before = pl.ds(low, rows), pl.ds(low - 1, rows)
    mid = sxy[here, :]
    push_u = sxx[before, :] - sxx[here, :] + pltpu.roll(mid, 1, 1) - mid
    side = syy[here, :]
    push_v = sxy[before, :] - mid + pltpu.roll(side, 1, 1) - side
    return push_u, push_v


def sweep_kernel(tile, ice, vel, visc, fric, drive, right, left, low_pack, high_pack, *refs):
    second, ease, lead, trail, wide_visc, wide_ice = refs[:6]
    (
        u, v, wide_fric, drive_u, drive_v, next_u, next_v, relax_u, relax_v, sxx, syy, sxy, turned,
        ice_s, sems,
    ) = refs[6:]
    cells, cells_y = visc.shape
    rows, wide = wide_visc.shape
    loads = copy_all([(ice, ice_s)], sems)
    upright = side_tiles(right, left, turned)
    wait_all(loads)
    own_rows = slice(PAD, PAD + cells)
    for index, field in enumerate((u, v, wide_visc, wide_fric, drive_u, drive_v, wide_ice)):
        at, depth = FIELDS[index]
        field[0:PAD, :] = jnp.zeros((PAD, wide), F32)
        field[PAD + cells :, :] = jnp.zeros((PAD, wide), F32)
        if index == ICE:
            for number in range(cells // tile):
                field[PAD + number * tile : PAD + (number + 1) * tile, 0:cells_y] = ice_line(
                    [ice_s[number, column] for column in range(ice_s.shape[1])], (tile, cells_y), tile
                )
        elif index in (VISC, FRIC):
            field[own_rows, 0:cells_y] = (visc if index == VISC else fric)[...]
        else:
            source = vel if index in (U, V) else drive
            field[own_rows, 0:cells_y] = source[index % DRIVE_U].astype(F32)
        field[own_rows, cells_y:wide] = side_tile(upright, index)
        field[PAD - depth : PAD, :] = low_pack[at : at + depth, :]
        field[PAD + cells : PAD + cells + depth, :] = high_pack[at : at + depth, :]
    blocks = range(8, rows - 8, 8)
    own = range(PAD, rows - PAD, 8)
    for low in blocks:
        here = pl.ds(low, 8)
        nu, drag = wide_visc[here, :], wide_fric[here, :]
        nu_x = wide_visc[pl.ds(low - 1, 8), :]
        nu_y = pltpu.roll(nu, 1, 1)
        inside = drag > 0.0
        for out, diag in ((relax_u, 5.0 * nu + 4.0 * nu_x + nu_y), (relax_v, 5.0 * nu + nu_x + 4.0 * nu_y)):
            out[here, :] = jnp.where(inside, 1.0 / jnp.where(inside, diag + drag, 1.0), 0.0)
    for low in blocks:
        here = pl.ds(low, 8)
        sxx[here, :], syy[here, :], sxy[here, :] = stress_block(u, v, wide_visc, low, 8, wide)
    for low in blocks:
        here = pl.ds(low, 8)
        pushes = image_block(sxx, syy, sxy, low, 8)
        for part, (push, speed, force, relax, after) in enumerate(
            zip(pushes, (u, v), (drive_u, drive_v), (relax_u, relax_v), (next_u, next_v))
        ):
            now, soft = speed[here, :], relax[here, :]
            move = soft * (force[here, :] - push - wide_fric[here, :] * now)
            after[here, :] = now + OMEGA * move
            slack = OMEGA * soft
            ease[part, here, :] = slack
            if low in own:
                factor = -wide_ice[here, 0:cells_y] * (slack * (move + now))[:, 0:cells_y]
                lead[part, pl.ds(low - PAD, 8), :] = factor
    for low in blocks:
        here = pl.ds(low, 8)
        sxx[here, :], syy[here, :], sxy[here, :] = stress_block(next_u, next_v, wide_visc, low, 8, wide)
    for low in blocks:
        here = pl.ds(low, 8)
        pushes = image_block(sxx, syy, sxy, low, 8)
        for part, (push, speed, force, relax) in enumerate(
            zip(pushes, (next_u, next_v), (drive_u, drive_v), (relax_u, relax_v))
        ):
            now = speed[here, :]
            move = relax[here, :] * (force[here, :] - push - wide_fric[here, :] * now)
            second[part, here, :] = wide_ice[here, :] * (now + OMEGA * move)
            if low in own:
                mine = pl.ds(low - PAD, 8)
                trail[part, mine, :] = (
                    -wide_ice[here, 0:cells_y] * (move + now)[:, 0:cells_y]
                    - wide_fric[here, 0:cells_y] * lead[part, mine, :]
                )


def final_kernel(groups, tile, early, *refs):
    pays = refs[:groups]
    apart = dict(zip(early, refs[groups : groups + len(early)]))
    second, ease, lead, trail, visc, ice = refs[groups + len(early) : groups + len(early) + 6]
    grad = refs[groups + len(early) + 6]
    misfit, u, v, sxx, syy, sxy, table, total, rows_x, rows_y, turned = refs[groups + len(early) + 7 :]
    rows, wide = visc.shape
    cells_y = wide - LANE
    cells = rows - 2 * PAD
    blocks = tile // PACK
    tiles_y = cells_y // tile
    slots = cells // tile * tiles_y
    lift = (u, v)
    for group in range(groups):
        rows_x[pl.ds(group, PACK, stride=groups), :] = pays[group][CAP * 2 * blocks].astype(F32)
        side = apart[group][0] if group in apart else pays[group][CAP * 2 * blocks + 1]
        rows_y[pl.ds(group, PACK, stride=groups), :] = side.astype(F32)

    def raw(source, number):
        return source[number * groups : (number + 1) * groups, :]

    def spread(source, number):
        return jnp.broadcast_to(raw(source, 8)[:, number : number + 1], (groups, LANE))

    def gathered(value):
        return jnp.sum(value, axis=0, keepdims=True)

    for position in range(slots):
        weights = [spread(rows_x, rank * slots + position) for rank in range(CAP)]
        for rank in range(CAP):
            at = (rank * slots + position) * groups
            table[at : at + groups, :] = weights[rank]
        total[position : position + 1, :] = gathered(sum(weights))
    for field in lift:
        field[0:PAD, :] = jnp.zeros((PAD, wide), F32)
        field[PAD + cells :, :] = jnp.zeros((PAD, wide), F32)
    turned[...] = jnp.zeros_like(turned)
    for side in range(2):
        at = PAD + cells if side == 0 else PAD - 1
        for column in range(2):
            lanes = slice(column * tile, (column + 1) * tile)
            weights = [spread(rows_x, 8 + (side * CAP + rank) * 2 + column) for rank in range(CAP)]
            weight = gathered(sum(weights))
            for part in range(2):
                seen = gathered(sum(weights[rank] * raw(rows_x, (side * CAP + rank) * 2 + part) for rank in range(CAP)))
                gap = weight * second[part, at : at + 1, lanes] - ice[at : at + 1, lanes] * seen
                lift[part][at : at + 1, lanes] = ease[part, at : at + 1, lanes] * gap
        lines = [[None] * 2 for _ in range(3)]
        for column in range(2):
            weights = [spread(rows_y, (side * CAP + rank) * 2 + column) for rank in range(CAP)]
            lines[2][column] = gathered(sum(weights))
            for part in range(2):
                lines[part][column] = gathered(
                    sum(weights[rank] * raw(rows_y, (side * CAP + rank) * 2 + part) for rank in range(CAP))
                )
        weights = [spread(rows_y, 8 + side * 6 + rank * 3 + 2) for rank in range(CAP)]
        corners = [
            gathered(sum(weights[rank] * spread(rows_y, 8 + side * 6 + rank * 3 + part) for rank in range(CAP)))
            for part in range(2)
        ] + [gathered(sum(weights))]
        lane = lax.broadcasted_iota(jnp.int32, (1, turned.shape[1]), 1)
        for number in range(3):
            line = jnp.concatenate(
                lines[number] + [jnp.zeros((1, turned.shape[1] - 2 * tile), F32)], axis=1
            )
            line = pltpu.roll(jnp.broadcast_to(line, (8, turned.shape[1])), PAD, 1)[0:1]
            corner = jnp.concatenate([corners[number]] * (turned.shape[1] // LANE), axis=1)
            line = jnp.where(lane == (PAD - 1 if side == 0 else PAD + cells), corner, line)
            at = number if side == 0 else LANE - 1 - number
            turned[at : at + 1, :] = line
    upright = jnp.transpose(turned[...])[0:rows]
    lane = lax.broadcasted_iota(jnp.int32, (rows, LANE), 1)

    def sides(number):
        after = pltpu.roll(upright, (LANE - number) % LANE, 1)
        before = pltpu.roll(upright, number, 1)
        return jnp.where(lane == 0, after, jnp.where(lane == LANE - 1, before, 0.0))

    weight = sides(2)
    for part in range(2):
        gap = weight * second[part, :, cells_y:wide] - ice[:, cells_y:wide] * sides(part)
        lift[part][:, cells_y:wide] = ease[part, :, cells_y:wide] * gap

    def step(index, carry):
        part, chunk = index // blocks, index % blocks
        sums = [jnp.zeros((PACK, LANE), F32) for _ in range(slots)]
        for group in range(groups):
            for rank in range(CAP):
                got = pays[group][rank * 2 * blocks + index].astype(F32)
                for position in range(slots):
                    sums[position] += table[pl.ds((rank * slots + position) * groups + group, 1), :] * got
        for position in range(slots):
            lanes = slice((position % tiles_y) * tile, (position % tiles_y + 1) * tile)
            at = pl.multiple_of((position // tiles_y) * tile + chunk * PACK, PACK)
            here = pl.ds(pl.multiple_of(at + PAD, PACK), PACK)
            gap = total[position : position + 1, :] * second[part, here, lanes] - ice[here, lanes] * sums[position]
            misfit[part, pl.ds(at, PACK), lanes] = gap
            sums[position] = ease[part, here, lanes] * gap

        for number, field in enumerate(lift):

            @pl.when(part == number)
            def _():
                for position in range(slots):
                    lanes = slice((position % tiles_y) * tile, (position % tiles_y + 1) * tile)
                    at = pl.multiple_of((position // tiles_y) * tile + chunk * PACK + PAD, PACK)
                    field[pl.ds(at, PACK), lanes] = sums[position]

        return carry

    lax.fori_loop(0, 2 * blocks, step, 0)
    for low in range(8, rows - PAD, 8):
        here = pl.ds(low, 8)
        sxx[here, :], syy[here, :], sxy[here, :] = stress_block(u, v, visc, low, 8, wide)
    for low in range(PAD, rows - PAD, 8):
        mine = pl.ds(low - PAD, 8)
        here = pl.ds(low, 8)
        sums = jnp.zeros((8, cells_y), F32)
        for part, push in enumerate(image_block(sxx, syy, sxy, low, 8)):
            sums += (misfit[part, mine, :] - push[:, 0:cells_y]) * lead[part, mine, :]
            sums += lift[part][here, 0:cells_y] * trail[part, mine, :]
        grad[mine, :] = sums


def body(vel0, visc, fric, drive, scene_obs, scene_weight, scene_owner, scene_slot, ice_mask):
    cells_x, cells_y = visc.shape
    tile = scene_obs.shape[-1]
    count = scene_obs.shape[1]
    groups = lax.axis_size("gx")
    blocks = tile // PACK
    rows, wide = cells_x + 2 * PAD, cells_y + LANE
    long = -(-rows // LANE) * LANE
    obs = scene_obs.reshape(count, 2 * blocks, PACK, LANE)
    owner, slot, weight = scene_owner.reshape(1, count), scene_slot, scene_weight
    limit = pltpu.CompilerParams(vmem_limit_bytes=40 << 20)
    dma = pltpu.SemaphoreType.DMA
    early = (groups // 2, groups // 2 + 1)
    late = tuple(step for step in range(groups) if step not in early)

    def shape(*dims, dtype=F32):
        return jax.ShapeDtypeStruct(dims, dtype)

    def short(*dims):
        return pltpu.VMEM(dims, jnp.bfloat16)

    def full(*dims):
        return pltpu.VMEM(dims, F32)

    bf16, i32 = jnp.bfloat16, jnp.int32
    deep = CAP * 2 * blocks
    tall = SCENES + count + 8
    pairs = {step: [(me, partner(me, step, groups)) for me in range(groups)] for step in range(1, groups)}
    scalars = [
        pltpu.SMEM((1, count), i32), pltpu.SMEM((1, count), i32), short(1, count), full(1, count),
        pltpu.SMEM((1, count), F32),
    ]
    places = [pltpu.SMEM(((groups + 2) * CAP,), i32), pltpu.SMEM((groups,), i32)]
    sent = pl.pallas_call(
        functools.partial(send_kernel, groups, count, tile, early),
        out_shape=[pltpu.VMEM((deep + 1, PACK, LANE), bf16)] * len(early),
        in_specs=[HBM] * 4,
        out_specs=[VMEM] * len(early),
        scratch_shapes=scalars + [short(4, count, PACK, LANE)] + places
        + [dma((3,)), dma((4,)), dma((len(early) * CAP,))],
        compiler_params=limit,
        name="send",
    )(*in_place(owner, slot, weight, obs))
    got = {step: lax.ppermute(value, "gx", pairs[step]) for step, value in zip(early, sent)}
    *pays, y_low, y_high = pl.pallas_call(
        functools.partial(pack_kernel, groups, count, tile, late),
        out_shape=[pltpu.VMEM((deep + 2, PACK, LANE), bf16)] * len(late) + [pltpu.VMEM((tall, cells_x), F32)] * 2,
        in_specs=[HBM] * 9,
        out_specs=[VMEM] * (len(late) + 2),
        scratch_shapes=scalars
        + [pltpu.SMEM(ice_mask.shape, i32), pltpu.VMEM((1, count), i32), pltpu.VMEM((1, count), i32)]
        + [short(*obs.shape), short(*vel0.shape), full(*visc.shape), full(*fric.shape), short(*drive.shape)] + places
        + [dma((3,)), dma((3,)), dma((5,)), dma((len(late) * CAP,))],
        compiler_params=limit,
        name="pack",
    )(*in_place(owner, slot, weight, ice_mask, obs, vel0, visc, fric, drive))
    right = from_behind(y_low, "gy", -1)
    left = from_behind(y_high, "gy", 1)
    outs = pl.pallas_call(
        functools.partial(widen_kernel, groups, count, tile, early, late),
        out_shape=[pltpu.VMEM((deep + 2, PACK, LANE), bf16)] * len(late)
        + [pltpu.VMEM((1, PACK, LANE), bf16)] * len(early)
        + [pltpu.VMEM((PACK, wide), F32)] * 2,
        in_specs=[HBM] * 5 + [VMEM] * (2 + len(late)),
        out_specs=[VMEM] * (len(late) + len(early) + 2),
        input_output_aliases={7 + number: number for number in range(len(late))},
        scratch_shapes=[
            pltpu.SMEM(ice_mask.shape, i32), pltpu.SMEM((2, 8, cells_x), F32), short(4, 16, cells_y),
            short(4, 16, cells_y), full(2, 8, cells_y), full(2, 8, cells_y), full(LANE, cells_x),
            pltpu.SMEM((2, (groups + 2) * CAP), i32), pltpu.SMEM((groups,), i32), dma((11,)),
        ],
        compiler_params=limit,
        name="widen",
    )(*in_place(ice_mask, vel0, visc, fric, drive), right, left, *pays)
    ready = dict(zip(late, outs))
    x_low, x_high = outs[-2:]
    high_pack = from_behind(x_low, "gx", -1)
    low_pack = from_behind(x_high, "gx", 1)
    got[0] = ready[0]
    for step in late[1:]:
        value = ready[step] if step > groups // 2 else after(ready[step], got[early[0]])
        got[step] = lax.ppermute(value, "gx", pairs[step])
    apart = [
        lax.ppermute(after(value, got[early[1]]), "gx", pairs[step])
        for step, value in zip(early, outs[len(late) :])
    ]
    base = pl.pallas_call(
        functools.partial(sweep_kernel, tile),
        out_shape=[shape(2, rows, wide)] * 2 + [shape(2, cells_x, cells_y)] * 2 + [shape(rows, wide)] * 2,
        in_specs=[HBM] + [VMEM] * 8,
        out_specs=[VMEM] * 6,
        scratch_shapes=[full(rows, wide)] * 12
        + [full(LANE, cells_x), pltpu.SMEM(ice_mask.shape, i32), dma((1,))],
        compiler_params=limit,
        name="sweep",
    )(ice_mask, vel0, visc, fric, drive, right, left, low_pack, high_pack)
    return pl.pallas_call(
        functools.partial(final_kernel, groups, tile, early),
        out_shape=shape(cells_x, cells_y),
        in_specs=[VMEM] * (groups + len(early) + 6),
        out_specs=VMEM,
        scratch_shapes=[full(2, cells_x, cells_y)] + [full(rows, wide)] * 5
        + [
            full(groups * CAP * 4, LANE), full(8, LANE), full(PACK * groups, LANE), full(PACK * groups, LANE),
            full(LANE, long),
        ],
        compiler_params=limit,
        name="final",
    )(*(got[step] for step in range(groups)), *apart, *base)


def solution(mesh):
    placed = (
        P(None, "gx", "gy"),
        P("gx", "gy"),
        P("gx", "gy"),
        P(None, "gx", "gy"),
        P("gy", "gx", None, None, None),
        P("gy", "gx"),
        P("gy", "gx", None),
        P("gy", "gx"),
        P("gx", "gy"),
    )
    return jax.shard_map(body, mesh=mesh, in_specs=placed, out_specs=P("gx", "gy"), check_vma=False)
```

time: 120 us -> 48.2 us (0.40)
  the two profiles are of different devices: /device:TPU:24 before, /device:TPU:0 now
where the time goes in v2:
time: 48.2 us; the launch traced here: 47.9 us
  starting transfers between devices  27.5 us (57%)
  Pallas kernels  13.9 us (29%)
  waiting for transfers between devices  6.34 us (13%)
    ppermute x5, starting transfers between devices, body(): got[step] = lax.ppermute(value, 'gx', pairs[step])  8.32 us
    ppermute x4, starting transfers between devices, from_behind(): lax.ppermute(value, axis, [(source, source + steps) for source in range(f...  7.83 us
    ppermute x2, starting transfers between devices, body(): lax.ppermute(after(value, got[early[1]]), 'gx', pairs[step])  5.97 us
    ppermute x5, waiting for transfers between devices, body(): got[step] = lax.ppermute(value, 'gx', pairs[step])  5.48 us
    ppermute x2, starting transfers between devices, body(): lax.ppermute(value, 'gx', pairs[step])  5.36 us
    pallas_call x1, Pallas kernels, body(): pl.pallas_call(functools.partial(sweep_kernel, tile), out_shape=[shape(2,...  3.84 us
    pallas_call x1, Pallas kernels, body(): pl.pallas_call(functools.partial(final_kernel, groups, tile, early), out_...  3.18 us
    pallas_call x1, Pallas kernels, body(): pl.pallas_call(functools.partial(pack_kernel, groups, count, tile, late),...  2.93 us
  transfers between devices with their start and end apart: 13, of which 5 were waited for; matrix products, arithmetic and copies ran while one was open for 0% of the time, Pallas kernels for 18%

profile of v2, /device:TPU:0, one launch (start us, length us, event | category | flops | bytes accessed | tf_op | source)
XLA Modules:
  0.0 47.9 jit_solution(9521676023593017063)
XLA Ops:
  0.0 1.9 %send.1 = (bf16[33,16,128]{2,1,0:T(8,128)(2,1)S(1)}, bf16[33,16,128]{2,1,0:T(8,128)(2,1)S(1)}) custom-call(s32[1,16]{1,0:T(1,128)} %bitcast.4, s32[1,16]{1,0:T(1,128)} %refs_1_.5, bf16[1,16]{1,0:T(2,128)(2,1)} %refs_2_.5, bf16[16,16,16,128]{3,2,1,0:T(8,128)(2,1)} %bitcast.2), custom_call_target="tpu_custom_call" | custom-call | tf_op jit(solution)/shard_map/send/pallas_call | solution.py:560
  1.9 5.0 %collective-permute-start.6 = (bf16[33,16,128]{2,1,0:T(8,128)(2,1)S(1)}, bf16[33,16,128]{2,1,0:T(8,128)(2,1)S(1)}, u32[]{:S(2)}, u32[]{:S(2)}) collective-permute-start(bf16[33,16,128]{2,1,0:T(8,128)(2,1)S(1)} %get-tuple-element.52), channel_id=1, source_target_pairs={{0,20},{4,16},{8,28},{12,24},{16,4},{20,0},{24,12},{28,8},{1,21},{... | collective-permute-start | bytes 405512 | tf_op jit(solution)/shard_map/ppermute | solution.py:570
  7.0 0.3 collective-permute-start.2
  7.3 2.9 %pack.1 = (bf16[34,16,128]{2,1,0:T(8,128)(2,1)S(1)}, bf16[34,16,128]{2,1,0:T(8,128)(2,1)S(1)}, bf16[34,16,128]{2,1,0:T(8,128)(2,1)S(1)}, bf16[34,16,128]{2,1,0:T...) custom-call(s32[1,16]{1,0:T(1,128)} %bitcast.5, ...), custom_call_target="tpu_custom_call" | custom-call | tf_op jit(solution)/shard_map/pack/pallas_call | solution.py:571
  10.2 1.3 %collective-permute-start = (f32[40,256]{1,0:T(8,128)S(1)}, f32[40,256]{1,0:T(8,128)S(1)}, u32[]{:S(2)}, u32[]{:S(2)}) collective-permute-start(f32[40,256]{1,0:T(8,128)S(1)} %get-tuple-element.36), channel_id=1, source_target_pairs={{1,0},{2,1},{3,2},{5,4},{6,5},{7,6},{9,8},{10,9},{11,10},{13,12},{... | collective-permute-start | bytes 122888 | tf_op jit(solution)/shard_map/ppermute | solution.py:33
  11.5 3.0 %collective-permute-start.1 = (f32[40,256]{1,0:T(8,128)S(1)}, f32[40,256]{1,0:T(8,128)S(1)}, u32[]{:S(2)}, u32[]{:S(2)}) collective-permute-start(f32[40,256]{1,0:T(8,128)S(1)} %get-tuple-element.37), channel_id=1, source_target_pairs={{0,1},{1,2},{2,3},{4,5},{5,6},{6,7},{8,9},{9,10},{10,11},{12,13},{... | collective-permute-start | bytes 122888 | tf_op jit(solution)/shard_map/ppermute | solution.py:33
  14.6 0.0 collective-permute-done.refs_5_.right
  14.6 0.8 %collective-permute-done.1.refs_6_.left = f32[40,256]{1,0:T(8,128)S(1)} collective-permute-done((f32[40,256]{1,0:T(8,128)S(1)}, f32[40,256]{1,0:T(8,128)S(1)}, u32[]{:S(2)}, u32[]{:S(2)}) %collective-permute-start.1) | collective-permute-done | bytes 40992 | tf_op jit(solution)/shard_map/ppermute | solution.py:33
  15.4 0.0 copy-start
  15.4 0.0 copy-start.1
  15.4 0.0 copy-start.2
  15.4 0.0 copy-start.3
  15.4 2.0 %widen.1 = (bf16[34,16,128]{2,1,0:T(8,128)(2,1)S(1)}, bf16[34,16,128]{2,1,0:T(8,128)(2,1)S(1)}, bf16[34,16,128]{2,1,0:T(8,128)(2,1)S(1)}, bf16[34,16,128]{2,1,0:...) custom-call(s32[2,2]{1,0:T(2,128)} %ice.1, ...), custom_call_target="tpu_custom_call", output_to_operand_aliasing={{0}: (7, {}), {1}: (8, {}), {2}: (9, {}), {3}: (10, {}), {4... | custom-call | tf_op jit(solution)/shard_map/widen/pallas_call | solution.py:585
  17.5 2.2 %collective-permute-start.11 = (f32[16,384]{1,0:T(8,128)S(1)}, f32[16,384]{1,0:T(8,128)S(1)}, u32[]{:S(2)}, u32[]{:S(2)}) collective-permute-start(f32[16,384]{1,0:T(8,128)S(1)} %get-tuple-element.59), channel_id=1, source_target_pairs={{0,4},{4,8},{8,12},{12,16},{16,20},{20,24},{24,28},{1,5},{5,9},{9,... | collective-permute-start | bytes 73736 | tf_op jit(solution)/shard_map/ppermute | solution.py:33
  19.7 1.3 %collective-permute-start.12 = (f32[16,384]{1,0:T(8,128)S(1)}, f32[16,384]{1,0:T(8,128)S(1)}, u32[]{:S(2)}, u32[]{:S(2)}) collective-permute-start(f32[16,384]{1,0:T(8,128)S(1)} %get-tuple-element.60), channel_id=1, source_target_pairs={{4,0},{8,4},{12,8},{16,12},{20,16},{24,20},{28,24},{5,1},{9,5},{13... | collective-permute-start | bytes 73736 | tf_op jit(solution)/shard_map/ppermute | solution.py:33
  21.0 0.0 collective-permute-done.6.refs_5_
  21.0 5.5 %collective-permute-start.10 = (bf16[1,16,128]{2,1,0:T(8,128)(2,1)S(1)}, bf16[1,16,128]{2,1,0:T(8,128)(2,1)S(1)}, u32[]{:S(2)}, u32[]{:S(2)}) collective-permute-start(bf16[1,16,128]{2,1,0:T(8,128)(2,1)S(1)} %get-tuple-element.58), channel_id=1, source_target_pairs={{0,20},{4,16},{8,28},{12,24},{16,4},{20,0},{24,12},{28,8},{1,21},{... | collective-permute-start | bytes 12296 | tf_op jit(solution)/shard_map/ppermute | solution.py:610
  26.5 0.5 %collective-permute-start.9 = (bf16[1,16,128]{2,1,0:T(8,128)(2,1)S(1)}, bf16[1,16,128]{2,1,0:T(8,128)(2,1)S(1)}, u32[]{:S(2)}, u32[]{:S(2)}) collective-permute-start(bf16[1,16,128]{2,1,0:T(8,128)(2,1)S(1)} %get-tuple-element.56), channel_id=1, source_target_pairs={{0,16},{4,20},{8,24},{12,28},{16,0},{20,4},{24,8},{28,12},{1,17},{... | collective-permute-start | bytes 12296 | tf_op jit(solution)/shard_map/ppermute | solution.py:610
  27.0 0.0 collective-permute-done.2.refs_4_
  27.0 2.9 %collective-permute-start.7 = (bf16[34,16,128]{2,1,0:T(8,128)(2,1)S(1)}, bf16[34,16,128]{2,1,0:T(8,128)(2,1)S(1)}, u32[]{:S(2)}, u32[]{:S(2)}) collective-permute-start(bf16[34,16,128]{2,1,0:T(8,128)(2,1)S(1)} %get-tuple-element.53), channel_id=1, source_target_pairs={{0,24},{4,28},{8,16},{12,20},{16,8},{20,12},{24,0},{28,4},{1,25},{... | collective-permute-start | bytes 417800 | tf_op jit(solution)/shard_map/ppermute | solution.py:608
  29.9 0.0 copy-start.4
  29.9 0.0 collective-permute-done.11.low_pack
  29.9 1.9 %collective-permute-start.8 = (bf16[34,16,128]{2,1,0:T(8,128)(2,1)S(1)}, bf16[34,16,128]{2,1,0:T(8,128)(2,1)S(1)}, u32[]{:S(2)}, u32[]{:S(2)}) collective-permute-start(bf16[34,16,128]{2,1,0:T(8,128)(2,1)S(1)} %get-tuple-element.54), channel_id=1, source_target_pairs={{0,28},{4,24},{8,20},{12,16},{16,12},{20,8},{24,4},{28,0},{1,29},{... | collective-permute-start | bytes 417800 | tf_op jit(solution)/shard_map/ppermute | solution.py:608
  31.9 0.0 collective-permute-done.12.high_pack
  31.9 0.0 collective-permute-start.5
  31.9 0.0 collective-permute-done.10.refs_9_
  31.9 2.0 %collective-permute-start.4 = (bf16[34,16,128]{2,1,0:T(8,128)(2,1)S(1)}, bf16[34,16,128]{2,1,0:T(8,128)(2,1)S(1)}, u32[]{:S(2)}, u32[]{:S(2)}) collective-permute-start(bf16[34,16,128]{2,1,0:T(8,128)(2,1)S(1)} %get-tuple-element.49), channel_id=1, source_target_pairs={{0,8},{4,12},{8,0},{12,4},{16,24},{20,28},{24,16},{28,20},{1,9},{5... | collective-permute-start | bytes 417800 | tf_op jit(solution)/shard_map/ppermute | solution.py:608
  33.9 0.0 collective-permute-done.9.refs_8_
  33.9 1.5 %collective-permute-start.3 = (bf16[34,16,128]{2,1,0:T(8,128)(2,1)S(1)}, bf16[34,16,128]{2,1,0:T(8,128)(2,1)S(1)}, u32[]{:S(2)}, u32[]{:S(2)}) collective-permute-start(bf16[34,16,128]{2,1,0:T(8,128)(2,1)S(1)} %get-tuple-element.47), channel_id=1, source_target_pairs={{0,4},{4,0},{8,12},{12,8},{16,20},{20,16},{24,28},{28,24},{1,5},{5... | collective-permute-start | bytes 417800 | tf_op jit(solution)/shard_map/ppermute | solution.py:608
  35.4 0.0 copy-done
  35.4 0.0 copy-done.1
  35.4 0.0 copy-done.2
  35.4 0.0 copy-done.3
  35.4 0.0 copy-done.4
  35.4 3.8 %sweep.1 = (f32[2,288,384]{2,1,0:T(8,128)S(1)}, f32[2,288,384]{2,1,0:T(8,128)S(1)}, f32[2,256,256]{2,1,0:T(8,128)S(1)}, f32[2,256,256]{2,1,0:T(8,128)S(1)}, f32[...) custom-call(s32[2,2]{1,0:T(2,128)S(1)} %copy-done.4, bf16[2,256,256]{2,1,0:T(8,128)(2,1)S(1)} %copy-done, ...), custom_call_target="tpu_custom_call" | custom-call | tf_op jit(solution)/shard_map/sweep/pallas_call | solution.py:613
  39.2 0.0 collective-permute-done.7.refs_6_
  39.2 0.2 collective-permute-done.8.refs_7_
  39.4 2.7 %collective-permute-done.5.refs_3_ = bf16[34,16,128]{2,1,0:T(8,128)(2,1)S(1)} collective-permute-done((bf16[34,16,128]{2,1,0:T(8,128)(2,1)S(1)}, bf16[34,16,128]{2,1,0:T(8,128)(2,1)S(1)}, u32[]{:S(2)}, u32[]{:S(2)}) %collective-permute-start.5) | collective-permute-done | bytes 139296 | tf_op jit(solution)/shard_map/ppermute | solution.py:608
  42.1 1.9 %collective-permute-done.4.refs_2_ = bf16[34,16,128]{2,1,0:T(8,128)(2,1)S(1)} collective-permute-done((bf16[34,16,128]{2,1,0:T(8,128)(2,1)S(1)}, bf16[34,16,128]{2,1,0:T(8,128)(2,1)S(1)}, u32[]{:S(2)}, u32[]{:S(2)}) %collective-permute-start.4) | collective-permute-done | bytes 139296 | tf_op jit(solution)/shard_map/ppermute | solution.py:608
  44.0 0.7 %collective-permute-done.3.refs_1_ = bf16[34,16,128]{2,1,0:T(8,128)(2,1)S(1)} collective-permute-done((bf16[34,16,128]{2,1,0:T(8,128)(2,1)S(1)}, bf16[34,16,128]{2,1,0:T(8,128)(2,1)S(1)}, u32[]{:S(2)}, u32[]{:S(2)}) %collective-permute-start.3) | collective-permute-done | bytes 139296 | tf_op jit(solution)/shard_map/ppermute | solution.py:608
  44.7 3.2 %final.1 = f32[256,256]{1,0:T(8,128)} custom-call(bf16[34,16,128]{2,1,0:T(8,128)(2,1)S(1)} %get-tuple-element.44.refs_0_, bf16[34,16,128]{2,1,0:T(8,128)(2,1)S(1)} %collective-permute-done.3.refs_1_, bf16[34,16,128]{2,1,0:T(8,128)(2,1)S(1)} %collective-permute-done.4.refs_2_, bf16[34,16,128]{2,1,0:T(8,128)(2,1)S(1)} %collective-permute-done.5.refs_3_, ...), custom_call_target="tpu_custom_call" | custom-call | tf_op jit(solution)/shard_map/final/pallas_call | solution.py:623
Async XLA Ops:
  1.9 19.1 %collective-permute-start.6 = (bf16[33,16,128]{2,1,0:T(8,128)(2,1)S(1)}, bf16[33,16,128]{2,1,0:T(8,128)(2,1)S(1)}, u32[]{:S(2)}, u32[]{:S(2)}) collective-permute-start(bf16[33,16,128]{2,1,0:T(8,128)(2,1)S(1)} %get-tuple-element.52), channel_id=1, source_target_pairs={{0,20},{4,16},{8,28},{12,24},{16,4},{20,0},{24,12},{28,8},{1,21},{... | collective-permute-start | bytes 405512 | tf_op jit(solution)/shard_map/ppermute | solution.py:570
  7.0 20.0 %collective-permute-start.2 = (bf16[33,16,128]{2,1,0:T(8,128)(2,1)S(1)}, bf16[33,16,128]{2,1,0:T(8,128)(2,1)S(1)}, u32[]{:S(2)}, u32[]{:S(2)}) collective-permute-start(bf16[33,16,128]{2,1,0:T(8,128)(2,1)S(1)} %get-tuple-element.46), channel_id=1, source_target_pairs={{0,16},{4,20},{8,24},{12,28},{16,0},{20,4},{24,8},{28,12},{1,17},{... | collective-permute-start | bytes 405512 | tf_op jit(solution)/shard_map/ppermute | solution.py:570
  10.2 4.3 %collective-permute-start = (f32[40,256]{1,0:T(8,128)S(1)}, f32[40,256]{1,0:T(8,128)S(1)}, u32[]{:S(2)}, u32[]{:S(2)}) collective-permute-start(f32[40,256]{1,0:T(8,128)S(1)} %get-tuple-element.36), channel_id=1, source_target_pairs={{1,0},{2,1},{3,2},{5,4},{6,5},{7,6},{9,8},{10,9},{11,10},{13,12},{... | collective-permute-start | bytes 122888 | tf_op jit(solution)/shard_map/ppermute | solution.py:33
  11.5 3.9 %collective-permute-start.1 = (f32[40,256]{1,0:T(8,128)S(1)}, f32[40,256]{1,0:T(8,128)S(1)}, u32[]{:S(2)}, u32[]{:S(2)}) collective-permute-start(f32[40,256]{1,0:T(8,128)S(1)} %get-tuple-element.37), channel_id=1, source_target_pairs={{0,1},{1,2},{2,3},{4,5},{5,6},{6,7},{8,9},{9,10},{10,11},{12,13},{... | collective-permute-start | bytes 122888 | tf_op jit(solution)/shard_map/ppermute | solution.py:33
  15.4 19.9 %copy-start = (bf16[2,256,256]{2,1,0:T(8,128)(2,1)S(1)}, bf16[2,256,256]{2,1,0:T(8,128)(2,1)}, u32[]{:S(2)}) copy-start(bf16[2,256,256]{2,1,0:T(8,128)(2,1)} %vel.1) | copy-start | bytes 786436
  15.4 19.9 %copy-start.1 = (f32[256,256]{1,0:T(8,128)S(1)}, f32[256,256]{1,0:T(8,128)}, u32[]{:S(2)}) copy-start(f32[256,256]{1,0:T(8,128)} %visc.1) | copy-start | bytes 786436
  15.4 19.9 %copy-start.2 = (f32[256,256]{1,0:T(8,128)S(1)}, f32[256,256]{1,0:T(8,128)}, u32[]{:S(2)}) copy-start(f32[256,256]{1,0:T(8,128)} %fric.1) | copy-start | bytes 786436
  15.4 19.9 %copy-start.3 = (bf16[2,256,256]{2,1,0:T(8,128)(2,1)S(1)}, bf16[2,256,256]{2,1,0:T(8,128)(2,1)}, u32[]{:S(2)}) copy-start(bf16[2,256,256]{2,1,0:T(8,128)(2,1)} %drive.1) | copy-start | bytes 786436
  17.5 12.4 %collective-permute-start.11 = (f32[16,384]{1,0:T(8,128)S(1)}, f32[16,384]{1,0:T(8,128)S(1)}, u32[]{:S(2)}, u32[]{:S(2)}) collective-permute-start(f32[16,384]{1,0:T(8,128)S(1)} %get-tuple-element.59), channel_id=1, source_target_pairs={{0,4},{4,8},{8,12},{12,16},{16,20},{20,24},{24,28},{1,5},{5,9},{9,... | collective-permute-start | bytes 73736 | tf_op jit(solution)/shard_map/ppermute | solution.py:33
  19.7 12.1 %collective-permute-start.12 = (f32[16,384]{1,0:T(8,128)S(1)}, f32[16,384]{1,0:T(8,128)S(1)}, u32[]{:S(2)}, u32[]{:S(2)}) collective-permute-start(f32[16,384]{1,0:T(8,128)S(1)} %get-tuple-element.60), channel_id=1, source_target_pairs={{4,0},{8,4},{12,8},{16,12},{20,16},{24,20},{28,24},{5,1},{9,5},{13... | collective-permute-start | bytes 73736 | tf_op jit(solution)/shard_map/ppermute | solution.py:33
  21.0 10.8 %collective-permute-start.10 = (bf16[1,16,128]{2,1,0:T(8,128)(2,1)S(1)}, bf16[1,16,128]{2,1,0:T(8,128)(2,1)S(1)}, u32[]{:S(2)}, u32[]{:S(2)}) collective-permute-start(bf16[1,16,128]{2,1,0:T(8,128)(2,1)S(1)} %get-tuple-element.58), channel_id=1, source_target_pairs={{0,20},{4,16},{8,28},{12,24},{16,4},{20,0},{24,12},{28,8},{1,21},{... | collective-permute-start | bytes 12296 | tf_op jit(solution)/shard_map/ppermute | solution.py:610
  26.5 7.4 %collective-permute-start.9 = (bf16[1,16,128]{2,1,0:T(8,128)(2,1)S(1)}, bf16[1,16,128]{2,1,0:T(8,128)(2,1)S(1)}, u32[]{:S(2)}, u32[]{:S(2)}) collective-permute-start(bf16[1,16,128]{2,1,0:T(8,128)(2,1)S(1)} %get-tuple-element.56), channel_id=1, source_target_pairs={{0,16},{4,20},{8,24},{12,28},{16,0},{20,4},{24,8},{28,12},{1,17},{... | collective-permute-start | bytes 12296 | tf_op jit(solution)/shard_map/ppermute | solution.py:610
  27.0 12.2 %collective-permute-start.7 = (bf16[34,16,128]{2,1,0:T(8,128)(2,1)S(1)}, bf16[34,16,128]{2,1,0:T(8,128)(2,1)S(1)}, u32[]{:S(2)}, u32[]{:S(2)}) collective-permute-start(bf16[34,16,128]{2,1,0:T(8,128)(2,1)S(1)} %get-tuple-element.53), channel_id=1, source_target_pairs={{0,24},{4,28},{8,16},{12,20},{16,8},{20,12},{24,0},{28,4},{1,25},{... | collective-permute-start | bytes 417800 | tf_op jit(solution)/shard_map/ppermute | solution.py:608
  29.9 5.4 %copy-start.4 = (s32[2,2]{1,0:T(2,128)S(1)}, s32[2,2]{1,0:T(2,128)}, u32[]{:S(2)}) copy-start(s32[2,2]{1,0:T(2,128)} %ice.1) | copy-start | bytes 52
  29.9 9.5 %collective-permute-start.8 = (bf16[34,16,128]{2,1,0:T(8,128)(2,1)S(1)}, bf16[34,16,128]{2,1,0:T(8,128)(2,1)S(1)}, u32[]{:S(2)}, u32[]{:S(2)}) collective-permute-start(bf16[34,16,128]{2,1,0:T(8,128)(2,1)S(1)} %get-tuple-element.54), channel_id=1, source_target_pairs={{0,28},{4,24},{8,20},{12,16},{16,12},{20,8},{24,4},{28,0},{1,29},{... | collective-permute-start | bytes 417800 | tf_op jit(solution)/shard_map/ppermute | solution.py:608
  31.9 10.2 %collective-permute-start.5 = (bf16[34,16,128]{2,1,0:T(8,128)(2,1)S(1)}, bf16[34,16,128]{2,1,0:T(8,128)(2,1)S(1)}, u32[]{:S(2)}, u32[]{:S(2)}) collective-permute-start(bf16[34,16,128]{2,1,0:T(8,128)(2,1)S(1)} %get-tuple-element.51), channel_id=1, source_target_pairs={{0,12},{4,8},{8,4},{12,0},{16,28},{20,24},{24,20},{28,16},{1,13},{... | collective-permute-start | bytes 417800 | tf_op jit(solution)/shard_map/ppermute | solution.py:608
  31.9 12.1 %collective-permute-start.4 = (bf16[34,16,128]{2,1,0:T(8,128)(2,1)S(1)}, bf16[34,16,128]{2,1,0:T(8,128)(2,1)S(1)}, u32[]{:S(2)}, u32[]{:S(2)}) collective-permute-start(bf16[34,16,128]{2,1,0:T(8,128)(2,1)S(1)} %get-tuple-element.49), channel_id=1, source_target_pairs={{0,8},{4,12},{8,0},{12,4},{16,24},{20,28},{24,16},{28,20},{1,9},{5... | collective-permute-start | bytes 417800 | tf_op jit(solution)/shard_map/ppermute | solution.py:608
  33.9 10.8 %collective-permute-start.3 = (bf16[34,16,128]{2,1,0:T(8,128)(2,1)S(1)}, bf16[34,16,128]{2,1,0:T(8,128)(2,1)S(1)}, u32[]{:S(2)}, u32[]{:S(2)}) collective-permute-start(bf16[34,16,128]{2,1,0:T(8,128)(2,1)S(1)} %get-tuple-element.47), channel_id=1, source_target_pairs={{0,4},{4,0},{8,12},{12,8},{16,20},{20,16},{24,28},{28,24},{1,5},{5... | collective-permute-start | bytes 417800 | tf_op jit(solution)/shard_map/ppermute | solution.py:608

commit v3 on v2

--- a/solution.py
+++ b/solution.py
@@ -22,9 +22,7 @@
 
 
 def partner(me, step, count):
-    if count & (count - 1) == 0:
-        return me ^ step
-    return (me + step) % count
+    return lax.rem(me + step, count) if isinstance(me, jax.Array) else (me + step) % count
 
 
 def from_behind(value, axis, steps):
@@ -128,11 +126,11 @@
     return copies
 
 
-def send_kernel(groups, count, tile, steps, *refs):
+def gather_kernel(groups, count, tile, *refs):
     owner, slot, weight, obs = refs[:4]
-    pays = refs[4 : 4 + len(steps)]
+    pays = refs[4 : 4 + groups]
     owner_s, slot_s, weight_b, weight_v, weight_s, edges, place, filled, scalar_sem, edge_sem, scene_sem = refs[
-        4 + len(steps) :
+        4 + groups :
     ]
     blocks = tile // PACK
     me = lax.axis_index("gx")
@@ -142,32 +140,21 @@
     scalars = load_scalars(owner, slot, weight, owner_s, slot_s, weight_b, weight_v, weight_s, scalar_sem)
     scalars[0].wait()
     fill_places(place, filled, groups, count, lambda scene: owner_s[0, scene])
-    copies = gather_scenes(obs, pays, steps, place, groups, blocks, me, scene_sem)
+    copies = gather_scenes(obs, pays, range(groups), place, groups, blocks, me, scene_sem)
     wait_all(scalars[1:] + loads)
-    for number, step in enumerate(steps):
+    for step in range(groups):
         to = partner(me, step, groups)
-        pays[number][CAP * 2 * blocks] = easting_block(
+        pays[step][CAP * 2 * blocks] = easting_block(
             to, place, slot_s, weight_s, lambda scene, part, side: edges[side * 2 + part, scene]
         )
     wait_all(copies)
 
 
-def pack_kernel(groups, count, tile, steps, *refs):
-    owner, slot, weight, ice, obs_h, vel_h, visc_h, fric_h, drive_h = refs[:9]
-    pays = refs[9 : 9 + len(steps)]
-    to_low, to_high = refs[9 + len(steps) : 11 + len(steps)]
-    (
-        owner_s, slot_s, weight_b, weight_v, weight_s, ice_s, owner_v, slot_v, obs, vel, visc, fric, drive,
-        place, filled, scalar_sem, more_sem, load_sem, scene_sem,
-    ) = refs[11 + len(steps) :]
-    blocks = tile // PACK
-    me = lax.axis_index("gx")
+def pack_kernel(count, tile, *refs):
+    owner, slot, weight, ice, obs_h, vel_h, visc_h, fric_h, drive_h, to_low, to_high = refs[:11]
+    ice_s, owner_v, slot_v, weight_v, obs, vel, visc, fric, drive, more_sem, load_sem = refs[11:]
     loads = copy_all([(vel_h, vel), (drive_h, drive), (visc_h, visc), (fric_h, fric), (obs_h, obs)], load_sem)
-    more = copy_all([(ice, ice_s), (owner, owner_v), (slot, slot_v)], more_sem)
-    scalars = load_scalars(owner, slot, weight, owner_s, slot_s, weight_b, weight_v, weight_s, scalar_sem)
-    scalars[0].wait()
-    fill_places(place, filled, groups, count, lambda scene: owner_s[0, scene])
-    copies = gather_scenes(obs_h, pays, steps, place, groups, blocks, me, scene_sem)
+    more = copy_all([(ice, ice_s), (owner, owner_v), (slot, slot_v), (weight, weight_v)], more_sem)
     picked = lax.broadcasted_iota(jnp.int32, (8, LANE), 0)
     across = lax.broadcasted_iota(jnp.int32, (8, LANE), 1)
     cells_y = visc.shape[1]
@@ -186,13 +173,7 @@
                 field = vel[index, :, lanes] if index in (U, V) else drive[index - DRIVE_U, :, lanes]
                 rows = columns_of(pick(first, jnp.bfloat16), field, None)
             target[at : at + depth, :] = rows[0:depth]
-    loads[4].wait()
-    both = (across == jnp.where(picked == 0, 0, LANE - 1)).astype(jnp.bfloat16)
-    for scene in range(count):
-        rows = columns_of(both, obs[scene].reshape(2 * tile, LANE), None)
-        to_low[SCENES + scene : SCENES + scene + 1, :] = rows[0:1]
-        to_high[SCENES + scene : SCENES + scene + 1, :] = rows[1:2]
-    wait_all(scalars[1:] + more)
+    wait_all(more)
     for target, at in ((to_low, 0), (to_high, ice_s.shape[1] - 1)):
         target[SCENES + count :, :] = jnp.zeros((8, target.shape[1]), F32)
         for number, values in enumerate((owner_v, slot_v, weight_v)):
@@ -201,13 +182,12 @@
         target[row : row + 1, :] = ice_line(
             [ice_s[number, at] for number in range(ice_s.shape[0])], (1, target.shape[1]), tile
         )
-    for number, step in enumerate(steps):
-        to = partner(me, step, groups)
-        pays[number][CAP * 2 * blocks] = easting_block(
-            to, place, slot_s, weight_s,
-            lambda scene, part, side: obs[scene, part * blocks + (0 if side == 0 else blocks - 1)],
-        )
-    wait_all(copies)
+    loads[4].wait()
+    both = (across == jnp.where(picked == 0, 0, LANE - 1)).astype(jnp.bfloat16)
+    for scene in range(count):
+        rows = columns_of(both, obs[scene].reshape(2 * tile, LANE), None)
+        to_low[SCENES + scene : SCENES + scene + 1, :] = rows[0:1]
+        to_high[SCENES + scene : SCENES + scene + 1, :] = rows[1:2]
 
 
 def side_tiles(right, left, turned):
@@ -225,14 +205,36 @@
     return jnp.where(lane < depth, after, jnp.where(lane >= LANE - depth, before, 0.0))
 
 
-def widen_kernel(groups, count, tile, early, late, *refs):
+def write_halo(pay, base, pack):
+    first = FIELDS[VISC][0]
+    last = FIELDS[FRIC][0] + FIELDS[FRIC][1]
+    for number in range(pack.shape[1] // LANE):
+        whole = pack[:, number * LANE : (number + 1) * LANE]
+        high = whole.astype(jnp.bfloat16)
+        rest = whole - high.astype(F32)
+        middle = rest.astype(jnp.bfloat16).astype(F32)
+        pay[base + 2 * number] = high
+        both = jnp.concatenate([middle[first:last], (rest - middle)[first:last]], axis=0)
+        fill = jnp.zeros((PACK - both.shape[0], LANE), F32)
+        pay[base + 2 * number + 1] = jnp.concatenate([both, fill], axis=0).astype(jnp.bfloat16)
+
+
+def read_halo(pay, base, pack, keep):
+    first = FIELDS[VISC][0]
+    count = FIELDS[FRIC][0] + FIELDS[FRIC][1] - first
+    for number in range(pack.shape[1] // LANE):
+        lanes = slice(number * LANE, (number + 1) * LANE)
+        more = pay[base + 2 * number + 1].astype(F32)
+        pack[:, lanes] = pay[base + 2 * number].astype(F32)
+        pack[first : first + count, lanes] += more[0:count]
+        pack[first : first + count, lanes] += more[count : 2 * count]
+    pack[...] = jnp.where(keep, pack[...], 0.0)
+
+
+def widen_kernel(groups, count, tile, *refs):
     ice, vel, visc, fric, drive, right, left = refs[:7]
-    pays = refs[7 + len(late) : 7 + 2 * len(late)]
-    apart = refs[7 + 2 * len(late) : 7 + 2 * len(late) + len(early)]
-    to_low, to_high = refs[7 + 2 * len(late) + len(early) : 9 + 2 * len(late) + len(early)]
-    ice_s, notes, first_b, last_b, first_f, last_f, turned, place, filled, sems = refs[
-        9 + 2 * len(late) + len(early) :
-    ]
+    pays = refs[7 + groups : 7 + 2 * groups]
+    ice_s, notes, first_b, last_b, first_f, last_f, turned, to_low, to_high, place, filled, sems = refs[7 + 2 * groups :]
     cells = visc.shape[0]
     cells_y = visc.shape[1]
     blocks = tile // PACK
@@ -265,12 +267,15 @@
         to_high[at : at + depth, 0:cells_y] = last[last.shape[0] - depth :]
         to_low[at : at + depth, cells_y:] = side_tile(upright[0:8], index)[0:depth]
         to_high[at : at + depth, cells_y:] = side_tile(upright[cells - 8 :], index)[8 - depth : 8]
+    base = CAP * 2 * blocks + 2
+    write_halo(pays[1], base, to_high[...])
+    write_halo(pays[groups - 1], base, to_low[...])
     packs = (right, left)
     for side in range(2):
         fill_places(place.at[side], filled, groups, count, lambda scene: notes[side, 0, scene].astype(jnp.int32))
     row = lax.broadcasted_iota(jnp.int32, (PACK, LANE), 0)
     lane = lax.broadcasted_iota(jnp.int32, (PACK, LANE), 1)
-    for number, step in enumerate(late + early):
+    for step in range(groups):
         to = partner(me, step, groups)
         block = jnp.zeros((PACK, LANE), F32)
         for side in range(2):
@@ -298,10 +303,7 @@
                     block = jnp.where((row == 8) & (lane == base + part), value, block)
                 value = jnp.where(where == (2 if side == 0 else 1), amount, 0.0)
                 block = jnp.where((row == 8) & (lane == base + 2), value, block)
-        if number < len(late):
-            pays[number][CAP * 2 * blocks + 1] = block.astype(jnp.bfloat16)
-        else:
-            apart[number - len(late)][0] = block.astype(jnp.bfloat16)
+        pays[step][CAP * 2 * blocks + 1] = block.astype(jnp.bfloat16)
 
 
 def stress_block(u, v, visc, low, rows, wide):
@@ -324,16 +326,20 @@
     return push_u, push_v
 
 
-def sweep_kernel(tile, ice, vel, visc, fric, drive, right, left, low_pack, high_pack, *refs):
+def sweep_kernel(groups, tile, ice, vel, visc, fric, drive, right, left, from_low, from_high, *refs):
     second, ease, lead, trail, wide_visc, wide_ice = refs[:6]
     (
         u, v, wide_fric, drive_u, drive_v, next_u, next_v, relax_u, relax_v, sxx, syy, sxy, turned,
-        ice_s, sems,
+        low_pack, high_pack, ice_s, sems,
     ) = refs[6:]
     cells, cells_y = visc.shape
     rows, wide = wide_visc.shape
     loads = copy_all([(ice, ice_s)], sems)
     upright = side_tiles(right, left, turned)
+    base = CAP * 2 * (tile // PACK) + 2
+    me = lax.axis_index("gx")
+    read_halo(from_low, base, low_pack, me > 0)
+    read_halo(from_high, base, high_pack, me < groups - 1)
     wait_all(loads)
     own_rows = slice(PAD, PAD + cells)
     for index, field in enumerate((u, v, wide_visc, wide_fric, drive_u, drive_v, wide_ice)):
@@ -400,12 +406,10 @@
                 )
 
 
-def final_kernel(groups, tile, early, *refs):
+def final_kernel(groups, tile, *refs):
     pays = refs[:groups]
-    apart = dict(zip(early, refs[groups : groups + len(early)]))
-    second, ease, lead, trail, visc, ice = refs[groups + len(early) : groups + len(early) + 6]
-    grad = refs[groups + len(early) + 6]
-    misfit, u, v, sxx, syy, sxy, table, total, rows_x, rows_y, turned = refs[groups + len(early) + 7 :]
+    second, ease, lead, trail, visc, ice, grad = refs[groups : groups + 7]
+    misfit, u, v, sxx, syy, sxy, table, total, rows_x, rows_y, turned = refs[groups + 7 :]
     rows, wide = visc.shape
     cells_y = wide - LANE
     cells = rows - 2 * PAD
@@ -415,8 +419,7 @@
     lift = (u, v)
     for group in range(groups):
         rows_x[pl.ds(group, PACK, stride=groups), :] = pays[group][CAP * 2 * blocks].astype(F32)
-        side = apart[group][0] if group in apart else pays[group][CAP * 2 * blocks + 1]
-        rows_y[pl.ds(group, PACK, stride=groups), :] = side.astype(F32)
+        rows_y[pl.ds(group, PACK, stride=groups), :] = pays[group][CAP * 2 * blocks + 1].astype(F32)
 
     def raw(source, number):
         return source[number * groups : (number + 1) * groups, :]
@@ -536,9 +539,6 @@
     owner, slot, weight = scene_owner.reshape(1, count), scene_slot, scene_weight
     limit = pltpu.CompilerParams(vmem_limit_bytes=40 << 20)
     dma = pltpu.SemaphoreType.DMA
-    early = (groups // 2, groups // 2 + 1)
-    late = tuple(step for step in range(groups) if step not in early)
-
     def shape(*dims, dtype=F32):
         return jax.ShapeDtypeStruct(dims, dtype)
 
@@ -551,79 +551,71 @@
     bf16, i32 = jnp.bfloat16, jnp.int32
     deep = CAP * 2 * blocks
     tall = SCENES + count + 8
-    pairs = {step: [(me, partner(me, step, groups)) for me in range(groups)] for step in range(1, groups)}
-    scalars = [
-        pltpu.SMEM((1, count), i32), pltpu.SMEM((1, count), i32), short(1, count), full(1, count),
-        pltpu.SMEM((1, count), F32),
+    halo = 2 * (wide // LANE)
+    pay_shapes = [
+        pltpu.VMEM((deep + 2 + (halo if step in (1, groups - 1) else 0), PACK, LANE), bf16) for step in range(groups)
     ]
     places = [pltpu.SMEM(((groups + 2) * CAP,), i32), pltpu.SMEM((groups,), i32)]
-    sent = pl.pallas_call(
-        functools.partial(send_kernel, groups, count, tile, early),
-        out_shape=[pltpu.VMEM((deep + 1, PACK, LANE), bf16)] * len(early),
-        in_specs=[HBM] * 4,
-        out_specs=[VMEM] * len(early),
-        scratch_shapes=scalars + [short(4, count, PACK, LANE)] + places
-        + [dma((3,)), dma((4,)), dma((len(early) * CAP,))],
-        compiler_params=limit,
-        name="send",
-    )(*in_place(owner, slot, weight, obs))
-    got = {step: lax.ppermute(value, "gx", pairs[step]) for step, value in zip(early, sent)}
-    *pays, y_low, y_high = pl.pallas_call(
-        functools.partial(pack_kernel, groups, count, tile, late),
-        out_shape=[pltpu.VMEM((deep + 2, PACK, LANE), bf16)] * len(late) + [pltpu.VMEM((tall, cells_x), F32)] * 2,
+    y_low, y_high = pl.pallas_call(
+        functools.partial(pack_kernel, count, tile),
+        out_shape=[pltpu.VMEM((tall, cells_x), F32)] * 2,
         in_specs=[HBM] * 9,
-        out_specs=[VMEM] * (len(late) + 2),
-        scratch_shapes=scalars
-        + [pltpu.SMEM(ice_mask.shape, i32), pltpu.VMEM((1, count), i32), pltpu.VMEM((1, count), i32)]
-        + [short(*obs.shape), short(*vel0.shape), full(*visc.shape), full(*fric.shape), short(*drive.shape)] + places
-        + [dma((3,)), dma((3,)), dma((5,)), dma((len(late) * CAP,))],
+        out_specs=[VMEM] * 2,
+        scratch_shapes=[
+            pltpu.SMEM(ice_mask.shape, i32), pltpu.VMEM((1, count), i32), pltpu.VMEM((1, count), i32), short(1, count),
+            short(*obs.shape), short(*vel0.shape), full(*visc.shape), full(*fric.shape), short(*drive.shape),
+            dma((4,)), dma((5,)),
+        ],
         compiler_params=limit,
         name="pack",
     )(*in_place(owner, slot, weight, ice_mask, obs, vel0, visc, fric, drive))
     right = from_behind(y_low, "gy", -1)
     left = from_behind(y_high, "gy", 1)
-    outs = pl.pallas_call(
-        functools.partial(widen_kernel, groups, count, tile, early, late),
-        out_shape=[pltpu.VMEM((deep + 2, PACK, LANE), bf16)] * len(late)
-        + [pltpu.VMEM((1, PACK, LANE), bf16)] * len(early)
-        + [pltpu.VMEM((PACK, wide), F32)] * 2,
-        in_specs=[HBM] * 5 + [VMEM] * (2 + len(late)),
-        out_specs=[VMEM] * (len(late) + len(early) + 2),
-        input_output_aliases={7 + number: number for number in range(len(late))},
+    pays = pl.pallas_call(
+        functools.partial(gather_kernel, groups, count, tile),
+        out_shape=pay_shapes,
+        in_specs=[HBM] * 4,
+        out_specs=[VMEM] * groups,
+        scratch_shapes=[
+            pltpu.SMEM((1, count), i32), pltpu.SMEM((1, count), i32), short(1, count), full(1, count),
+            pltpu.SMEM((1, count), F32), short(4, count, PACK, LANE), *places, dma((3,)), dma((4,)),
+            dma((groups * CAP,)),
+        ],
+        compiler_params=limit,
+        name="gather",
+    )(*in_place(after(owner, y_low), slot, weight, obs))
+    ready = pl.pallas_call(
+        functools.partial(widen_kernel, groups, count, tile),
+        out_shape=pay_shapes,
+        in_specs=[HBM] * 5 + [VMEM] * (2 + groups),
+        out_specs=[VMEM] * groups,
+        input_output_aliases={7 + step: step for step in range(groups)},
         scratch_shapes=[
             pltpu.SMEM(ice_mask.shape, i32), pltpu.SMEM((2, 8, cells_x), F32), short(4, 16, cells_y),
-            short(4, 16, cells_y), full(2, 8, cells_y), full(2, 8, cells_y), full(LANE, cells_x),
-            pltpu.SMEM((2, (groups + 2) * CAP), i32), pltpu.SMEM((groups,), i32), dma((11,)),
+            short(4, 16, cells_y), full(2, 8, cells_y), full(2, 8, cells_y), full(LANE, cells_x), full(PACK, wide),
+            full(PACK, wide), pltpu.SMEM((2, (groups + 2) * CAP), i32), pltpu.SMEM((groups,), i32), dma((11,)),
         ],
         compiler_params=limit,
         name="widen",
     )(*in_place(ice_mask, vel0, visc, fric, drive), right, left, *pays)
-    ready = dict(zip(late, outs))
-    x_low, x_high = outs[-2:]
-    high_pack = from_behind(x_low, "gx", -1)
-    low_pack = from_behind(x_high, "gx", 1)
-    got[0] = ready[0]
-    for step in late[1:]:
-        value = ready[step] if step > groups // 2 else after(ready[step], got[early[0]])
-        got[step] = lax.ppermute(value, "gx", pairs[step])
-    apart = [
-        lax.ppermute(after(value, got[early[1]]), "gx", pairs[step])
-        for step, value in zip(early, outs[len(late) :])
-    ]
+    got = [ready[0]]
+    for step in range(1, groups):
+        pairs = [(me, partner(me, step, groups)) for me in range(groups)]
+        got.append(lax.ppermute(ready[step], "gx", pairs))
     base = pl.pallas_call(
-        functools.partial(sweep_kernel, tile),
+        functools.partial(sweep_kernel, groups, tile),
         out_shape=[shape(2, rows, wide)] * 2 + [shape(2, cells_x, cells_y)] * 2 + [shape(rows, wide)] * 2,
         in_specs=[HBM] + [VMEM] * 8,
         out_specs=[VMEM] * 6,
         scratch_shapes=[full(rows, wide)] * 12
-        + [full(LANE, cells_x), pltpu.SMEM(ice_mask.shape, i32), dma((1,))],
+        + [full(LANE, cells_x), full(PACK, wide), full(PACK, wide), pltpu.SMEM(ice_mask.shape, i32), dma((1,))],
         compiler_params=limit,
         name="sweep",
-    )(ice_mask, vel0, visc, fric, drive, right, left, low_pack, high_pack)
+    )(ice_mask, vel0, visc, fric, drive, right, left, got[1], got[groups - 1])
     return pl.pallas_call(
-        functools.partial(final_kernel, groups, tile, early),
+        functools.partial(final_kernel, groups, tile),
         out_shape=shape(cells_x, cells_y),
-        in_specs=[VMEM] * (groups + len(early) + 6),
+        in_specs=[VMEM] * (groups + 6),
         out_specs=VMEM,
         scratch_shapes=[full(2, cells_x, cells_y)] + [full(rows, wide)] * 5
         + [
@@ -632,7 +624,7 @@
         ],
         compiler_params=limit,
         name="final",
-    )(*(got[step] for step in range(groups)), *apart, *base)
+    )(*got, *base)
 
 
 def solution(mesh):

time: 48.2 us -> 45 us (0.934)
  the two profiles are of different devices: /device:TPU:0 before, /device:TPU:27 now
where the time goes in v3:
time: 45 us; the launch traced here: 44.7 us
  waiting for transfers between devices  17.6 us (39%)
  Pallas kernels  13.8 us (31%)
  starting transfers between devices  13.1 us (29%)
    ppermute x7, waiting for transfers between devices, body(): got.append(lax.ppermute(ready[step], 'gx', pairs))  16.6 us
    ppermute x7, starting transfers between devices, body(): got.append(lax.ppermute(ready[step], 'gx', pairs))  7.51 us
    ppermute x2, starting transfers between devices, from_behind(): lax.ppermute(value, axis, [(source, source + steps) for source in range(f...  5.63 us
    pallas_call x1, Pallas kernels, body(): pl.pallas_call(functools.partial(sweep_kernel, groups, tile), out_shape=[...  3.83 us
    pallas_call x1, Pallas kernels, body(): pl.pallas_call(functools.partial(final_kernel, groups, tile), out_shape=s...  3.17 us
    pallas_call x1, Pallas kernels, body(): pl.pallas_call(functools.partial(pack_kernel, count, tile), out_shape=[pl...  2.36 us
    pallas_call x1, Pallas kernels, body(): pl.pallas_call(functools.partial(gather_kernel, groups, count, tile), out...  2.35 us
    pallas_call x1, Pallas kernels, body(): pl.pallas_call(functools.partial(widen_kernel, groups, count, tile), out_...  2.06 us
  transfers between devices with their start and end apart: 9, of which 4 were waited for; matrix products, arithmetic and copies ran while one was open for 0% of the time, Pallas kernels for 14%

profile of v3, /device:TPU:27, one launch (start us, length us, event | category | flops | bytes accessed | tf_op | source)
XLA Modules:
  0.0 44.7 jit_solution(16323421013375061321)
XLA Ops:
  0.0 2.4 %pack.1 = (f32[40,256]{1,0:T(8,128)S(1)}, f32[40,256]{1,0:T(8,128)S(1)}) custom-call(s32[1,16]{1,0:T(1,128)} %bitcast.4, s32[1,16]{1,0:T(1,128)} %refs_1_.4, bf16[1,16]{1,0:T(2,128)(2,1)} %refs_2_.4, s32[2,2]{1,0:T(2,128)} %ice.1, bf16[16,16,16,128]{3,2,1,0:T(8,128)(2,1)} %bitcast.2, bf16[2,256,256]{2,1,0:T(8,128)(2,1)} %vel.1, f32[256,256]{1,0:T(8,128)} %visc.1, ...), custom_call_target="tpu_custom_call" | custom-call | tf_op jit(solution)/shard_map/pack/pallas_call | solution.py:559
  2.4 3.7 %collective-permute-start.1 = (f32[40,256]{1,0:T(8,128)S(1)}, f32[40,256]{1,0:T(8,128)S(1)}, u32[]{:S(2)}, u32[]{:S(2)}) collective-permute-start(f32[40,256]{1,0:T(8,128)S(1)} %get-tuple-element.31), channel_id=1, source_target_pairs={{0,1},{1,2},{2,3},{4,5},{5,6},{6,7},{8,9},{9,10},{10,11},{12,13},{... | collective-permute-start | bytes 122888 | tf_op jit(solution)/shard_map/ppermute | solution.py:31
  6.1 1.9 %collective-permute-start = (f32[40,256]{1,0:T(8,128)S(1)}, f32[40,256]{1,0:T(8,128)S(1)}, u32[]{:S(2)}, u32[]{:S(2)}) collective-permute-start(f32[40,256]{1,0:T(8,128)S(1)} %get-tuple-element.30), channel_id=1, source_target_pairs={{1,0},{2,1},{3,2},{5,4},{6,5},{7,6},{9,8},{10,9},{11,10},{13,12},{... | collective-permute-start | bytes 122888 | tf_op jit(solution)/shard_map/ppermute | solution.py:31
  8.0 2.4 %gather.1 = (bf16[34,16,128]{2,1,0:T(8,128)(2,1)S(1)}, bf16[40,16,128]{2,1,0:T(8,128)(2,1)S(1)}, bf16[34,16,128]{2,1,0:T(8,128)(2,1)S(1)}, bf16[34,16,128]{2,1,0...) custom-call(s32[1,16]{1,0:T(1,128)} %bitcast.5, ...), custom_call_target="tpu_custom_call" | custom-call | tf_op jit(solution)/shard_map/gather/pallas_call | solution.py:574
  10.4 0.0 collective-permute-done.1.refs_6_.left
  10.4 1.0 %collective-permute-done.refs_5_.right = f32[40,256]{1,0:T(8,128)S(1)} collective-permute-done((f32[40,256]{1,0:T(8,128)S(1)}, f32[40,256]{1,0:T(8,128)S(1)}, u32[]{:S(2)}, u32[]{:S(2)}) %collective-permute-start) | collective-permute-done | bytes 40992 | tf_op jit(solution)/shard_map/ppermute | solution.py:31
  11.4 0.0 copy-start
  11.4 0.0 copy-start.1
  11.4 0.0 copy-start.2
  11.4 0.0 copy-start.3
  11.4 2.1 %widen.1 = (bf16[34,16,128]{2,1,0:T(8,128)(2,1)S(1)}, bf16[40,16,128]{2,1,0:T(8,128)(2,1)S(1)}, bf16[34,16,128]{2,1,0:T(8,128)(2,1)S(1)}, bf16[34,16,128]{2,1,0:...) custom-call(s32[2,2]{1,0:T(2,128)} %ice.1, ...), custom_call_target="tpu_custom_call", output_to_operand_aliasing={{0}: (7, {}), {1}: (8, {}), {2}: (9, {}), {3}: (10, {}), {4... | custom-call | tf_op jit(solution)/shard_map/widen/pallas_call | solution.py:587
  13.5 0.1 collective-permute-start.2
  13.6 1.5 %collective-permute-start.8 = (bf16[40,16,128]{2,1,0:T(8,128)(2,1)S(1)}, bf16[40,16,128]{2,1,0:T(8,128)(2,1)S(1)}, u32[]{:S(2)}, u32[]{:S(2)}) collective-permute-start(bf16[40,16,128]{2,1,0:T(8,128)(2,1)S(1)} %get-tuple-element.48), channel_id=1, source_target_pairs={{0,28},{4,0},{8,4},{12,8},{16,12},{20,16},{24,20},{28,24},{1,29},{... | collective-permute-start | bytes 491528 | tf_op jit(solution)/shard_map/ppermute | solution.py:604
  15.0 0.0 collective-permute-start.3
  15.0 2.2 %collective-permute-start.4 = (bf16[34,16,128]{2,1,0:T(8,128)(2,1)S(1)}, bf16[34,16,128]{2,1,0:T(8,128)(2,1)S(1)}, u32[]{:S(2)}, u32[]{:S(2)}) collective-permute-start(bf16[34,16,128]{2,1,0:T(8,128)(2,1)S(1)} %get-tuple-element.44), channel_id=1, source_target_pairs={{0,12},{4,16},{8,20},{12,24},{16,28},{20,0},{24,4},{28,8},{1,13},{... | collective-permute-start | bytes 417800 | tf_op jit(solution)/shard_map/ppermute | solution.py:604
  17.2 2.9 %collective-permute-start.5 = (bf16[34,16,128]{2,1,0:T(8,128)(2,1)S(1)}, bf16[34,16,128]{2,1,0:T(8,128)(2,1)S(1)}, u32[]{:S(2)}, u32[]{:S(2)}) collective-permute-start(bf16[34,16,128]{2,1,0:T(8,128)(2,1)S(1)} %get-tuple-element.45), channel_id=1, source_target_pairs={{0,16},{4,20},{8,24},{12,28},{16,0},{20,4},{24,8},{28,12},{1,17},{... | collective-permute-start | bytes 417800 | tf_op jit(solution)/shard_map/ppermute | solution.py:604
  20.1 0.0 collective-permute-done.2.from_low.refs_1_
  20.2 0.0 copy-start.4
  20.2 0.0 collective-permute-start.6
  20.2 2.1 %collective-permute-done.8.from_high.refs_7_ = bf16[40,16,128]{2,1,0:T(8,128)(2,1)S(1)} collective-permute-done((bf16[40,16,128]{2,1,0:T(8,128)(2,1)S(1)}, bf16[40,16,128]{2,1,0:T(8,128)(2,1)S(1)}, u32[]{:S(2)}, u32[]{:S(2)}) %collective-permute-start.8) | collective-permute-done | bytes 163872 | tf_op jit(solution)/shard_map/ppermute | solution.py:604
  22.3 0.8 %collective-permute-start.7 = (bf16[34,16,128]{2,1,0:T(8,128)(2,1)S(1)}, bf16[34,16,128]{2,1,0:T(8,128)(2,1)S(1)}, u32[]{:S(2)}, u32[]{:S(2)}) collective-permute-start(bf16[34,16,128]{2,1,0:T(8,128)(2,1)S(1)} %get-tuple-element.47), channel_id=1, source_target_pairs={{0,24},{4,28},{8,0},{12,4},{16,8},{20,12},{24,16},{28,20},{1,25},{... | collective-permute-start | bytes 417800 | tf_op jit(solution)/shard_map/ppermute | solution.py:604
  23.1 0.0 copy-done
  23.1 0.0 copy-done.1
  23.1 0.0 copy-done.2
  23.1 0.0 copy-done.3
  23.1 0.0 copy-done.4
  23.1 3.8 %sweep.1 = (f32[2,288,384]{2,1,0:T(8,128)S(1)}, f32[2,288,384]{2,1,0:T(8,128)S(1)}, f32[2,256,256]{2,1,0:T(8,128)S(1)}, f32[2,256,256]{2,1,0:T(8,128)S(1)}, f32[...) custom-call(s32[2,2]{1,0:T(2,128)S(1)} %copy-done.4, bf16[2,256,256]{2,1,0:T(8,128)(2,1)S(1)} %copy-done, ...), custom_call_target="tpu_custom_call" | custom-call | tf_op jit(solution)/shard_map/sweep/pallas_call | solution.py:605
  27.0 0.0 collective-permute-done.3.refs_2_
  27.0 0.0 collective-permute-done.4.refs_3_
  27.0 11.8 %collective-permute-done.5.refs_4_ = bf16[34,16,128]{2,1,0:T(8,128)(2,1)S(1)} collective-permute-done((bf16[34,16,128]{2,1,0:T(8,128)(2,1)S(1)}, bf16[34,16,128]{2,1,0:T(8,128)(2,1)S(1)}, u32[]{:S(2)}, u32[]{:S(2)}) %collective-permute-start.5) | collective-permute-done | bytes 139296 | tf_op jit(solution)/shard_map/ppermute | solution.py:604
  38.8 2.7 %collective-permute-done.6.refs_5_ = bf16[34,16,128]{2,1,0:T(8,128)(2,1)S(1)} collective-permute-done((bf16[34,16,128]{2,1,0:T(8,128)(2,1)S(1)}, bf16[34,16,128]{2,1,0:T(8,128)(2,1)S(1)}, u32[]{:S(2)}, u32[]{:S(2)}) %collective-permute-start.6) | collective-permute-done | bytes 139296 | tf_op jit(solution)/shard_map/ppermute | solution.py:604
  41.5 0.0 collective-permute-done.7.refs_6_
  41.5 3.2 %final.1 = f32[256,256]{1,0:T(8,128)} custom-call(bf16[34,16,128]{2,1,0:T(8,128)(2,1)S(1)} %get-tuple-element.41.refs_0_, bf16[40,16,128]{2,1,0:T(8,128)(2,1)S(1)} %collective-permute-done.2.from_low.refs_1_, bf16[34,16,128]{2,1,0:T(8,128)(2,1)S(1)} %collective-permute-done.3.refs_2_, bf16[34,16,128]{2,1,0:T(8,128)(2,1)S(1)} %collective-permute-done.4.refs_3_, ...), custom_call_target="tpu_custom_call" | custom-call | tf_op jit(solution)/shard_map/final/pallas_call | solution.py:615
Async XLA Ops:
  2.4 8.0 %collective-permute-start.1 = (f32[40,256]{1,0:T(8,128)S(1)}, f32[40,256]{1,0:T(8,128)S(1)}, u32[]{:S(2)}, u32[]{:S(2)}) collective-permute-start(f32[40,256]{1,0:T(8,128)S(1)} %get-tuple-element.31), channel_id=1, source_target_pairs={{0,1},{1,2},{2,3},{4,5},{5,6},{6,7},{8,9},{9,10},{10,11},{12,13},{... | collective-permute-start | bytes 122888 | tf_op jit(solution)/shard_map/ppermute | solution.py:31
  6.1 5.3 %collective-permute-start = (f32[40,256]{1,0:T(8,128)S(1)}, f32[40,256]{1,0:T(8,128)S(1)}, u32[]{:S(2)}, u32[]{:S(2)}) collective-permute-start(f32[40,256]{1,0:T(8,128)S(1)} %get-tuple-element.30), channel_id=1, source_target_pairs={{1,0},{2,1},{3,2},{5,4},{6,5},{7,6},{9,8},{10,9},{11,10},{13,12},{... | collective-permute-start | bytes 122888 | tf_op jit(solution)/shard_map/ppermute | solution.py:31
  11.4 11.7 %copy-start = (bf16[2,256,256]{2,1,0:T(8,128)(2,1)S(1)}, bf16[2,256,256]{2,1,0:T(8,128)(2,1)}, u32[]{:S(2)}) copy-start(bf16[2,256,256]{2,1,0:T(8,128)(2,1)} %vel.1) | copy-start | bytes 786436
  11.4 11.7 %copy-start.1 = (f32[256,256]{1,0:T(8,128)S(1)}, f32[256,256]{1,0:T(8,128)}, u32[]{:S(2)}) copy-start(f32[256,256]{1,0:T(8,128)} %visc.1) | copy-start | bytes 786436
  11.4 11.7 %copy-start.2 = (f32[256,256]{1,0:T(8,128)S(1)}, f32[256,256]{1,0:T(8,128)}, u32[]{:S(2)}) copy-start(f32[256,256]{1,0:T(8,128)} %fric.1) | copy-start | bytes 786436
  11.4 11.7 %copy-start.3 = (bf16[2,256,256]{2,1,0:T(8,128)(2,1)S(1)}, bf16[2,256,256]{2,1,0:T(8,128)(2,1)}, u32[]{:S(2)}) copy-start(bf16[2,256,256]{2,1,0:T(8,128)(2,1)} %drive.1) | copy-start | bytes 786436
  13.5 6.7 %collective-permute-start.2 = (bf16[40,16,128]{2,1,0:T(8,128)(2,1)S(1)}, bf16[40,16,128]{2,1,0:T(8,128)(2,1)S(1)}, u32[]{:S(2)}, u32[]{:S(2)}) collective-permute-start(bf16[40,16,128]{2,1,0:T(8,128)(2,1)S(1)} %get-tuple-element.42), channel_id=1, source_target_pairs={{0,4},{4,8},{8,12},{12,16},{16,20},{20,24},{24,28},{28,0},{1,5},{5... | collective-permute-start | bytes 491528 | tf_op jit(solution)/shard_map/ppermute | solution.py:604
  13.6 8.7 %collective-permute-start.8 = (bf16[40,16,128]{2,1,0:T(8,128)(2,1)S(1)}, bf16[40,16,128]{2,1,0:T(8,128)(2,1)S(1)}, u32[]{:S(2)}, u32[]{:S(2)}) collective-permute-start(bf16[40,16,128]{2,1,0:T(8,128)(2,1)S(1)} %get-tuple-element.48), channel_id=1, source_target_pairs={{0,28},{4,0},{8,4},{12,8},{16,12},{20,16},{24,20},{28,24},{1,29},{... | collective-permute-start | bytes 491528 | tf_op jit(solution)/shard_map/ppermute | solution.py:604
  15.0 12.0 %collective-permute-start.3 = (bf16[34,16,128]{2,1,0:T(8,128)(2,1)S(1)}, bf16[34,16,128]{2,1,0:T(8,128)(2,1)S(1)}, u32[]{:S(2)}, u32[]{:S(2)}) collective-permute-start(bf16[34,16,128]{2,1,0:T(8,128)(2,1)S(1)} %get-tuple-element.43), channel_id=1, source_target_pairs={{0,8},{4,12},{8,16},{12,20},{16,24},{20,28},{24,0},{28,4},{1,9},{5... | collective-permute-start | bytes 417800 | tf_op jit(solution)/shard_map/ppermute | solution.py:604
  15.0 12.0 %collective-permute-start.4 = (bf16[34,16,128]{2,1,0:T(8,128)(2,1)S(1)}, bf16[34,16,128]{2,1,0:T(8,128)(2,1)S(1)}, u32[]{:S(2)}, u32[]{:S(2)}) collective-permute-start(bf16[34,16,128]{2,1,0:T(8,128)(2,1)S(1)} %get-tuple-element.44), channel_id=1, source_target_pairs={{0,12},{4,16},{8,20},{12,24},{16,28},{20,0},{24,4},{28,8},{1,13},{... | collective-permute-start | bytes 417800 | tf_op jit(solution)/shard_map/ppermute | solution.py:604
  17.2 21.5 %collective-permute-start.5 = (bf16[34,16,128]{2,1,0:T(8,128)(2,1)S(1)}, bf16[34,16,128]{2,1,0:T(8,128)(2,1)S(1)}, u32[]{:S(2)}, u32[]{:S(2)}) collective-permute-start(bf16[34,16,128]{2,1,0:T(8,128)(2,1)S(1)} %get-tuple-element.45), channel_id=1, source_target_pairs={{0,16},{4,20},{8,24},{12,28},{16,0},{20,4},{24,8},{28,12},{1,17},{... | collective-permute-start | bytes 417800 | tf_op jit(solution)/shard_map/ppermute | solution.py:604
  20.2 3.0 %copy-start.4 = (s32[2,2]{1,0:T(2,128)S(1)}, s32[2,2]{1,0:T(2,128)}, u32[]{:S(2)}) copy-start(s32[2,2]{1,0:T(2,128)} %ice.1) | copy-start | bytes 52
  20.2 21.3 %collective-permute-start.6 = (bf16[34,16,128]{2,1,0:T(8,128)(2,1)S(1)}, bf16[34,16,128]{2,1,0:T(8,128)(2,1)S(1)}, u32[]{:S(2)}, u32[]{:S(2)}) collective-permute-start(bf16[34,16,128]{2,1,0:T(8,128)(2,1)S(1)} %get-tuple-element.46), channel_id=1, source_target_pairs={{0,20},{4,24},{8,28},{12,0},{16,4},{20,8},{24,12},{28,16},{1,21},{... | collective-permute-start | bytes 417800 | tf_op jit(solution)/shard_map/ppermute | solution.py:604
  22.3 19.2 %collective-permute-start.7 = (bf16[34,16,128]{2,1,0:T(8,128)(2,1)S(1)}, bf16[34,16,128]{2,1,0:T(8,128)(2,1)S(1)}, u32[]{:S(2)}, u32[]{:S(2)}) collective-permute-start(bf16[34,16,128]{2,1,0:T(8,128)(2,1)S(1)} %get-tuple-element.47), channel_id=1, source_target_pairs={{0,24},{4,28},{8,0},{12,4},{16,8},{20,12},{24,16},{28,20},{1,25},{... | collective-permute-start | bytes 417800 | tf_op jit(solution)/shard_map/ppermute | solution.py:604

commit v4 on v3

--- a/solution.py
+++ b/solution.py
@@ -21,8 +21,12 @@
 F32 = jnp.float32
 
 
-def partner(me, step, count):
-    return lax.rem(me + step, count) if isinstance(me, jax.Array) else (me + step) % count
+def partner(me, step):
+    return me ^ step
+
+
+def halo_steps(groups):
+    return [step for step in range(1, groups) if step & (step + 1) == 0]
 
 
 def from_behind(value, axis, steps):
@@ -118,7 +122,7 @@
 def gather_scenes(obs, pays, steps, place, groups, blocks, me, sems):
     copies = []
     for number, step in enumerate(steps):
-        to = partner(me, step, groups)
+        to = partner(me, step)
         for rank in range(CAP):
             scene = jnp.maximum(place[(to + 1) * CAP + rank], 0)
             target = pays[number].at[pl.ds(rank * 2 * blocks, 2 * blocks)]
@@ -143,7 +147,7 @@
     copies = gather_scenes(obs, pays, range(groups), place, groups, blocks, me, scene_sem)
     wait_all(scalars[1:] + loads)
     for step in range(groups):
-        to = partner(me, step, groups)
+        to = partner(me, step)
         pays[step][CAP * 2 * blocks] = easting_block(
             to, place, slot_s, weight_s, lambda scene, part, side: edges[side * 2 + part, scene]
         )
@@ -219,22 +223,27 @@
         pay[base + 2 * number + 1] = jnp.concatenate([both, fill], axis=0).astype(jnp.bfloat16)
 
 
-def read_halo(pay, base, pack, keep):
+def read_halo(pays, base, pack, me, beside):
     first = FIELDS[VISC][0]
     count = FIELDS[FRIC][0] + FIELDS[FRIC][1] - first
     for number in range(pack.shape[1] // LANE):
         lanes = slice(number * LANE, (number + 1) * LANE)
-        more = pay[base + 2 * number + 1].astype(F32)
-        pack[:, lanes] = pay[base + 2 * number].astype(F32)
+        high, more = jnp.zeros((PACK, LANE), F32), jnp.zeros((PACK, LANE), F32)
+        for step, pay in pays.items():
+            here = partner(me, step) == beside
+            high = jnp.where(here, pay[base + 2 * number].astype(F32), high)
+            more = jnp.where(here, pay[base + 2 * number + 1].astype(F32), more)
+        pack[:, lanes] = high
         pack[first : first + count, lanes] += more[0:count]
         pack[first : first + count, lanes] += more[count : 2 * count]
-    pack[...] = jnp.where(keep, pack[...], 0.0)
-
-
-def widen_kernel(groups, count, tile, *refs):
+
+
+def widen_kernel(groups, count, tile, early, late, *refs):
     ice, vel, visc, fric, drive, right, left = refs[:7]
-    pays = refs[7 + groups : 7 + 2 * groups]
-    ice_s, notes, first_b, last_b, first_f, last_f, turned, to_low, to_high, place, filled, sems = refs[7 + 2 * groups :]
+    pays = dict(zip(late, refs[7 + len(late) :]))
+    refs = refs[7 + 2 * len(late) :]
+    apart = dict(zip(early, refs))
+    ice_s, notes, first_b, last_b, first_f, last_f, turned, to_low, to_high, place, filled, sems = refs[len(early) :]
     cells = visc.shape[0]
     cells_y = visc.shape[1]
     blocks = tile // PACK
@@ -268,15 +277,15 @@
         to_low[at : at + depth, cells_y:] = side_tile(upright[0:8], index)[0:depth]
         to_high[at : at + depth, cells_y:] = side_tile(upright[cells - 8 :], index)[8 - depth : 8]
     base = CAP * 2 * blocks + 2
-    write_halo(pays[1], base, to_high[...])
-    write_halo(pays[groups - 1], base, to_low[...])
+    for step in halo_steps(groups):
+        write_halo(pays[step], base, jnp.where(partner(me, step) > me, to_high[...], to_low[...]))
     packs = (right, left)
     for side in range(2):
         fill_places(place.at[side], filled, groups, count, lambda scene: notes[side, 0, scene].astype(jnp.int32))
     row = lax.broadcasted_iota(jnp.int32, (PACK, LANE), 0)
     lane = lax.broadcasted_iota(jnp.int32, (PACK, LANE), 1)
     for step in range(groups):
-        to = partner(me, step, groups)
+        to = partner(me, step)
         block = jnp.zeros((PACK, LANE), F32)
         for side in range(2):
             for rank in range(CAP):
@@ -303,7 +312,10 @@
                     block = jnp.where((row == 8) & (lane == base + part), value, block)
                 value = jnp.where(where == (2 if side == 0 else 1), amount, 0.0)
                 block = jnp.where((row == 8) & (lane == base + 2), value, block)
-        pays[step][CAP * 2 * blocks + 1] = block.astype(jnp.bfloat16)
+        if step in early:
+            apart[step][0] = block.astype(jnp.bfloat16)
+        else:
+            pays[step][CAP * 2 * blocks + 1] = block.astype(jnp.bfloat16)
 
 
 def stress_block(u, v, visc, low, rows, wide):
@@ -326,7 +338,10 @@
     return push_u, push_v
 
 
-def sweep_kernel(groups, tile, ice, vel, visc, fric, drive, right, left, from_low, from_high, *refs):
+def sweep_kernel(groups, tile, ice, vel, visc, fric, drive, right, left, *refs):
+    steps = halo_steps(groups)
+    pays = dict(zip(steps, refs))
+    refs = refs[len(steps) :]
     second, ease, lead, trail, wide_visc, wide_ice = refs[:6]
     (
         u, v, wide_fric, drive_u, drive_v, next_u, next_v, relax_u, relax_v, sxx, syy, sxy, turned,
@@ -338,8 +353,8 @@
     upright = side_tiles(right, left, turned)
     base = CAP * 2 * (tile // PACK) + 2
     me = lax.axis_index("gx")
-    read_halo(from_low, base, low_pack, me > 0)
-    read_halo(from_high, base, high_pack, me < groups - 1)
+    read_halo(pays, base, low_pack, me, me - 1)
+    read_halo(pays, base, high_pack, me, me + 1)
     wait_all(loads)
     own_rows = slice(PAD, PAD + cells)
     for index, field in enumerate((u, v, wide_visc, wide_fric, drive_u, drive_v, wide_ice)):
@@ -406,8 +421,10 @@
                 )
 
 
-def final_kernel(groups, tile, *refs):
+def final_kernel(groups, tile, early, *refs):
     pays = refs[:groups]
+    apart = dict(zip(early, refs[groups:]))
+    refs = refs[len(early) :]
     second, ease, lead, trail, visc, ice, grad = refs[groups : groups + 7]
     misfit, u, v, sxx, syy, sxy, table, total, rows_x, rows_y, turned = refs[groups + 7 :]
     rows, wide = visc.shape
@@ -419,7 +436,8 @@
     lift = (u, v)
     for group in range(groups):
         rows_x[pl.ds(group, PACK, stride=groups), :] = pays[group][CAP * 2 * blocks].astype(F32)
-        rows_y[pl.ds(group, PACK, stride=groups), :] = pays[group][CAP * 2 * blocks + 1].astype(F32)
+        side = apart[group][0] if group in early else pays[group][CAP * 2 * blocks + 1]
+        rows_y[pl.ds(group, PACK, stride=groups), :] = side.astype(F32)
 
     def raw(source, number):
         return source[number * groups : (number + 1) * groups, :]
@@ -551,11 +569,36 @@
     bf16, i32 = jnp.bfloat16, jnp.int32
     deep = CAP * 2 * blocks
     tall = SCENES + count + 8
+    half = groups // 2
+    early = (half, half + 1)
+    late = tuple(step for step in range(groups) if step not in early)
     halo = 2 * (wide // LANE)
-    pay_shapes = [
-        pltpu.VMEM((deep + 2 + (halo if step in (1, groups - 1) else 0), PACK, LANE), bf16) for step in range(groups)
-    ]
+
+    def pay(step):
+        more = 0 if step in early else 1 + (halo if step in halo_steps(groups) else 0)
+        return pltpu.VMEM((deep + 1 + more, PACK, LANE), bf16)
+
+    def move(step, value, *others):
+        pairs = [(me, partner(me, step)) for me in range(groups)]
+        return lax.ppermute(after(value, *others) if others else value, "gx", pairs)
+
     places = [pltpu.SMEM(((groups + 2) * CAP,), i32), pltpu.SMEM((groups,), i32)]
+    pays = pl.pallas_call(
+        functools.partial(gather_kernel, groups, count, tile),
+        out_shape=[pay(step) for step in range(groups)],
+        in_specs=[HBM] * 4,
+        out_specs=[VMEM] * groups,
+        scratch_shapes=[
+            pltpu.SMEM((1, count), i32), pltpu.SMEM((1, count), i32), short(1, count), full(1, count),
+            pltpu.SMEM((1, count), F32), short(4, count, PACK, LANE), *places, dma((3,)), dma((4,)),
+            dma((groups * CAP,)),
+        ],
+        compiler_params=limit,
+        name="gather",
+    )(*in_place(owner, slot, weight, obs))
+    got = [pays[0]] * groups
+    for step in early:
+        got[step] = move(step, pays[step])
     y_low, y_high = pl.pallas_call(
         functools.partial(pack_kernel, count, tile),
         out_shape=[pltpu.VMEM((tall, cells_x), F32)] * 2,
@@ -568,28 +611,15 @@
         ],
         compiler_params=limit,
         name="pack",
-    )(*in_place(owner, slot, weight, ice_mask, obs, vel0, visc, fric, drive))
+    )(*in_place(after(owner, pays[half]), slot, weight, ice_mask, obs, vel0, visc, fric, drive))
     right = from_behind(y_low, "gy", -1)
     left = from_behind(y_high, "gy", 1)
-    pays = pl.pallas_call(
-        functools.partial(gather_kernel, groups, count, tile),
-        out_shape=pay_shapes,
-        in_specs=[HBM] * 4,
+    outs = pl.pallas_call(
+        functools.partial(widen_kernel, groups, count, tile, early, late),
+        out_shape=[pay(step) for step in late] + [pltpu.VMEM((1, PACK, LANE), bf16)] * len(early),
+        in_specs=[HBM] * 5 + [VMEM] * (2 + len(late)),
         out_specs=[VMEM] * groups,
-        scratch_shapes=[
-            pltpu.SMEM((1, count), i32), pltpu.SMEM((1, count), i32), short(1, count), full(1, count),
-            pltpu.SMEM((1, count), F32), short(4, count, PACK, LANE), *places, dma((3,)), dma((4,)),
-            dma((groups * CAP,)),
-        ],
-        compiler_params=limit,
-        name="gather",
-    )(*in_place(after(owner, y_low), slot, weight, obs))
-    ready = pl.pallas_call(
-        functools.partial(widen_kernel, groups, count, tile),
-        out_shape=pay_shapes,
-        in_specs=[HBM] * 5 + [VMEM] * (2 + groups),
-        out_specs=[VMEM] * groups,
-        input_output_aliases={7 + step: step for step in range(groups)},
+        input_output_aliases={7 + number: number for number in range(len(late))},
         scratch_shapes=[
             pltpu.SMEM(ice_mask.shape, i32), pltpu.SMEM((2, 8, cells_x), F32), short(4, 16, cells_y),
             short(4, 16, cells_y), full(2, 8, cells_y), full(2, 8, cells_y), full(LANE, cells_x), full(PACK, wide),
@@ -597,25 +627,30 @@
         ],
         compiler_params=limit,
         name="widen",
-    )(*in_place(ice_mask, vel0, visc, fric, drive), right, left, *pays)
-    got = [ready[0]]
-    for step in range(1, groups):
-        pairs = [(me, partner(me, step, groups)) for me in range(groups)]
-        got.append(lax.ppermute(ready[step], "gx", pairs))
+    )(*in_place(ice_mask, vel0, visc, fric, drive), after(right, got[half]), left, *(pays[step] for step in late))
+    ready = dict(zip(late, outs))
+    got[0] = ready[0]
+    order = [groups - 1, 1, *range(half + 2, groups - 1), half - 1, *(step for step in range(2, half - 1))]
+    waits = {half + 2: half + 1}
+    for step in order:
+        got[step] = move(step, ready[step], *([got[waits[step]]] if step in waits else []))
+    apart = [
+        move(step, value, got[wait]) for step, value, wait in zip(early, outs[len(late) :], (1, half - 1))
+    ]
     base = pl.pallas_call(
         functools.partial(sweep_kernel, groups, tile),
         out_shape=[shape(2, rows, wide)] * 2 + [shape(2, cells_x, cells_y)] * 2 + [shape(rows, wide)] * 2,
-        in_specs=[HBM] + [VMEM] * 8,
+        in_specs=[HBM] + [VMEM] * (6 + len(halo_steps(groups))),
         out_specs=[VMEM] * 6,
         scratch_shapes=[full(rows, wide)] * 12
         + [full(LANE, cells_x), full(PACK, wide), full(PACK, wide), pltpu.SMEM(ice_mask.shape, i32), dma((1,))],
         compiler_params=limit,
         name="sweep",
-    )(ice_mask, vel0, visc, fric, drive, right, left, got[1], got[groups - 1])
+    )(ice_mask, vel0, visc, fric, drive, right, left, *(got[step] for step in halo_steps(groups)))
     return pl.pallas_call(
-        functools.partial(final_kernel, groups, tile),
+        functools.partial(final_kernel, groups, tile, early),
         out_shape=shape(cells_x, cells_y),
-        in_specs=[VMEM] * (groups + 6),
+        in_specs=[VMEM] * (groups + len(early) + 6),
         out_specs=VMEM,
         scratch_shapes=[full(2, cells_x, cells_y)] + [full(rows, wide)] * 5
         + [
@@ -624,7 +659,7 @@
         ],
         compiler_params=limit,
         name="final",
-    )(*got, *base)
+    )(*got, *apart, *base)
 
 
 def solution(mesh):

time: 45 us -> 42.8 us (0.951)
  the two profiles are of different devices: /device:TPU:27 before, /device:TPU:0 now
where the time goes in v4:
time: 42.8 us; the launch traced here: 42.5 us
  starting transfers between devices  20.7 us (48%)
  Pallas kernels  13.8 us (32%)
  waiting for transfers between devices  7.93 us (19%)
    ppermute x9, starting transfers between devices, move(): return lax.ppermute(after(value, *others) if others else value, 'gx', pairs)  16.3 us
    ppermute x9, waiting for transfers between devices, move(): return lax.ppermute(after(value, *others) if others else value, 'gx', pairs)  7.92 us
    ppermute x2, starting transfers between devices, from_behind(): lax.ppermute(value, axis, [(source, source + steps) for source in range(f...  4.32 us
    pallas_call x1, Pallas kernels, body(): pl.pallas_call(functools.partial(sweep_kernel, groups, tile), out_shape=[...  3.85 us
    pallas_call x1, Pallas kernels, body(): pl.pallas_call(functools.partial(final_kernel, groups, tile, early), out_...  3.17 us
    pallas_call x1, Pallas kernels, body(): pl.pallas_call(functools.partial(pack_kernel, count, tile), out_shape=[pl...  2.36 us
    pallas_call x1, Pallas kernels, body(): pl.pallas_call(functools.partial(gather_kernel, groups, count, tile), out...  2.34 us
    pallas_call x1, Pallas kernels, body(): pl.pallas_call(functools.partial(widen_kernel, groups, count, tile, early...  2.06 us
  transfers between devices with their start and end apart: 11, of which 5 were waited for; matrix products, arithmetic and copies ran while one was open for 0% of the time, Pallas kernels for 19%

profile of v4, /device:TPU:0, one launch (start us, length us, event | category | flops | bytes accessed | tf_op | source)
XLA Modules:
  0.0 42.5 jit_solution(11090372920270880022)
XLA Ops:
  0.0 2.3 %gather.1 = (bf16[34,16,128]{2,1,0:T(8,128)(2,1)S(1)}, bf16[40,16,128]{2,1,0:T(8,128)(2,1)S(1)}, bf16[34,16,128]{2,1,0:T(8,128)(2,1)S(1)}, bf16[40,16,128]{2,1,0...) custom-call(s32[1,16]{1,0:T(1,128)} %bitcast.4, ...), custom_call_target="tpu_custom_call" | custom-call | tf_op jit(solution)/shard_map/gather/pallas_call | solution.py:586
  2.3 4.1 %collective-permute-start.1 = (bf16[33,16,128]{2,1,0:T(8,128)(2,1)S(1)}, bf16[33,16,128]{2,1,0:T(8,128)(2,1)S(1)}, u32[]{:S(2)}, u32[]{:S(2)}) collective-permute-start(bf16[33,16,128]{2,1,0:T(8,128)(2,1)S(1)} %get-tuple-element.34), channel_id=1, source_target_pairs={{0,16},{4,20},{8,24},{12,28},{16,0},{20,4},{24,8},{28,12},{1,17},{... | collective-permute-start | bytes 405512 | tf_op jit(solution)/shard_map/ppermute | solution.py:583
  6.4 1.3 %collective-permute-start.6 = (bf16[33,16,128]{2,1,0:T(8,128)(2,1)S(1)}, bf16[33,16,128]{2,1,0:T(8,128)(2,1)S(1)}, u32[]{:S(2)}, u32[]{:S(2)}) collective-permute-start(bf16[33,16,128]{2,1,0:T(8,128)(2,1)S(1)} %get-tuple-element.49), channel_id=1, source_target_pairs={{0,20},{4,16},{8,28},{12,24},{16,4},{20,0},{24,12},{28,8},{1,21},{... | collective-permute-start | bytes 405512 | tf_op jit(solution)/shard_map/ppermute | solution.py:583
  7.7 2.4 %pack.1 = (f32[40,256]{1,0:T(8,128)S(1)}, f32[40,256]{1,0:T(8,128)S(1)}) custom-call(s32[1,16]{1,0:T(1,128)} %bitcast.5, s32[1,16]{1,0:T(1,128)} %refs_1_.4, bf16[1,16]{1,0:T(2,128)(2,1)} %refs_2_.4, s32[2,2]{1,0:T(2,128)} %ice.1, bf16[16,16,16,128]{3,2,1,0:T(8,128)(2,1)} %bitcast.3, bf16[2,256,256]{2,1,0:T(8,128)(2,1)} %vel.1, f32[256,256]{1,0:T(8,128)} %visc.1, ...), custom_call_target="tpu_custom_call" | custom-call | tf_op jit(solution)/shard_map/pack/pallas_call | solution.py:602
  10.1 1.3 %collective-permute-start = (f32[40,256]{1,0:T(8,128)S(1)}, f32[40,256]{1,0:T(8,128)S(1)}, u32[]{:S(2)}, u32[]{:S(2)}) collective-permute-start(f32[40,256]{1,0:T(8,128)S(1)} %get-tuple-element.36), channel_id=1, source_target_pairs={{1,0},{2,1},{3,2},{5,4},{6,5},{7,6},{9,8},{10,9},{11,10},{13,12},{... | collective-permute-start | bytes 122888 | tf_op jit(solution)/shard_map/ppermute | solution.py:35
  11.4 3.0 %collective-permute-start.2 = (f32[40,256]{1,0:T(8,128)S(1)}, f32[40,256]{1,0:T(8,128)S(1)}, u32[]{:S(2)}, u32[]{:S(2)}) collective-permute-start(f32[40,256]{1,0:T(8,128)S(1)} %get-tuple-element.38), channel_id=1, source_target_pairs={{0,1},{1,2},{2,3},{4,5},{5,6},{6,7},{8,9},{9,10},{10,11},{12,13},{... | collective-permute-start | bytes 122888 | tf_op jit(solution)/shard_map/ppermute | solution.py:35
  14.4 0.0 collective-permute-done.refs_5_.right
  14.4 2.2 %collective-permute-done.1.refs_4_ = bf16[33,16,128]{2,1,0:T(8,128)(2,1)S(1)} collective-permute-done((bf16[33,16,128]{2,1,0:T(8,128)(2,1)S(1)}, bf16[33,16,128]{2,1,0:T(8,128)(2,1)S(1)}, u32[]{:S(2)}, u32[]{:S(2)}) %collective-permute-start.1) | collective-permute-done | bytes 135200 | tf_op jit(solution)/shard_map/ppermute | solution.py:583
  16.7 0.0 collective-permute-done.2.refs_6_.left
  16.7 0.0 copy-start
  16.7 0.0 copy-start.1
  16.7 0.0 copy-start.2
  16.7 0.0 copy-start.3
  16.7 2.1 %widen.1 = (bf16[34,16,128]{2,1,0:T(8,128)(2,1)S(1)}, bf16[40,16,128]{2,1,0:T(8,128)(2,1)S(1)}, bf16[34,16,128]{2,1,0:T(8,128)(2,1)S(1)}, bf16[40,16,128]{2,1,0:...) custom-call(s32[2,2]{1,0:T(2,128)} %ice.1, ...), custom_call_target="tpu_custom_call", output_to_operand_aliasing={{0}: (7, {}), {1}: (8, {}), {2}: (9, {}), {3}: (10, {}), {4... | custom-call | tf_op jit(solution)/shard_map/widen/pallas_call | solution.py:617
  18.7 1.9 %collective-permute-start.3 = (bf16[40,16,128]{2,1,0:T(8,128)(2,1)S(1)}, bf16[40,16,128]{2,1,0:T(8,128)(2,1)S(1)}, u32[]{:S(2)}, u32[]{:S(2)}) collective-permute-start(bf16[40,16,128]{2,1,0:T(8,128)(2,1)S(1)} %get-tuple-element.46), channel_id=1, source_target_pairs={{0,4},{4,0},{8,12},{12,8},{16,20},{20,16},{24,28},{28,24},{1,5},{5... | collective-permute-start | bytes 491528 | tf_op jit(solution)/shard_map/ppermute | solution.py:583
  20.6 0.0 collective-permute-start.5
  20.7 2.4 %collective-permute-start.8 = (bf16[40,16,128]{2,1,0:T(8,128)(2,1)S(1)}, bf16[40,16,128]{2,1,0:T(8,128)(2,1)S(1)}, u32[]{:S(2)}, u32[]{:S(2)}) collective-permute-start(bf16[40,16,128]{2,1,0:T(8,128)(2,1)S(1)} %get-tuple-element.52), channel_id=1, source_target_pairs={{0,28},{4,24},{8,20},{12,16},{16,12},{20,8},{24,4},{28,0},{1,29},{... | collective-permute-start | bytes 491528 | tf_op jit(solution)/shard_map/ppermute | solution.py:583
  23.1 0.0 collective-permute-done.6.refs_5_
  23.1 1.9 %collective-permute-start.7 = (bf16[34,16,128]{2,1,0:T(8,128)(2,1)S(1)}, bf16[34,16,128]{2,1,0:T(8,128)(2,1)S(1)}, u32[]{:S(2)}, u32[]{:S(2)}) collective-permute-start(bf16[34,16,128]{2,1,0:T(8,128)(2,1)S(1)} %get-tuple-element.51), channel_id=1, source_target_pairs={{0,24},{4,28},{8,16},{12,20},{16,8},{20,12},{24,0},{28,4},{1,25},{... | collective-permute-start | bytes 417800 | tf_op jit(solution)/shard_map/ppermute | solution.py:583
  25.0 0.6 %collective-permute-start.4 = (bf16[34,16,128]{2,1,0:T(8,128)(2,1)S(1)}, bf16[34,16,128]{2,1,0:T(8,128)(2,1)S(1)}, u32[]{:S(2)}, u32[]{:S(2)}) collective-permute-start(bf16[34,16,128]{2,1,0:T(8,128)(2,1)S(1)} %get-tuple-element.47), channel_id=1, source_target_pairs={{0,8},{4,12},{8,0},{12,4},{16,24},{20,28},{24,16},{28,20},{1,9},{5... | collective-permute-start | bytes 417800 | tf_op jit(solution)/shard_map/ppermute | solution.py:583
  25.6 2.8 %collective-permute-done.3.refs_0_.refs_1_ = bf16[40,16,128]{2,1,0:T(8,128)(2,1)S(1)} collective-permute-done((bf16[40,16,128]{2,1,0:T(8,128)(2,1)S(1)}, bf16[40,16,128]{2,1,0:T(8,128)(2,1)S(1)}, u32[]{:S(2)}, u32[]{:S(2)}) %collective-permute-start.3) | collective-permute-done | bytes 163872 | tf_op jit(solution)/shard_map/ppermute | solution.py:583
  28.4 0.0 copy-start.4
  28.4 3.7 %collective-permute-start.9 = (bf16[1,16,128]{2,1,0:T(8,128)(2,1)S(1)}, bf16[1,16,128]{2,1,0:T(8,128)(2,1)S(1)}, u32[]{:S(2)}, u32[]{:S(2)}) collective-permute-start(bf16[1,16,128]{2,1,0:T(8,128)(2,1)S(1)} %get-tuple-element.54), channel_id=1, source_target_pairs={{0,16},{4,20},{8,24},{12,28},{16,0},{20,4},{24,8},{28,12},{1,17},{... | collective-permute-start | bytes 12296 | tf_op jit(solution)/shard_map/ppermute | solution.py:583
  32.1 0.0 collective-permute-done.5.refs_1_.refs_3_
  32.1 0.4 %collective-permute-start.10 = (bf16[1,16,128]{2,1,0:T(8,128)(2,1)S(1)}, bf16[1,16,128]{2,1,0:T(8,128)(2,1)S(1)}, u32[]{:S(2)}, u32[]{:S(2)}) collective-permute-start(bf16[1,16,128]{2,1,0:T(8,128)(2,1)S(1)} %get-tuple-element.56), channel_id=1, source_target_pairs={{0,20},{4,16},{8,28},{12,24},{16,4},{20,0},{24,12},{28,8},{1,21},{... | collective-permute-start | bytes 12296 | tf_op jit(solution)/shard_map/ppermute | solution.py:583
  32.6 0.0 collective-permute-done.8.refs_2_.refs_7_
  32.6 0.0 copy-done
  32.6 0.0 copy-done.1
  32.6 0.0 copy-done.2
  32.6 0.0 copy-done.3
  32.6 0.0 copy-done.4
  32.6 3.9 %sweep.1 = (f32[2,288,384]{2,1,0:T(8,128)S(1)}, f32[2,288,384]{2,1,0:T(8,128)S(1)}, f32[2,256,256]{2,1,0:T(8,128)S(1)}, f32[2,256,256]{2,1,0:T(8,128)S(1)}, f32[...) custom-call(s32[2,2]{1,0:T(2,128)S(1)} %copy-done.4, bf16[2,256,256]{2,1,0:T(8,128)(2,1)S(1)} %copy-done, ...), custom_call_target="tpu_custom_call" | custom-call | tf_op jit(solution)/shard_map/sweep/pallas_call | solution.py:640
  36.5 0.0 collective-permute-done.7.refs_6_
  36.5 0.1 collective-permute-done.4.refs_2_
  36.6 2.4 %collective-permute-done.9.refs_8_ = bf16[1,16,128]{2,1,0:T(8,128)(2,1)S(1)} collective-permute-done((bf16[1,16,128]{2,1,0:T(8,128)(2,1)S(1)}, bf16[1,16,128]{2,1,0:T(8,128)(2,1)S(1)}, u32[]{:S(2)}, u32[]{:S(2)}) %collective-permute-start.9) | collective-permute-done | bytes 4128 | tf_op jit(solution)/shard_map/ppermute | solution.py:583
  39.0 0.4 collective-permute-done.10.refs_9_
  39.3 3.2 %final.1 = f32[256,256]{1,0:T(8,128)} custom-call(bf16[34,16,128]{2,1,0:T(8,128)(2,1)S(1)} %get-tuple-element.45.refs_0_, bf16[40,16,128]{2,1,0:T(8,128)(2,1)S(1)} %collective-permute-done.3.refs_0_.refs_1_, bf16[34,16,128]{2,1,0:T(8,128)(2,1)S(1)} %collective-permute-done.4.refs_2_, bf16[40,16,128]{2,1,0:T(8,128)(2,1)S(1)} %collective-permute-done.5.refs_1_.refs_3_, ...), custom_call_target="tpu_custom_call" | custom-call | tf_op jit(solution)/shard_map/final/pallas_call | solution.py:650
Async XLA Ops:
  2.3 14.3 %collective-permute-start.1 = (bf16[33,16,128]{2,1,0:T(8,128)(2,1)S(1)}, bf16[33,16,128]{2,1,0:T(8,128)(2,1)S(1)}, u32[]{:S(2)}, u32[]{:S(2)}) collective-permute-start(bf16[33,16,128]{2,1,0:T(8,128)(2,1)S(1)} %get-tuple-element.34), channel_id=1, source_target_pairs={{0,16},{4,20},{8,24},{12,28},{16,0},{20,4},{24,8},{28,12},{1,17},{... | collective-permute-start | bytes 405512 | tf_op jit(solution)/shard_map/ppermute | solution.py:583
  6.4 16.6 %collective-permute-start.6 = (bf16[33,16,128]{2,1,0:T(8,128)(2,1)S(1)}, bf16[33,16,128]{2,1,0:T(8,128)(2,1)S(1)}, u32[]{:S(2)}, u32[]{:S(2)}) collective-permute-start(bf16[33,16,128]{2,1,0:T(8,128)(2,1)S(1)} %get-tuple-element.49), channel_id=1, source_target_pairs={{0,20},{4,16},{8,28},{12,24},{16,4},{20,0},{24,12},{28,8},{1,21},{... | collective-permute-start | bytes 405512 | tf_op jit(solution)/shard_map/ppermute | solution.py:583
  10.1 4.3 %collective-permute-start = (f32[40,256]{1,0:T(8,128)S(1)}, f32[40,256]{1,0:T(8,128)S(1)}, u32[]{:S(2)}, u32[]{:S(2)}) collective-permute-start(f32[40,256]{1,0:T(8,128)S(1)} %get-tuple-element.36), channel_id=1, source_target_pairs={{1,0},{2,1},{3,2},{5,4},{6,5},{7,6},{9,8},{10,9},{11,10},{13,12},{... | collective-permute-start | bytes 122888 | tf_op jit(solution)/shard_map/ppermute | solution.py:35
  11.4 5.3 %collective-permute-start.2 = (f32[40,256]{1,0:T(8,128)S(1)}, f32[40,256]{1,0:T(8,128)S(1)}, u32[]{:S(2)}, u32[]{:S(2)}) collective-permute-start(f32[40,256]{1,0:T(8,128)S(1)} %get-tuple-element.38), channel_id=1, source_target_pairs={{0,1},{1,2},{2,3},{4,5},{5,6},{6,7},{8,9},{9,10},{10,11},{12,13},{... | collective-permute-start | bytes 122888 | tf_op jit(solution)/shard_map/ppermute | solution.py:35
  16.7 15.9 %copy-start = (bf16[2,256,256]{2,1,0:T(8,128)(2,1)S(1)}, bf16[2,256,256]{2,1,0:T(8,128)(2,1)}, u32[]{:S(2)}) copy-start(bf16[2,256,256]{2,1,0:T(8,128)(2,1)} %vel.1) | copy-start | bytes 786436
  16.7 15.9 %copy-start.1 = (f32[256,256]{1,0:T(8,128)S(1)}, f32[256,256]{1,0:T(8,128)}, u32[]{:S(2)}) copy-start(f32[256,256]{1,0:T(8,128)} %visc.1) | copy-start | bytes 786436
  16.7 15.9 %copy-start.2 = (f32[256,256]{1,0:T(8,128)S(1)}, f32[256,256]{1,0:T(8,128)}, u32[]{:S(2)}) copy-start(f32[256,256]{1,0:T(8,128)} %fric.1) | copy-start | bytes 786436
  16.7 15.9 %copy-start.3 = (bf16[2,256,256]{2,1,0:T(8,128)(2,1)S(1)}, bf16[2,256,256]{2,1,0:T(8,128)(2,1)}, u32[]{:S(2)}) copy-start(bf16[2,256,256]{2,1,0:T(8,128)(2,1)} %drive.1) | copy-start | bytes 786436
  18.7 9.7 %collective-permute-start.3 = (bf16[40,16,128]{2,1,0:T(8,128)(2,1)S(1)}, bf16[40,16,128]{2,1,0:T(8,128)(2,1)S(1)}, u32[]{:S(2)}, u32[]{:S(2)}) collective-permute-start(bf16[40,16,128]{2,1,0:T(8,128)(2,1)S(1)} %get-tuple-element.46), channel_id=1, source_target_pairs={{0,4},{4,0},{8,12},{12,8},{16,20},{20,16},{24,28},{28,24},{1,5},{5... | collective-permute-start | bytes 491528 | tf_op jit(solution)/shard_map/ppermute | solution.py:583
  20.6 11.5 %collective-permute-start.5 = (bf16[40,16,128]{2,1,0:T(8,128)(2,1)S(1)}, bf16[40,16,128]{2,1,0:T(8,128)(2,1)S(1)}, u32[]{:S(2)}, u32[]{:S(2)}) collective-permute-start(bf16[40,16,128]{2,1,0:T(8,128)(2,1)S(1)} %get-tuple-element.48), channel_id=1, source_target_pairs={{0,12},{4,8},{8,4},{12,0},{16,28},{20,24},{24,20},{28,16},{1,13},{... | collective-permute-start | bytes 491528 | tf_op jit(solution)/shard_map/ppermute | solution.py:583
  20.7 11.9 %collective-permute-start.8 = (bf16[40,16,128]{2,1,0:T(8,128)(2,1)S(1)}, bf16[40,16,128]{2,1,0:T(8,128)(2,1)S(1)}, u32[]{:S(2)}, u32[]{:S(2)}) collective-permute-start(bf16[40,16,128]{2,1,0:T(8,128)(2,1)S(1)} %get-tuple-element.52), channel_id=1, source_target_pairs={{0,28},{4,24},{8,20},{12,16},{16,12},{20,8},{24,4},{28,0},{1,29},{... | collective-permute-start | bytes 491528 | tf_op jit(solution)/shard_map/ppermute | solution.py:583
  23.1 13.4 %collective-permute-start.7 = (bf16[34,16,128]{2,1,0:T(8,128)(2,1)S(1)}, bf16[34,16,128]{2,1,0:T(8,128)(2,1)S(1)}, u32[]{:S(2)}, u32[]{:S(2)}) collective-permute-start(bf16[34,16,128]{2,1,0:T(8,128)(2,1)S(1)} %get-tuple-element.51), channel_id=1, source_target_pairs={{0,24},{4,28},{8,16},{12,20},{16,8},{20,12},{24,0},{28,4},{1,25},{... | collective-permute-start | bytes 417800 | tf_op jit(solution)/shard_map/ppermute | solution.py:583
  25.0 11.6 %collective-permute-start.4 = (bf16[34,16,128]{2,1,0:T(8,128)(2,1)S(1)}, bf16[34,16,128]{2,1,0:T(8,128)(2,1)S(1)}, u32[]{:S(2)}, u32[]{:S(2)}) collective-permute-start(bf16[34,16,128]{2,1,0:T(8,128)(2,1)S(1)} %get-tuple-element.47), channel_id=1, source_target_pairs={{0,8},{4,12},{8,0},{12,4},{16,24},{20,28},{24,16},{28,20},{1,9},{5... | collective-permute-start | bytes 417800 | tf_op jit(solution)/shard_map/ppermute | solution.py:583
  28.4 4.2 %copy-start.4 = (s32[2,2]{1,0:T(2,128)S(1)}, s32[2,2]{1,0:T(2,128)}, u32[]{:S(2)}) copy-start(s32[2,2]{1,0:T(2,128)} %ice.1) | copy-start | bytes 52
  28.4 10.5 %collective-permute-start.9 = (bf16[1,16,128]{2,1,0:T(8,128)(2,1)S(1)}, bf16[1,16,128]{2,1,0:T(8,128)(2,1)S(1)}, u32[]{:S(2)}, u32[]{:S(2)}) collective-permute-start(bf16[1,16,128]{2,1,0:T(8,128)(2,1)S(1)} %get-tuple-element.54), channel_id=1, source_target_pairs={{0,16},{4,20},{8,24},{12,28},{16,0},{20,4},{24,8},{28,12},{1,17},{... | collective-permute-start | bytes 12296 | tf_op jit(solution)/shard_map/ppermute | solution.py:583
  32.1 7.2 %collective-permute-start.10 = (bf16[1,16,128]{2,1,0:T(8,128)(2,1)S(1)}, bf16[1,16,128]{2,1,0:T(8,128)(2,1)S(1)}, u32[]{:S(2)}, u32[]{:S(2)}) collective-permute-start(bf16[1,16,128]{2,1,0:T(8,128)(2,1)S(1)} %get-tuple-element.56), channel_id=1, source_target_pairs={{0,20},{4,16},{8,28},{12,24},{16,4},{20,0},{24,12},{28,8},{1,21},{... | collective-permute-start | bytes 12296 | tf_op jit(solution)/shard_map/ppermute | solution.py:583

commit v5 on v4

--- a/solution.py
+++ b/solution.py
@@ -14,7 +14,6 @@
 PACK = 16
 FIELDS = ((0, 3), (3, 3), (6, 3), (9, 2), (11, 2), (13, 2), (15, 1))
 U, V, VISC, FRIC, DRIVE_U, DRIVE_V, ICE = range(7)
-SCENES = PACK
 
 VMEM = pl.BlockSpec(memory_space=pltpu.VMEM)
 HBM = pl.BlockSpec(memory_space=pltpu.HBM)
@@ -29,18 +28,24 @@
     return [step for step in range(1, groups) if step & (step + 1) == 0]
 
 
-def from_behind(value, axis, steps):
-    count = lax.axis_size(axis)
-    first, last = (max(0, -steps), min(count, count - steps))
-    return lax.ppermute(value, axis, [(source, source + steps) for source in range(first, last)])
-
-
 def after(value, *others):
     return lax.optimization_barrier((value, *others))[0]
 
 
 def in_place(*values):
     return [pltpu.with_memory_space_constraint(value, pltpu.HBM) for value in values]
+
+
+def swap(even, odd):
+    count = lax.axis_size("gy")
+    near = [(me, me ^ 1) for me in range(count)]
+    far = [(me, me + 1 if me % 2 else me - 1) for me in range(1, count - 1)]
+    return lax.ppermute(even, "gy", near), lax.ppermute(odd, "gy", far)
+
+
+def both_sides(first, second):
+    even = lax.rem(lax.axis_index("gy"), 2) == 0
+    return jnp.where(even, first, second), jnp.where(even, second, first)
 
 
 def copy_all(pairs, sems, first=0):
@@ -154,50 +159,96 @@
     wait_all(copies)
 
 
-def pack_kernel(count, tile, *refs):
-    owner, slot, weight, ice, obs_h, vel_h, visc_h, fric_h, drive_h, to_low, to_high = refs[:11]
-    ice_s, owner_v, slot_v, weight_v, obs, vel, visc, fric, drive, more_sem, load_sem = refs[11:]
+def northing_block(side, to, place, slot_s, weight_s, lines, tile):
+    row = lax.broadcasted_iota(jnp.int32, (8, LANE), 0)
+    lane = lax.broadcasted_iota(jnp.int32, (8, LANE), 1)
+    block = jnp.zeros((8, LANE), F32)
+    for rank in range(CAP):
+        spot = place[(to + 1) * CAP + rank]
+        scene = jnp.maximum(spot, 0)
+        amount = jnp.where(spot >= 0, weight_s[0, scene], 0.0)
+        where = slot_s[0, scene]
+        line = lines[pl.ds(scene, 1), :]
+        for part in range(2):
+            block = jnp.where(row == rank * 2 + part, line[:, part * LANE : (part + 1) * LANE], block)
+            value = jnp.where(where == part * 2 + side, amount, 0.0)
+            block = jnp.where((row == 4) & (lane == rank * 2 + part), value, block)
+        spot = place[(to + (0 if side == 0 else 2)) * CAP + rank]
+        scene = jnp.maximum(spot, 0)
+        amount = jnp.where(spot >= 0, weight_s[0, scene], 0.0)
+        line = lines[pl.ds(scene, 1), :]
+        at = tile - 1 if side == 0 else 0
+        base = 8 + rank * 3
+        for part in range(2):
+            value = jnp.broadcast_to(line[:, part * LANE + at : part * LANE + at + 1], (1, LANE))
+            block = jnp.where((row == 4) & (lane == base + part), value, block)
+        value = jnp.where(slot_s[0, scene] == (2 if side == 0 else 1), amount, 0.0)
+        block = jnp.where((row == 4) & (lane == base + 2), value, block)
+    return block
+
+
+def pack_kernel(groups, count, tile, *refs):
+    owner, slot, weight, ice, obs_h, vel_h, visc_h, fric_h, drive_h, first, second, edge = refs[:12]
+    (
+        owner_s, slot_s, weight_b, weight_v, weight_s, ice_s, obs, vel, visc, fric, drive, to_low, to_high, lines,
+        place, filled, scalar_sem, more_sem, load_sem,
+    ) = refs[12:]
     loads = copy_all([(vel_h, vel), (drive_h, drive), (visc_h, visc), (fric_h, fric), (obs_h, obs)], load_sem)
-    more = copy_all([(ice, ice_s), (owner, owner_v), (slot, slot_v), (weight, weight_v)], more_sem)
+    more = copy_all([(ice, ice_s)], more_sem)
+    scalars = load_scalars(owner, slot, weight, owner_s, slot_s, weight_b, weight_v, weight_s, scalar_sem)
     picked = lax.broadcasted_iota(jnp.int32, (8, LANE), 0)
     across = lax.broadcasted_iota(jnp.int32, (8, LANE), 1)
-    cells_y = visc.shape[1]
-
-    def pick(first, kind):
-        return (across == picked + first).astype(kind)
-
-    wait_all(loads[:4])
-    for index, (at, depth) in enumerate(FIELDS[:-1]):
-        for target, low, first in ((to_low, 0, 0), (to_high, cells_y - LANE, LANE - depth)):
-            lanes = slice(low, low + LANE)
-            if index in (VISC, FRIC):
-                field = (visc if index == VISC else fric)[:, lanes]
-                rows = columns_of(pick(first, F32), field, lax.Precision.HIGHEST)
-            else:
-                field = vel[index, :, lanes] if index in (U, V) else drive[index - DRIVE_U, :, lanes]
-                rows = columns_of(pick(first, jnp.bfloat16), field, None)
+    cells, cells_y = visc.shape
+    scalars[0].wait()
+    fill_places(place, filled, groups, count, lambda scene: owner_s[0, scene])
+
+    def pick(start, kind):
+        return (across == picked + start).astype(kind)
+
+    wait_all(loads[:4] + more)
+    for index, (at, depth) in enumerate(FIELDS):
+        if index == ICE:
+            for target, column in ((to_low, 0), (to_high, ice_s.shape[1] - 1)):
+                target[at : at + 1, :] = ice_line([ice_s[row, column] for row in range(ice_s.shape[0])], (1, cells), tile)
+            for number, row in enumerate((0, ice_s.shape[0] - 1)):
+                edge[number, at : at + 1, :] = ice_line(
+                    [ice_s[row, column] for column in range(ice_s.shape[1])], (1, cells_y), tile
+                )
+            continue
+        field = {VISC: visc, FRIC: fric}.get(index)
+        if field is None:
+            field = vel.at[index] if index in (U, V) else drive.at[index - DRIVE_U]
+        precise = index in (VISC, FRIC)
+        for target, low, start in ((to_low, 0, 0), (to_high, cells_y - LANE, LANE - depth)):
+            rows = columns_of(
+                pick(start, F32 if precise else jnp.bfloat16), field[:, low : low + LANE],
+                lax.Precision.HIGHEST if precise else None,
+            )
             target[at : at + depth, :] = rows[0:depth]
-    wait_all(more)
-    for target, at in ((to_low, 0), (to_high, ice_s.shape[1] - 1)):
-        target[SCENES + count :, :] = jnp.zeros((8, target.shape[1]), F32)
-        for number, values in enumerate((owner_v, slot_v, weight_v)):
-            target[SCENES + count + number : SCENES + count + number + 1, 0:count] = values[...].astype(F32)
-        row = FIELDS[ICE][0]
-        target[row : row + 1, :] = ice_line(
-            [ice_s[number, at] for number in range(ice_s.shape[0])], (1, target.shape[1]), tile
-        )
+        edge[0, at : at + depth, :] = field[0:16, :].astype(F32)[0:depth]
+        edge[1, at : at + depth, :] = field[cells - 16 : cells, :].astype(F32)[16 - depth : 16]
     loads[4].wait()
     both = (across == jnp.where(picked == 0, 0, LANE - 1)).astype(jnp.bfloat16)
     for scene in range(count):
         rows = columns_of(both, obs[scene].reshape(2 * tile, LANE), None)
-        to_low[SCENES + scene : SCENES + scene + 1, :] = rows[0:1]
-        to_high[SCENES + scene : SCENES + scene + 1, :] = rows[1:2]
+        lines[0, scene : scene + 1, :] = rows[0:1]
+        lines[1, scene : scene + 1, :] = rows[1:2]
+    wait_all(scalars[1:])
+    half = groups // 2
+    for side, target in enumerate((to_low, to_high)):
+        for to in range(groups):
+            at = PACK + to % half * 8
+            lanes = slice(to // half * LANE, (to // half + 1) * LANE)
+            target[at : at + 8, lanes] = northing_block(side, to, place, slot_s, weight_s, lines.at[side], tile)
+    even = lax.rem(lax.axis_index("gy"), 2) == 0
+    first[...] = jnp.where(even, to_high[...], to_low[...])
+    second[...] = jnp.where(even, to_low[...], to_high[...])
 
 
 def side_tiles(right, left, turned):
     turned[...] = jnp.zeros_like(turned)
-    turned[0:PACK, :] = right[0:PACK, :]
-    turned[PACK : 2 * PACK, :] = left[0:PACK, :]
+    turned[0:PACK, :] = right
+    turned[PACK : 2 * PACK, :] = left
     return jnp.transpose(turned[...])
 
 
@@ -238,84 +289,35 @@
         pack[first : first + count, lanes] += more[count : 2 * count]
 
 
-def widen_kernel(groups, count, tile, early, late, *refs):
-    ice, vel, visc, fric, drive, right, left = refs[:7]
-    pays = dict(zip(late, refs[7 + len(late) :]))
-    refs = refs[7 + 2 * len(late) :]
+def widen_kernel(groups, tile, early, late, *refs):
+    first, second, edge = refs[:3]
+    pays = dict(zip(late, refs[3 + len(late) :]))
+    refs = refs[3 + 2 * len(late) :]
     apart = dict(zip(early, refs))
-    ice_s, notes, first_b, last_b, first_f, last_f, turned, to_low, to_high, place, filled, sems = refs[len(early) :]
-    cells = visc.shape[0]
-    cells_y = visc.shape[1]
+    turned, to_low, to_high = refs[len(early) :]
+    cells_y = edge.shape[2]
     blocks = tile // PACK
     me = lax.axis_index("gx")
-    tail = pl.ds(SCENES + count, 8)
-    loads = copy_all(
-        [
-            (right.at[tail], notes.at[0]), (left.at[tail], notes.at[1]), (ice, ice_s),
-            (vel.at[:, 0:16], first_b.at[0:2]), (drive.at[:, 0:16], first_b.at[2:4]),
-            (vel.at[:, cells - 16 : cells], last_b.at[0:2]), (drive.at[:, cells - 16 : cells], last_b.at[2:4]),
-            (visc.at[0:8], first_f.at[0]), (fric.at[0:8], first_f.at[1]),
-            (visc.at[cells - 8 : cells], last_f.at[0]), (fric.at[cells - 8 : cells], last_f.at[1]),
-        ],
-        sems,
-    )
-    upright = side_tiles(right, left, turned)
-    wait_all(loads)
+    half = groups // 2
+    for step in late + early:
+        to = partner(me, step)
+        here = pl.ds(pl.multiple_of(PACK + lax.rem(to, half) * 8, 8), 8)
+        sides = both_sides(first[here, :], second[here, :])
+        block = jnp.concatenate([jnp.where(to < half, side[:, 0:LANE], side[:, LANE:]) for side in sides], axis=0)
+        if step in early:
+            apart[step][0] = block.astype(jnp.bfloat16)
+        else:
+            pays[step][CAP * 2 * blocks + 1] = block.astype(jnp.bfloat16)
+    upright = side_tiles(*both_sides(first[0:PACK, :], second[0:PACK, :]), turned)
+    cells = upright.shape[0]
+    to_low[:, 0:cells_y] = edge[0]
+    to_high[:, 0:cells_y] = edge[1]
     for index, (at, depth) in enumerate(FIELDS):
-        if index == ICE:
-            first, last = (
-                ice_line([ice_s[number, column] for column in range(ice_s.shape[1])], (1, cells_y), tile)
-                for number in (0, ice_s.shape[0] - 1)
-            )
-        elif index in (VISC, FRIC):
-            first, last = first_f[index - VISC], last_f[index - VISC]
-        else:
-            number = index if index in (U, V) else index - DRIVE_U + 2
-            first, last = first_b[number].astype(F32), last_b[number].astype(F32)
-        to_low[at : at + depth, 0:cells_y] = first[0:depth]
-        to_high[at : at + depth, 0:cells_y] = last[last.shape[0] - depth :]
         to_low[at : at + depth, cells_y:] = side_tile(upright[0:8], index)[0:depth]
         to_high[at : at + depth, cells_y:] = side_tile(upright[cells - 8 :], index)[8 - depth : 8]
     base = CAP * 2 * blocks + 2
     for step in halo_steps(groups):
         write_halo(pays[step], base, jnp.where(partner(me, step) > me, to_high[...], to_low[...]))
-    packs = (right, left)
-    for side in range(2):
-        fill_places(place.at[side], filled, groups, count, lambda scene: notes[side, 0, scene].astype(jnp.int32))
-    row = lax.broadcasted_iota(jnp.int32, (PACK, LANE), 0)
-    lane = lax.broadcasted_iota(jnp.int32, (PACK, LANE), 1)
-    for step in range(groups):
-        to = partner(me, step)
-        block = jnp.zeros((PACK, LANE), F32)
-        for side in range(2):
-            for rank in range(CAP):
-                spot = place[side, (to + 1) * CAP + rank]
-                scene = jnp.maximum(spot, 0)
-                amount = jnp.where(spot >= 0, notes[side, 2, scene], 0.0)
-                where = notes[side, 1, scene].astype(jnp.int32)
-                line = packs[side][pl.ds(SCENES + scene, 1), :]
-                for part in range(2):
-                    block = jnp.where(
-                        row == (side * CAP + rank) * 2 + part, line[:, part * LANE : (part + 1) * LANE], block
-                    )
-                    value = jnp.where(where == part * 2 + side, amount, 0.0)
-                    block = jnp.where((row == 8) & (lane == (side * CAP + rank) * 2 + part), value, block)
-                spot = place[side, (to + (0 if side == 0 else 2)) * CAP + rank]
-                scene = jnp.maximum(spot, 0)
-                amount = jnp.where(spot >= 0, notes[side, 2, scene], 0.0)
-                where = notes[side, 1, scene].astype(jnp.int32)
-                line = packs[side][pl.ds(SCENES + scene, 1), :]
-                at = tile - 1 if side == 0 else 0
-                base = 8 + side * 6 + rank * 3
-                for part in range(2):
-                    value = jnp.broadcast_to(line[:, part * LANE + at : part * LANE + at + 1], (1, LANE))
-                    block = jnp.where((row == 8) & (lane == base + part), value, block)
-                value = jnp.where(where == (2 if side == 0 else 1), amount, 0.0)
-                block = jnp.where((row == 8) & (lane == base + 2), value, block)
-        if step in early:
-            apart[step][0] = block.astype(jnp.bfloat16)
-        else:
-            pays[step][CAP * 2 * blocks + 1] = block.astype(jnp.bfloat16)
 
 
 def stress_block(u, v, visc, low, rows, wide):
@@ -338,27 +340,71 @@
     return push_u, push_v
 
 
-def sweep_kernel(groups, tile, ice, vel, visc, fric, drive, right, left, *refs):
-    steps = halo_steps(groups)
-    pays = dict(zip(steps, refs))
-    refs = refs[len(steps) :]
-    second, ease, lead, trail, wide_visc, wide_ice = refs[:6]
-    (
-        u, v, wide_fric, drive_u, drive_v, next_u, next_v, relax_u, relax_v, sxx, syy, sxy, turned,
-        low_pack, high_pack, ice_s, sems,
-    ) = refs[6:]
+def relaxation(fields, work, wide, cells_y, spans, outs, shift, own_of):
+    u, v, visc, fric, drive_u, drive_v, ice = fields
+    next_u, next_v, relax_u, relax_v, sxx, syy, sxy = work
+    second, ease, lead, trail = outs
+    for low in spans[0]:
+        here = pl.ds(low, 8)
+        nu, drag = visc[here, :], fric[here, :]
+        nu_x = visc[pl.ds(low - 1, 8), :]
+        nu_y = pltpu.roll(nu, 1, 1)
+        inside = drag > 0.0
+        for out, diag in ((relax_u, 5.0 * nu + 4.0 * nu_x + nu_y), (relax_v, 5.0 * nu + nu_x + 4.0 * nu_y)):
+            out[here, :] = jnp.where(inside, 1.0 / jnp.where(inside, diag + drag, 1.0), 0.0)
+    for low in spans[1]:
+        here = pl.ds(low, 8)
+        sxx[here, :], syy[here, :], sxy[here, :] = stress_block(u, v, visc, low, 8, wide)
+    for low in spans[2]:
+        here, there = pl.ds(low, 8), pl.ds(low + shift, 8)
+        pushes = image_block(sxx, syy, sxy, low, 8)
+        for part, (push, speed, force, relax, then) in enumerate(
+            zip(pushes, (u, v), (drive_u, drive_v), (relax_u, relax_v), (next_u, next_v))
+        ):
+            now, soft = speed[here, :], relax[here, :]
+            move = soft * (force[here, :] - push - fric[here, :] * now)
+            then[here, :] = now + OMEGA * move
+            if low in spans[4]:
+                slack = OMEGA * soft
+                ease[part, there, :] = slack
+                if own_of(low) is not None:
+                    factor = -ice[here, 0:cells_y] * (slack * (move + now))[:, 0:cells_y]
+                    lead[part, pl.ds(own_of(low), 8), :] = factor
+    for low in spans[3]:
+        here = pl.ds(low, 8)
+        sxx[here, :], syy[here, :], sxy[here, :] = stress_block(next_u, next_v, visc, low, 8, wide)
+    for low in spans[4]:
+        here, there = pl.ds(low, 8), pl.ds(low + shift, 8)
+        pushes = image_block(sxx, syy, sxy, low, 8)
+        for part, (push, speed, force, relax) in enumerate(
+            zip(pushes, (next_u, next_v), (drive_u, drive_v), (relax_u, relax_v))
+        ):
+            now = speed[here, :]
+            move = relax[here, :] * (force[here, :] - push - fric[here, :] * now)
+            second[part, there, :] = ice[here, :] * (now + OMEGA * move)
+            if own_of(low) is not None:
+                mine = pl.ds(own_of(low), 8)
+                trail[part, mine, :] = (
+                    -ice[here, 0:cells_y] * (move + now)[:, 0:cells_y] - fric[here, 0:cells_y] * lead[part, mine, :]
+                )
+
+
+STRIP = 32
+
+
+def sweep_kernel(tile, ice, vel, visc, fric, drive, first, then, *refs):
+    second, ease, lead, trail, wide_visc, wide_ice, strips = refs[:7]
+    u, v, wide_fric, drive_u, drive_v = refs[7:12]
+    work = refs[12:19]
+    turned, ice_s, sems = refs[19:]
     cells, cells_y = visc.shape
     rows, wide = wide_visc.shape
     loads = copy_all([(ice, ice_s)], sems)
-    upright = side_tiles(right, left, turned)
-    base = CAP * 2 * (tile // PACK) + 2
-    me = lax.axis_index("gx")
-    read_halo(pays, base, low_pack, me, me - 1)
-    read_halo(pays, base, high_pack, me, me + 1)
+    upright = side_tiles(*both_sides(first[0:PACK, :], then[0:PACK, :]), turned)
     wait_all(loads)
     own_rows = slice(PAD, PAD + cells)
-    for index, field in enumerate((u, v, wide_visc, wide_fric, drive_u, drive_v, wide_ice)):
-        at, depth = FIELDS[index]
+    fields = (u, v, wide_visc, wide_fric, drive_u, drive_v, wide_ice)
+    for index, field in enumerate(fields):
         field[0:PAD, :] = jnp.zeros((PAD, wide), F32)
         field[PAD + cells :, :] = jnp.zeros((PAD, wide), F32)
         if index == ICE:
@@ -372,53 +418,47 @@
             source = vel if index in (U, V) else drive
             field[own_rows, 0:cells_y] = source[index % DRIVE_U].astype(F32)
         field[own_rows, cells_y:wide] = side_tile(upright, index)
-        field[PAD - depth : PAD, :] = low_pack[at : at + depth, :]
-        field[PAD + cells : PAD + cells + depth, :] = high_pack[at : at + depth, :]
+        strips[index, 0] = field[8 : 8 + STRIP, :]
+        strips[index, 1] = field[rows - 8 - STRIP : rows - 8, :]
     blocks = range(8, rows - 8, 8)
-    own = range(PAD, rows - PAD, 8)
-    for low in blocks:
-        here = pl.ds(low, 8)
-        nu, drag = wide_visc[here, :], wide_fric[here, :]
-        nu_x = wide_visc[pl.ds(low - 1, 8), :]
-        nu_y = pltpu.roll(nu, 1, 1)
-        inside = drag > 0.0
-        for out, diag in ((relax_u, 5.0 * nu + 4.0 * nu_x + nu_y), (relax_v, 5.0 * nu + nu_x + 4.0 * nu_y)):
-            out[here, :] = jnp.where(inside, 1.0 / jnp.where(inside, diag + drag, 1.0), 0.0)
-    for low in blocks:
-        here = pl.ds(low, 8)
-        sxx[here, :], syy[here, :], sxy[here, :] = stress_block(u, v, wide_visc, low, 8, wide)
-    for low in blocks:
-        here = pl.ds(low, 8)
-        pushes = image_block(sxx, syy, sxy, low, 8)
-        for part, (push, speed, force, relax, after) in enumerate(
-            zip(pushes, (u, v), (drive_u, drive_v), (relax_u, relax_v), (next_u, next_v))
-        ):
-            now, soft = speed[here, :], relax[here, :]
-            move = soft * (force[here, :] - push - wide_fric[here, :] * now)
-            after[here, :] = now + OMEGA * move
-            slack = OMEGA * soft
-            ease[part, here, :] = slack
-            if low in own:
-                factor = -wide_ice[here, 0:cells_y] * (slack * (move + now))[:, 0:cells_y]
-                lead[part, pl.ds(low - PAD, 8), :] = factor
-    for low in blocks:
-        here = pl.ds(low, 8)
-        sxx[here, :], syy[here, :], sxy[here, :] = stress_block(next_u, next_v, wide_visc, low, 8, wide)
-    for low in blocks:
-        here = pl.ds(low, 8)
-        pushes = image_block(sxx, syy, sxy, low, 8)
-        for part, (push, speed, force, relax) in enumerate(
-            zip(pushes, (next_u, next_v), (drive_u, drive_v), (relax_u, relax_v))
-        ):
-            now = speed[here, :]
-            move = relax[here, :] * (force[here, :] - push - wide_fric[here, :] * now)
-            second[part, here, :] = wide_ice[here, :] * (now + OMEGA * move)
-            if low in own:
-                mine = pl.ds(low - PAD, 8)
-                trail[part, mine, :] = (
-                    -wide_ice[here, 0:cells_y] * (move + now)[:, 0:cells_y]
-                    - wide_fric[here, 0:cells_y] * lead[part, mine, :]
-                )
+    relaxation(
+        fields, work, wide, cells_y, [blocks] * 5, (second, ease, lead, trail), 0,
+        lambda low: low - PAD if PAD <= low < PAD + cells else None,
+    )
+
+
+def trim_kernel(groups, tile, *refs):
+    steps = halo_steps(groups)
+    pays = dict(zip(steps, refs))
+    strips = refs[len(steps)]
+    second, ease, lead, trail, visc, ice = refs[len(steps) + 7 : len(steps) + 13]
+    refs = refs[len(steps) + 13 :]
+    fields, work, pack = refs[:7], refs[7:14], refs[14]
+    rows, wide = visc.shape
+    cells_y = wide - LANE
+    cells = rows - 2 * PAD
+    base = CAP * 2 * (tile // PACK) + 2
+    me = lax.axis_index("gx")
+    spans = (
+        [(8, 16, 24), (8, 16, 24), (8, 16, 24), (8, 16), (8, 16)],
+        [(16, 24, 32), (8, 16, 24, 32), (16, 24, 32), (16, 24, 32), (24, 32)],
+    )
+    for strip in range(2):
+        read_halo(pays, base, pack, me, me - 1 if strip == 0 else me + 1)
+        shift = 0 if strip == 0 else rows - 16 - STRIP
+        edge = PAD if strip == 0 else PAD + cells - shift
+        for index, field in enumerate(fields):
+            at, depth = FIELDS[index]
+            field[8 : 8 + STRIP, :] = strips[index, strip]
+            target = slice(edge - depth, edge) if strip == 0 else slice(edge, edge + depth)
+            field[target, :] = pack[at : at + depth, :]
+            if index in (VISC, ICE):
+                (visc if index == VISC else ice)[target.start + shift : target.stop + shift, :] = pack[at : at + depth, :]
+        own = {0: (16, 0), 1: (24, cells - 8)}[strip]
+        relaxation(
+            fields, work, wide, cells_y, spans[strip], (second, ease, lead, trail), shift,
+            lambda low, own=own: own[1] if low == own[0] else None,
+        )
 
 
 def final_kernel(groups, tile, early, *refs):
@@ -442,8 +482,8 @@
     def raw(source, number):
         return source[number * groups : (number + 1) * groups, :]
 
-    def spread(source, number):
-        return jnp.broadcast_to(raw(source, 8)[:, number : number + 1], (groups, LANE))
+    def spread(source, number, row=8):
+        return jnp.broadcast_to(raw(source, row)[:, number : number + 1], (groups, LANE))
 
     def gathered(value):
         return jnp.sum(value, axis=0, keepdims=True)
@@ -470,15 +510,15 @@
                 lift[part][at : at + 1, lanes] = ease[part, at : at + 1, lanes] * gap
         lines = [[None] * 2 for _ in range(3)]
         for column in range(2):
-            weights = [spread(rows_y, (side * CAP + rank) * 2 + column) for rank in range(CAP)]
+            weights = [spread(rows_y, rank * 2 + column, side * 8 + 4) for rank in range(CAP)]
             lines[2][column] = gathered(sum(weights))
             for part in range(2):
                 lines[part][column] = gathered(
-                    sum(weights[rank] * raw(rows_y, (side * CAP + rank) * 2 + part) for rank in range(CAP))
+                    sum(weights[rank] * raw(rows_y, side * 8 + rank * 2 + part) for rank in range(CAP))
                 )
-        weights = [spread(rows_y, 8 + side * 6 + rank * 3 + 2) for rank in range(CAP)]
+        weights = [spread(rows_y, 8 + rank * 3 + 2, side * 8 + 4) for rank in range(CAP)]
         corners = [
-            gathered(sum(weights[rank] * spread(rows_y, 8 + side * 6 + rank * 3 + part) for rank in range(CAP)))
+            gathered(sum(weights[rank] * spread(rows_y, 8 + rank * 3 + part, side * 8 + 4) for rank in range(CAP)))
             for part in range(2)
         ] + [gathered(sum(weights))]
         lane = lax.broadcasted_iota(jnp.int32, (1, turned.shape[1]), 1)
@@ -568,7 +608,7 @@
 
     bf16, i32 = jnp.bfloat16, jnp.int32
     deep = CAP * 2 * blocks
-    tall = SCENES + count + 8
+    tall = PACK + groups // 2 * 8
     half = groups // 2
     early = (half, half + 1)
     late = tuple(step for step in range(groups) if step not in early)
@@ -582,6 +622,10 @@
         pairs = [(me, partner(me, step)) for me in range(groups)]
         return lax.ppermute(after(value, *others) if others else value, "gx", pairs)
 
+    scalars = [
+        pltpu.SMEM((1, count), i32), pltpu.SMEM((1, count), i32), short(1, count), full(1, count),
+        pltpu.SMEM((1, count), F32),
+    ]
     places = [pltpu.SMEM(((groups + 2) * CAP,), i32), pltpu.SMEM((groups,), i32)]
     pays = pl.pallas_call(
         functools.partial(gather_kernel, groups, count, tile),
@@ -589,8 +633,7 @@
         in_specs=[HBM] * 4,
         out_specs=[VMEM] * groups,
         scratch_shapes=[
-            pltpu.SMEM((1, count), i32), pltpu.SMEM((1, count), i32), short(1, count), full(1, count),
-            pltpu.SMEM((1, count), F32), short(4, count, PACK, LANE), *places, dma((3,)), dma((4,)),
+            *scalars, short(4, count, PACK, LANE), *places, dma((3,)), dma((4,)),
             dma((groups * CAP,)),
         ],
         compiler_params=limit,
@@ -599,54 +642,59 @@
     got = [pays[0]] * groups
     for step in early:
         got[step] = move(step, pays[step])
-    y_low, y_high = pl.pallas_call(
-        functools.partial(pack_kernel, count, tile),
-        out_shape=[pltpu.VMEM((tall, cells_x), F32)] * 2,
+    *north, edge = pl.pallas_call(
+        functools.partial(pack_kernel, groups, count, tile),
+        out_shape=[pltpu.VMEM((tall, cells_x), F32)] * 2 + [pltpu.VMEM((2, PACK, cells_y), F32)],
         in_specs=[HBM] * 9,
-        out_specs=[VMEM] * 2,
-        scratch_shapes=[
-            pltpu.SMEM(ice_mask.shape, i32), pltpu.VMEM((1, count), i32), pltpu.VMEM((1, count), i32), short(1, count),
-            short(*obs.shape), short(*vel0.shape), full(*visc.shape), full(*fric.shape), short(*drive.shape),
-            dma((4,)), dma((5,)),
+        out_specs=[VMEM] * 3,
+        scratch_shapes=scalars + [
+            pltpu.SMEM(ice_mask.shape, i32), short(*obs.shape), short(*vel0.shape), full(*visc.shape),
+            full(*fric.shape), short(*drive.shape), full(tall, cells_x), full(tall, cells_x), full(2, count, cells_x),
+            *places, dma((3,)), dma((1,)), dma((5,)),
         ],
         compiler_params=limit,
         name="pack",
     )(*in_place(after(owner, pays[half]), slot, weight, ice_mask, obs, vel0, visc, fric, drive))
-    right = from_behind(y_low, "gy", -1)
-    left = from_behind(y_high, "gy", 1)
+    first, second = swap(*north)
     outs = pl.pallas_call(
-        functools.partial(widen_kernel, groups, count, tile, early, late),
+        functools.partial(widen_kernel, groups, tile, early, late),
         out_shape=[pay(step) for step in late] + [pltpu.VMEM((1, PACK, LANE), bf16)] * len(early),
-        in_specs=[HBM] * 5 + [VMEM] * (2 + len(late)),
+        in_specs=[VMEM] * (3 + len(late)),
         out_specs=[VMEM] * groups,
-        input_output_aliases={7 + number: number for number in range(len(late))},
-        scratch_shapes=[
-            pltpu.SMEM(ice_mask.shape, i32), pltpu.SMEM((2, 8, cells_x), F32), short(4, 16, cells_y),
-            short(4, 16, cells_y), full(2, 8, cells_y), full(2, 8, cells_y), full(LANE, cells_x), full(PACK, wide),
-            full(PACK, wide), pltpu.SMEM((2, (groups + 2) * CAP), i32), pltpu.SMEM((groups,), i32), dma((11,)),
-        ],
+        input_output_aliases={3 + number: number for number in range(len(late))},
+        scratch_shapes=[full(LANE, cells_x), full(PACK, wide), full(PACK, wide)],
         compiler_params=limit,
         name="widen",
-    )(*in_place(ice_mask, vel0, visc, fric, drive), after(right, got[half]), left, *(pays[step] for step in late))
+    )(first, second, edge, *(pays[step] for step in late))
     ready = dict(zip(late, outs))
     got[0] = ready[0]
-    order = [groups - 1, 1, *range(half + 2, groups - 1), half - 1, *(step for step in range(2, half - 1))]
-    waits = {half + 2: half + 1}
+    order = [groups - 1, 1, *range(half + 2, groups - 1), half - 1, *range(2, half - 1)]
+    waits = {half + 2: half, 2: half + 1}
     for step in order:
         got[step] = move(step, ready[step], *([got[waits[step]]] if step in waits else []))
-    apart = [
-        move(step, value, got[wait]) for step, value, wait in zip(early, outs[len(late) :], (1, half - 1))
-    ]
-    base = pl.pallas_call(
-        functools.partial(sweep_kernel, groups, tile),
-        out_shape=[shape(2, rows, wide)] * 2 + [shape(2, cells_x, cells_y)] * 2 + [shape(rows, wide)] * 2,
-        in_specs=[HBM] + [VMEM] * (6 + len(halo_steps(groups))),
-        out_specs=[VMEM] * 6,
-        scratch_shapes=[full(rows, wide)] * 12
-        + [full(LANE, cells_x), full(PACK, wide), full(PACK, wide), pltpu.SMEM(ice_mask.shape, i32), dma((1,))],
+    strip = shape(len(FIELDS), 2, STRIP, wide)
+    base_shapes = [shape(2, rows, wide)] * 2 + [shape(2, cells_x, cells_y)] * 2 + [shape(rows, wide)] * 2
+    *base, strips = pl.pallas_call(
+        functools.partial(sweep_kernel, tile),
+        out_shape=base_shapes + [strip],
+        in_specs=[HBM] + [VMEM] * 6,
+        out_specs=[VMEM] * 7,
+        scratch_shapes=[full(rows, wide)] * 12 + [full(LANE, cells_x), pltpu.SMEM(ice_mask.shape, i32), dma((1,))],
         compiler_params=limit,
         name="sweep",
-    )(ice_mask, vel0, visc, fric, drive, right, left, *(got[step] for step in halo_steps(groups)))
+    )(ice_mask, vel0, visc, fric, drive, after(first, got[half + 1]), second)
+    apart = [move(step, value, strips) for step, value in zip(early, outs[len(late) :])]
+    near = [got[step] for step in halo_steps(groups)]
+    base = pl.pallas_call(
+        functools.partial(trim_kernel, groups, tile),
+        out_shape=base_shapes,
+        in_specs=[VMEM] * (len(near) + 7),
+        out_specs=[VMEM] * 6,
+        input_output_aliases={len(near) + 1 + number: number for number in range(6)},
+        scratch_shapes=[full(STRIP + 16, wide)] * 14 + [full(PACK, wide)],
+        compiler_params=limit,
+        name="trim",
+    )(*near, strips, *base)
     return pl.pallas_call(
         functools.partial(final_kernel, groups, tile, early),
         out_shape=shape(cells_x, cells_y),

time: 42.8 us -> 38.3 us (0.89)
  starting transfers between devices: 20.7 us -> 18.1 us
  waiting for transfers between devices: 7.93 us -> 6.69 us
  Pallas kernels: 13.8 us -> 12.9 us
    ppermute x2, starting transfers between devices: 4.32 us -> 0.73 us  [swap(): return (lax.ppermute(even, 'gy', near), lax.ppermute(odd, 'gy', far))]
    ppermute x9, waiting for transfers between devices: 7.92 us -> 6.14 us  [move(): return lax.ppermute(after(value, *others) if others else value, 'gx', pairs)]
    ppermute x9, starting transfers between devices: 16.3 us -> 17.4 us  [move(): return lax.ppermute(after(value, *others) if others else value, 'gx', pairs)]
    pallas_call x3 -> x4, Pallas kernels: 8.26 us -> 7.41 us  [the longest x1 3.82 us: body(): pl.pallas_call(functools.partial(sweep_kernel, tile), out_shape=base_shap...]
    ppermute x2, waiting for transfers between devices: 0.01 us -> 0.55 us  [swap(): return (lax.ppermute(even, 'gy', near), lax.ppermute(odd, 'gy', far))]
  transfers between devices with their start and end apart: 11 -> 11, of which waited for: 5 -> 4; matrix products, arithmetic and copies ran while one was open for 0% -> 0% of each run, Pallas kernels for 19% -> 20%
where the time goes in v5:
time: 38.3 us; the launch traced here: 37.9 us
  starting transfers between devices  18.1 us (47%)
  Pallas kernels  12.9 us (34%)
  waiting for transfers between devices  6.69 us (17%)
    ppermute x9, starting transfers between devices, move(): return lax.ppermute(after(value, *others) if others else value, 'gx', pairs)  17.4 us
    ppermute x9, waiting for transfers between devices, move(): return lax.ppermute(after(value, *others) if others else value, 'gx', pairs)  6.14 us
    pallas_call x1, Pallas kernels, body(): pl.pallas_call(functools.partial(sweep_kernel, tile), out_shape=base_shap...  3.82 us
    pallas_call x1, Pallas kernels, body(): pl.pallas_call(functools.partial(final_kernel, groups, tile, early), out_...  3.19 us
    pallas_call x1, Pallas kernels, body(): pl.pallas_call(functools.partial(pack_kernel, groups, count, tile), out_s...  2.82 us
    pallas_call x1, Pallas kernels, body(): pl.pallas_call(functools.partial(gather_kernel, groups, count, tile), out...  2.34 us
  transfers between devices with their start and end apart: 11, of which 4 were waited for; matrix products, arithmetic and copies ran while one was open for 0% of the time, Pallas kernels for 20%

profile of v5, /device:TPU:0, one launch (start us, length us, event | category | flops | bytes accessed | tf_op | source)
XLA Modules:
  0.0 37.9 jit_solution(4509240165096675985)
XLA Ops:
  0.0 2.3 %gather.1 = (bf16[34,16,128]{2,1,0:T(8,128)(2,1)S(1)}, bf16[40,16,128]{2,1,0:T(8,128)(2,1)S(1)}, bf16[34,16,128]{2,1,0:T(8,128)(2,1)S(1)}, bf16[40,16,128]{2,1,0...) custom-call(s32[1,16]{1,0:T(1,128)} %bitcast.4, ...), custom_call_target="tpu_custom_call" | custom-call | tf_op jit(solution)/shard_map/gather/pallas_call | solution.py:630
  2.3 5.0 %collective-permute-start.3 = (bf16[33,16,128]{2,1,0:T(8,128)(2,1)S(1)}, bf16[33,16,128]{2,1,0:T(8,128)(2,1)S(1)}, u32[]{:S(2)}, u32[]{:S(2)}) collective-permute-start(bf16[33,16,128]{2,1,0:T(8,128)(2,1)S(1)} %get-tuple-element.57), channel_id=1, source_target_pairs={{0,20},{4,16},{8,28},{12,24},{16,4},{20,0},{24,12},{28,8},{1,21},{... | collective-permute-start | bytes 405512 | tf_op jit(solution)/shard_map/ppermute | solution.py:623
  7.4 0.3 collective-permute-start.6
  7.7 2.8 %pack.1 = (f32[48,256]{1,0:T(8,128)S(1)}, f32[48,256]{1,0:T(8,128)S(1)}, f32[2,16,256]{2,1,0:T(8,128)S(1)}) custom-call(s32[1,16]{1,0:T(1,128)} %bitcast.5, s32[1,16]{1,0:T(1,128)} %refs_1_.3, bf16[1,16]{1,0:T(2,128)(2,1)} %refs_2_.3, s32[2,2]{1,0:T(2,128)} %ice.1, bf16[16,16,16,128]{3,2,1,0:T(8,128)(2,1)} %bitcast.3, bf16[2,256,256]{2,1,0:T(8,128)(2,1)} %vel.1, ...), custom_call_target="tpu_custom_call" | custom-call | tf_op jit(solution)/shard_map/pack/pallas_call | solution.py:645
  10.5 0.1 collective-permute-start
  10.6 0.7 %collective-permute-start.1 = (f32[48,256]{1,0:T(8,128)S(1)}, f32[48,256]{1,0:T(8,128)S(1)}, u32[]{:S(2)}, u32[]{:S(2)}) collective-permute-start(f32[48,256]{1,0:T(8,128)S(1)} %get-tuple-element.46), channel_id=1, source_target_pairs={{1,2},{2,1},{5,6},{6,5},{9,10},{10,9},{13,14},{14,13},{17,18},{18,... | collective-permute-start | bytes 147464 | tf_op jit(solution)/shard_map/ppermute | solution.py:43
  11.3 0.5 %collective-permute-done.refs_0_.first = f32[48,256]{1,0:T(8,128)S(1)} collective-permute-done((f32[48,256]{1,0:T(8,128)S(1)}, f32[48,256]{1,0:T(8,128)S(1)}, u32[]{:S(2)}, u32[]{:S(2)}) %collective-permute-start) | collective-permute-done | bytes 49184 | tf_op jit(solution)/shard_map/ppermute | solution.py:43
  11.8 0.0 collective-permute-done.1.refs_1_.then
  11.8 0.0 copy-start
  11.8 0.0 copy-start.1
  11.8 0.0 copy-start.2
  11.9 0.0 copy-start.3
  11.9 0.2 widen.1
  12.1 0.4 collective-permute-start.2
  12.5 2.7 %collective-permute-start.5 = (bf16[40,16,128]{2,1,0:T(8,128)(2,1)S(1)}, bf16[40,16,128]{2,1,0:T(8,128)(2,1)S(1)}, u32[]{:S(2)}, u32[]{:S(2)}) collective-permute-start(bf16[40,16,128]{2,1,0:T(8,128)(2,1)S(1)} %get-tuple-element.59), channel_id=1, source_target_pairs={{0,12},{4,8},{8,4},{12,0},{16,28},{20,24},{24,20},{28,16},{1,13},{... | collective-permute-start | bytes 491528 | tf_op jit(solution)/shard_map/ppermute | solution.py:623
  15.2 2.4 %collective-permute-start.8 = (bf16[40,16,128]{2,1,0:T(8,128)(2,1)S(1)}, bf16[40,16,128]{2,1,0:T(8,128)(2,1)S(1)}, u32[]{:S(2)}, u32[]{:S(2)}) collective-permute-start(bf16[40,16,128]{2,1,0:T(8,128)(2,1)S(1)} %get-tuple-element.62), channel_id=1, source_target_pairs={{0,28},{4,24},{8,20},{12,16},{16,12},{20,8},{24,4},{28,0},{1,29},{... | collective-permute-start | bytes 491528 | tf_op jit(solution)/shard_map/ppermute | solution.py:623
  17.6 0.0 collective-permute-done.3.refs_5_
  17.7 0.0 copy-start.4
  17.7 2.1 %collective-permute-done.6.refs_4_ = bf16[33,16,128]{2,1,0:T(8,128)(2,1)S(1)} collective-permute-done((bf16[33,16,128]{2,1,0:T(8,128)(2,1)S(1)}, bf16[33,16,128]{2,1,0:T(8,128)(2,1)S(1)}, u32[]{:S(2)}, u32[]{:S(2)}) %collective-permute-start.6) | collective-permute-done | bytes 135200 | tf_op jit(solution)/shard_map/ppermute | solution.py:623
  19.8 5.0 %collective-permute-start.7 = (bf16[34,16,128]{2,1,0:T(8,128)(2,1)S(1)}, bf16[34,16,128]{2,1,0:T(8,128)(2,1)S(1)}, u32[]{:S(2)}, u32[]{:S(2)}) collective-permute-start(bf16[34,16,128]{2,1,0:T(8,128)(2,1)S(1)} %get-tuple-element.61), channel_id=1, source_target_pairs={{0,24},{4,28},{8,16},{12,20},{16,8},{20,12},{24,0},{28,4},{1,25},{... | collective-permute-start | bytes 417800 | tf_op jit(solution)/shard_map/ppermute | solution.py:623
  24.8 0.0 collective-permute-start.4
  24.8 0.0 copy-done
  24.8 0.0 copy-done.1
  24.8 0.0 copy-done.2
  24.8 0.0 copy-done.3
  24.8 0.0 copy-done.4
  24.8 3.8 %sweep.1 = (f32[2,288,384]{2,1,0:T(8,128)S(1)}, f32[2,288,384]{2,1,0:T(8,128)S(1)}, f32[2,256,256]{2,1,0:T(8,128)S(1)}, f32[2,256,256]{2,1,0:T(8,128)S(1)}, f32[...) custom-call(s32[2,2]{1,0:T(2,128)S(1)} %copy-done.4, bf16[2,256,256]{2,1,0:T(8,128)(2,1)S(1)} %copy-done, ...), custom_call_target="tpu_custom_call" | custom-call | tf_op jit(solution)/shard_map/sweep/pallas_call | solution.py:677
  28.6 0.0 collective-permute-done.2.refs_0_.refs_1_
  28.6 0.6 %collective-permute-start.9 = (bf16[1,16,128]{2,1,0:T(8,128)(2,1)S(1)}, bf16[1,16,128]{2,1,0:T(8,128)(2,1)S(1)}, u32[]{:S(2)}, u32[]{:S(2)}) collective-permute-start(bf16[1,16,128]{2,1,0:T(8,128)(2,1)S(1)} %get-tuple-element.66), channel_id=1, source_target_pairs={{0,16},{4,20},{8,24},{12,28},{16,0},{20,4},{24,8},{28,12},{1,17},{... | collective-permute-start | bytes 12296 | tf_op jit(solution)/shard_map/ppermute | solution.py:623
  29.3 0.0 collective-permute-done.5.refs_1_.refs_3_
  29.3 0.9 %collective-permute-start.10 = (bf16[1,16,128]{2,1,0:T(8,128)(2,1)S(1)}, bf16[1,16,128]{2,1,0:T(8,128)(2,1)S(1)}, u32[]{:S(2)}, u32[]{:S(2)}) collective-permute-start(bf16[1,16,128]{2,1,0:T(8,128)(2,1)S(1)} %get-tuple-element.68), channel_id=1, source_target_pairs={{0,20},{4,16},{8,28},{12,24},{16,4},{20,0},{24,12},{28,8},{1,21},{... | collective-permute-start | bytes 12296 | tf_op jit(solution)/shard_map/ppermute | solution.py:623
  30.1 0.0 collective-permute-done.8.refs_2_.refs_7_
  30.1 0.5 %trim.1 = (f32[2,288,384]{2,1,0:T(8,128)S(1)}, f32[2,288,384]{2,1,0:T(8,128)S(1)}, f32[2,256,256]{2,1,0:T(8,128)S(1)}, f32[2,256,256]{2,1,0:T(8,128)S(1)}, f32[2...) custom-call(bf16[40,16,128]{2,1,0:T(8,128)(2,1)S(1)} %collective-per, ...), custom_call_target="tpu_custom_call", output_to_operand_aliasing={{0}: (4, {}), {1}: (5, {}), {2}: (6, {}), {3}: (7, {}), {4}... | custom-call | tf_op jit(solution)/shard_map/trim/pallas_call | solution.py:688
  30.7 2.5 %collective-permute-done.9.refs_8_ = bf16[1,16,128]{2,1,0:T(8,128)(2,1)S(1)} collective-permute-done((bf16[1,16,128]{2,1,0:T(8,128)(2,1)S(1)}, bf16[1,16,128]{2,1,0:T(8,128)(2,1)S(1)}, u32[]{:S(2)}, u32[]{:S(2)}) %collective-permute-start.9) | collective-permute-done | bytes 4128 | tf_op jit(solution)/shard_map/ppermute | solution.py:623
  33.2 1.5 %collective-permute-done.10.refs_9_ = bf16[1,16,128]{2,1,0:T(8,128)(2,1)S(1)} collective-permute-done((bf16[1,16,128]{2,1,0:T(8,128)(2,1)S(1)}, bf16[1,16,128]{2,1,0:T(8,128)(2,1)S(1)}, u32[]{:S(2)}, u32[]{:S(2)}) %collective-permute-start.10) | collective-permute-done | bytes 4128 | tf_op jit(solution)/shard_map/ppermute | solution.py:623
  34.7 0.0 collective-permute-done.7.refs_6_
  34.7 0.0 collective-permute-done.4.refs_2_
  34.7 3.2 %final.1 = f32[256,256]{1,0:T(8,128)} custom-call(bf16[34,16,128]{2,1,0:T(8,128)(2,1)S(1)} %get-tuple-element.54.refs_0_, bf16[40,16,128]{2,1,0:T(8,128)(2,1)S(1)} %collective-permute-done.2.refs_0_.refs_1_, bf16[34,16,128]{2,1,0:T(8,128)(2,1)S(1)} %collective-permute-done.4.refs_2_, bf16[40,16,128]{2,1,0:T(8,128)(2,1)S(1)} %collective-permute-done.5.refs_1_.refs_3_, ...), custom_call_target="tpu_custom_call" | custom-call | tf_op jit(solution)/shard_map/final/pallas_call | solution.py:698
Async XLA Ops:
  2.3 15.3 %collective-permute-start.3 = (bf16[33,16,128]{2,1,0:T(8,128)(2,1)S(1)}, bf16[33,16,128]{2,1,0:T(8,128)(2,1)S(1)}, u32[]{:S(2)}, u32[]{:S(2)}) collective-permute-start(bf16[33,16,128]{2,1,0:T(8,128)(2,1)S(1)} %get-tuple-element.57), channel_id=1, source_target_pairs={{0,20},{4,16},{8,28},{12,24},{16,4},{20,0},{24,12},{28,8},{1,21},{... | collective-permute-start | bytes 405512 | tf_op jit(solution)/shard_map/ppermute | solution.py:623
  7.4 12.4 %collective-permute-start.6 = (bf16[33,16,128]{2,1,0:T(8,128)(2,1)S(1)}, bf16[33,16,128]{2,1,0:T(8,128)(2,1)S(1)}, u32[]{:S(2)}, u32[]{:S(2)}) collective-permute-start(bf16[33,16,128]{2,1,0:T(8,128)(2,1)S(1)} %get-tuple-element.43), channel_id=1, source_target_pairs={{0,16},{4,20},{8,24},{12,28},{16,0},{20,4},{24,8},{28,12},{1,17},{... | collective-permute-start | bytes 405512 | tf_op jit(solution)/shard_map/ppermute | solution.py:623
  10.5 1.3 %collective-permute-start = (f32[48,256]{1,0:T(8,128)S(1)}, f32[48,256]{1,0:T(8,128)S(1)}, u32[]{:S(2)}, u32[]{:S(2)}) collective-permute-start(f32[48,256]{1,0:T(8,128)S(1)} %get-tuple-element.45), channel_id=1, source_target_pairs={{0,1},{1,0},{2,3},{3,2},{4,5},{5,4},{6,7},{7,6},{8,9},{9,8},{10,11... | collective-permute-start | bytes 147464 | tf_op jit(solution)/shard_map/ppermute | solution.py:43
  10.6 1.2 %collective-permute-start.1 = (f32[48,256]{1,0:T(8,128)S(1)}, f32[48,256]{1,0:T(8,128)S(1)}, u32[]{:S(2)}, u32[]{:S(2)}) collective-permute-start(f32[48,256]{1,0:T(8,128)S(1)} %get-tuple-element.46), channel_id=1, source_target_pairs={{1,2},{2,1},{5,6},{6,5},{9,10},{10,9},{13,14},{14,13},{17,18},{18,... | collective-permute-start | bytes 147464 | tf_op jit(solution)/shard_map/ppermute | solution.py:43
  11.8 12.9 %copy-start = (bf16[2,256,256]{2,1,0:T(8,128)(2,1)S(1)}, bf16[2,256,256]{2,1,0:T(8,128)(2,1)}, u32[]{:S(2)}) copy-start(bf16[2,256,256]{2,1,0:T(8,128)(2,1)} %vel.1) | copy-start | bytes 786436
  11.8 12.9 %copy-start.1 = (f32[256,256]{1,0:T(8,128)S(1)}, f32[256,256]{1,0:T(8,128)}, u32[]{:S(2)}) copy-start(f32[256,256]{1,0:T(8,128)} %visc.1) | copy-start | bytes 786436
  11.8 12.9 %copy-start.2 = (f32[256,256]{1,0:T(8,128)S(1)}, f32[256,256]{1,0:T(8,128)}, u32[]{:S(2)}) copy-start(f32[256,256]{1,0:T(8,128)} %fric.1) | copy-start | bytes 786436
  11.9 12.9 %copy-start.3 = (bf16[2,256,256]{2,1,0:T(8,128)(2,1)S(1)}, bf16[2,256,256]{2,1,0:T(8,128)(2,1)}, u32[]{:S(2)}) copy-start(bf16[2,256,256]{2,1,0:T(8,128)(2,1)} %drive.1) | copy-start | bytes 786436
  12.1 16.5 %collective-permute-start.2 = (bf16[40,16,128]{2,1,0:T(8,128)(2,1)S(1)}, bf16[40,16,128]{2,1,0:T(8,128)(2,1)S(1)}, u32[]{:S(2)}, u32[]{:S(2)}) collective-permute-start(bf16[40,16,128]{2,1,0:T(8,128)(2,1)S(1)} %get-tuple-element.55), channel_id=1, source_target_pairs={{0,4},{4,0},{8,12},{12,8},{16,20},{20,16},{24,28},{28,24},{1,5},{5... | collective-permute-start | bytes 491528 | tf_op jit(solution)/shard_map/ppermute | solution.py:623
  12.5 16.8 %collective-permute-start.5 = (bf16[40,16,128]{2,1,0:T(8,128)(2,1)S(1)}, bf16[40,16,128]{2,1,0:T(8,128)(2,1)S(1)}, u32[]{:S(2)}, u32[]{:S(2)}) collective-permute-start(bf16[40,16,128]{2,1,0:T(8,128)(2,1)S(1)} %get-tuple-element.59), channel_id=1, source_target_pairs={{0,12},{4,8},{8,4},{12,0},{16,28},{20,24},{24,20},{28,16},{1,13},{... | collective-permute-start | bytes 491528 | tf_op jit(solution)/shard_map/ppermute | solution.py:623
  15.2 14.9 %collective-permute-start.8 = (bf16[40,16,128]{2,1,0:T(8,128)(2,1)S(1)}, bf16[40,16,128]{2,1,0:T(8,128)(2,1)S(1)}, u32[]{:S(2)}, u32[]{:S(2)}) collective-permute-start(bf16[40,16,128]{2,1,0:T(8,128)(2,1)S(1)} %get-tuple-element.62), channel_id=1, source_target_pairs={{0,28},{4,24},{8,20},{12,16},{16,12},{20,8},{24,4},{28,0},{1,29},{... | collective-permute-start | bytes 491528 | tf_op jit(solution)/shard_map/ppermute | solution.py:623
  17.7 7.1 %copy-start.4 = (s32[2,2]{1,0:T(2,128)S(1)}, s32[2,2]{1,0:T(2,128)}, u32[]{:S(2)}) copy-start(s32[2,2]{1,0:T(2,128)} %ice.1) | copy-start | bytes 52
  19.8 14.9 %collective-permute-start.7 = (bf16[34,16,128]{2,1,0:T(8,128)(2,1)S(1)}, bf16[34,16,128]{2,1,0:T(8,128)(2,1)S(1)}, u32[]{:S(2)}, u32[]{:S(2)}) collective-permute-start(bf16[34,16,128]{2,1,0:T(8,128)(2,1)S(1)} %get-tuple-element.61), channel_id=1, source_target_pairs={{0,24},{4,28},{8,16},{12,20},{16,8},{20,12},{24,0},{28,4},{1,25},{... | collective-permute-start | bytes 417800 | tf_op jit(solution)/shard_map/ppermute | solution.py:623
  24.8 9.9 %collective-permute-start.4 = (bf16[34,16,128]{2,1,0:T(8,128)(2,1)S(1)}, bf16[34,16,128]{2,1,0:T(8,128)(2,1)S(1)}, u32[]{:S(2)}, u32[]{:S(2)}) collective-permute-start(bf16[34,16,128]{2,1,0:T(8,128)(2,1)S(1)} %get-tuple-element.58), channel_id=1, source_target_pairs={{0,8},{4,12},{8,0},{12,4},{16,24},{20,28},{24,16},{28,20},{1,9},{5... | collective-permute-start | bytes 417800 | tf_op jit(solution)/shard_map/ppermute | solution.py:623
  28.6 4.6 %collective-permute-start.9 = (bf16[1,16,128]{2,1,0:T(8,128)(2,1)S(1)}, bf16[1,16,128]{2,1,0:T(8,128)(2,1)S(1)}, u32[]{:S(2)}, u32[]{:S(2)}) collective-permute-start(bf16[1,16,128]{2,1,0:T(8,128)(2,1)S(1)} %get-tuple-element.66), channel_id=1, source_target_pairs={{0,16},{4,20},{8,24},{12,28},{16,0},{20,4},{24,8},{28,12},{1,17},{... | collective-permute-start | bytes 12296 | tf_op jit(solution)/shard_map/ppermute | solution.py:623
  29.3 5.4 %collective-permute-start.10 = (bf16[1,16,128]{2,1,0:T(8,128)(2,1)S(1)}, bf16[1,16,128]{2,1,0:T(8,128)(2,1)S(1)}, u32[]{:S(2)}, u32[]{:S(2)}) collective-permute-start(bf16[1,16,128]{2,1,0:T(8,128)(2,1)S(1)} %get-tuple-element.68), channel_id=1, source_target_pairs={{0,20},{4,16},{8,28},{12,24},{16,4},{20,0},{24,12},{28,8},{1,21},{... | collective-permute-start | bytes 12296 | tf_op jit(solution)/shard_map/ppermute | solution.py:623

commit v6 on v5

--- a/solution.py
+++ b/solution.py
@@ -83,10 +83,15 @@
         filled[who] = rank + 1
 
 
-def columns_of(pick, block, precision):
-    return lax.dot_general(
-        pick, block, (((1,), (1,)), ((), ())), precision=precision, preferred_element_type=F32
-    )
+def split(value):
+    high = value.astype(jnp.bfloat16)
+    rest = value - high.astype(F32)
+    middle = rest.astype(jnp.bfloat16)
+    return high, middle, (rest - middle.astype(F32)).astype(jnp.bfloat16)
+
+
+def columns_of(pick, block):
+    return lax.dot_general(pick, block, (((1,), (1,)), ((), ())), preferred_element_type=F32)
 
 
 def load_scalars(owner, slot, weight, owner_s, slot_s, weight_b, weight_v, weight_s, sems):
@@ -202,8 +207,11 @@
     scalars[0].wait()
     fill_places(place, filled, groups, count, lambda scene: owner_s[0, scene])
 
-    def pick(start, kind):
-        return (across == picked + start).astype(kind)
+    def pick(depth):
+        picked = lax.broadcasted_iota(jnp.int32, (8, cells_y), 0)
+        across = lax.broadcasted_iota(jnp.int32, (8, cells_y), 1)
+        wanted = jnp.where(picked < depth, picked, picked + cells_y - 2 * depth)
+        return (across == wanted).astype(jnp.bfloat16)
 
     wait_all(loads[:4] + more)
     for index, (at, depth) in enumerate(FIELDS):
@@ -218,19 +226,16 @@
         field = {VISC: visc, FRIC: fric}.get(index)
         if field is None:
             field = vel.at[index] if index in (U, V) else drive.at[index - DRIVE_U]
-        precise = index in (VISC, FRIC)
-        for target, low, start in ((to_low, 0, 0), (to_high, cells_y - LANE, LANE - depth)):
-            rows = columns_of(
-                pick(start, F32 if precise else jnp.bfloat16), field[:, low : low + LANE],
-                lax.Precision.HIGHEST if precise else None,
-            )
-            target[at : at + depth, :] = rows[0:depth]
+        parts = [field[...]] if index not in (VISC, FRIC) else split(field[...])
+        rows = sum(columns_of(pick(depth), part) for part in parts)
+        to_low[at : at + depth, :] = rows[0:depth]
+        to_high[at : at + depth, :] = rows[depth : 2 * depth]
         edge[0, at : at + depth, :] = field[0:16, :].astype(F32)[0:depth]
         edge[1, at : at + depth, :] = field[cells - 16 : cells, :].astype(F32)[16 - depth : 16]
     loads[4].wait()
     both = (across == jnp.where(picked == 0, 0, LANE - 1)).astype(jnp.bfloat16)
     for scene in range(count):
-        rows = columns_of(both, obs[scene].reshape(2 * tile, LANE), None)
+        rows = columns_of(both, obs[scene].reshape(2 * tile, LANE))
         lines[0, scene : scene + 1, :] = rows[0:1]
         lines[1, scene : scene + 1, :] = rows[1:2]
     wait_all(scalars[1:])
@@ -340,24 +345,24 @@
     return push_u, push_v
 
 
-def relaxation(fields, work, wide, cells_y, spans, outs, shift, own_of):
+def relaxation(fields, work, wide, cells_y, spans, outs, shift, own_of, size=8):
     u, v, visc, fric, drive_u, drive_v, ice = fields
     next_u, next_v, relax_u, relax_v, sxx, syy, sxy = work
     second, ease, lead, trail = outs
     for low in spans[0]:
-        here = pl.ds(low, 8)
+        here = pl.ds(low, size)
         nu, drag = visc[here, :], fric[here, :]
-        nu_x = visc[pl.ds(low - 1, 8), :]
+        nu_x = visc[pl.ds(low - 1, size), :]
         nu_y = pltpu.roll(nu, 1, 1)
         inside = drag > 0.0
         for out, diag in ((relax_u, 5.0 * nu + 4.0 * nu_x + nu_y), (relax_v, 5.0 * nu + nu_x + 4.0 * nu_y)):
             out[here, :] = jnp.where(inside, 1.0 / jnp.where(inside, diag + drag, 1.0), 0.0)
     for low in spans[1]:
-        here = pl.ds(low, 8)
-        sxx[here, :], syy[here, :], sxy[here, :] = stress_block(u, v, visc, low, 8, wide)
+        here = pl.ds(low, size)
+        sxx[here, :], syy[here, :], sxy[here, :] = stress_block(u, v, visc, low, size, wide)
     for low in spans[2]:
-        here, there = pl.ds(low, 8), pl.ds(low + shift, 8)
-        pushes = image_block(sxx, syy, sxy, low, 8)
+        here, there = pl.ds(low, size), pl.ds(low + shift, size)
+        pushes = image_block(sxx, syy, sxy, low, size)
         for part, (push, speed, force, relax, then) in enumerate(
             zip(pushes, (u, v), (drive_u, drive_v), (relax_u, relax_v), (next_u, next_v))
         ):
@@ -369,13 +374,13 @@
                 ease[part, there, :] = slack
                 if own_of(low) is not None:
                     factor = -ice[here, 0:cells_y] * (slack * (move + now))[:, 0:cells_y]
-                    lead[part, pl.ds(own_of(low), 8), :] = factor
+                    lead[part, pl.ds(own_of(low), size), :] = factor
     for low in spans[3]:
-        here = pl.ds(low, 8)
-        sxx[here, :], syy[here, :], sxy[here, :] = stress_block(next_u, next_v, visc, low, 8, wide)
+        here = pl.ds(low, size)
+        sxx[here, :], syy[here, :], sxy[here, :] = stress_block(next_u, next_v, visc, low, size, wide)
     for low in spans[4]:
-        here, there = pl.ds(low, 8), pl.ds(low + shift, 8)
-        pushes = image_block(sxx, syy, sxy, low, 8)
+        here, there = pl.ds(low, size), pl.ds(low + shift, size)
+        pushes = image_block(sxx, syy, sxy, low, size)
         for part, (push, speed, force, relax) in enumerate(
             zip(pushes, (next_u, next_v), (drive_u, drive_v), (relax_u, relax_v))
         ):
@@ -383,7 +388,7 @@
             move = relax[here, :] * (force[here, :] - push - fric[here, :] * now)
             second[part, there, :] = ice[here, :] * (now + OMEGA * move)
             if own_of(low) is not None:
-                mine = pl.ds(own_of(low), 8)
+                mine = pl.ds(own_of(low), size)
                 trail[part, mine, :] = (
                     -ice[here, 0:cells_y] * (move + now)[:, 0:cells_y] - fric[here, 0:cells_y] * lead[part, mine, :]
                 )
@@ -420,11 +425,9 @@
         field[own_rows, cells_y:wide] = side_tile(upright, index)
         strips[index, 0] = field[8 : 8 + STRIP, :]
         strips[index, 1] = field[rows - 8 - STRIP : rows - 8, :]
-    blocks = range(8, rows - 8, 8)
-    relaxation(
-        fields, work, wide, cells_y, [blocks] * 5, (second, ease, lead, trail), 0,
-        lambda low: low - PAD if PAD <= low < PAD + cells else None,
-    )
+    last = PAD + cells
+    spans = [range(PAD, last, 32)] * 5
+    relaxation(fields, work, wide, cells_y, spans, (second, ease, lead, trail), 0, lambda low: low - PAD, 32)
 
 
 def trim_kernel(groups, tile, *refs):
@@ -572,14 +575,15 @@
         return carry
 
     lax.fori_loop(0, 2 * blocks, step, 0)
-    for low in range(8, rows - PAD, 8):
-        here = pl.ds(low, 8)
-        sxx[here, :], syy[here, :], sxy[here, :] = stress_block(u, v, visc, low, 8, wide)
-    for low in range(PAD, rows - PAD, 8):
-        mine = pl.ds(low - PAD, 8)
-        here = pl.ds(low, 8)
-        sums = jnp.zeros((8, cells_y), F32)
-        for part, push in enumerate(image_block(sxx, syy, sxy, low, 8)):
+    for low in (8, *range(PAD, rows - PAD, 32)):
+        size = 32 if low >= PAD else 8
+        here = pl.ds(low, size)
+        sxx[here, :], syy[here, :], sxy[here, :] = stress_block(u, v, visc, low, size, wide)
+    for low in range(PAD, rows - PAD, 32):
+        mine = pl.ds(low - PAD, 32)
+        here = pl.ds(low, 32)
+        sums = jnp.zeros((32, cells_y), F32)
+        for part, push in enumerate(image_block(sxx, syy, sxy, low, 32)):
             sums += (misfit[part, mine, :] - push[:, 0:cells_y]) * lead[part, mine, :]
             sums += lift[part][here, 0:cells_y] * trail[part, mine, :]
         grad[mine, :] = sums
@@ -610,7 +614,7 @@
     deep = CAP * 2 * blocks
     tall = PACK + groups // 2 * 8
     half = groups // 2
-    early = (half, half + 1)
+    early = (half + 1, half)
     late = tuple(step for step in range(groups) if step not in early)
     halo = 2 * (wide // LANE)
 
@@ -669,9 +673,10 @@
     ready = dict(zip(late, outs))
     got[0] = ready[0]
     order = [groups - 1, 1, *range(half + 2, groups - 1), half - 1, *range(2, half - 1)]
-    waits = {half + 2: half, 2: half + 1}
+    ties = {half + 2: [got[half + 1]], 2: [got[half]], 1: [], half - 1: [], groups - 1: []}
     for step in order:
-        got[step] = move(step, ready[step], *([got[waits[step]]] if step in waits else []))
+        got[step] = move(step, ready[step], *ties.get(step, []))
+    apart = [move(step, value, *more) for step, value, more in zip(early, outs[len(late) :], ([got[half]], [got[half]]))]
     strip = shape(len(FIELDS), 2, STRIP, wide)
     base_shapes = [shape(2, rows, wide)] * 2 + [shape(2, cells_x, cells_y)] * 2 + [shape(rows, wide)] * 2
     *base, strips = pl.pallas_call(
@@ -682,8 +687,7 @@
         scratch_shapes=[full(rows, wide)] * 12 + [full(LANE, cells_x), pltpu.SMEM(ice_mask.shape, i32), dma((1,))],
         compiler_params=limit,
         name="sweep",
-    )(ice_mask, vel0, visc, fric, drive, after(first, got[half + 1]), second)
-    apart = [move(step, value, strips) for step, value in zip(early, outs[len(late) :])]
+    )(ice_mask, vel0, visc, fric, drive, after(first, *[got[half]]), second)
     near = [got[step] for step in halo_steps(groups)]
     base = pl.pallas_call(
         functools.partial(trim_kernel, groups, tile),

time: 38.3 us -> 37.1 us (0.969)
  waiting for transfers between devices: 6.69 us -> 4.12 us
  starting transfers between devices: 18.1 us -> 19.9 us
  Pallas kernels: 12.9 us -> 12.4 us
    ppermute x9, waiting for transfers between devices: 6.14 us -> 3.57 us  [move(): return lax.ppermute(after(value, *others) if others else value, 'gx', pairs)]
    ppermute x9, starting transfers between devices: 17.4 us -> 19.2 us  [move(): return lax.ppermute(after(value, *others) if others else value, 'gx', pairs)]
  transfers between devices with their start and end apart: 11 -> 11, of which waited for: 4 -> 4; matrix products, arithmetic and copies ran while one was open for 0% -> 0% of each run, Pallas kernels for 20% -> 19%
where the time goes in v6:
time: 37.1 us; the launch traced here: 36.6 us
  starting transfers between devices  19.9 us (54%)
  Pallas kernels  12.4 us (33%)
  waiting for transfers between devices  4.12 us (11%)
    ppermute x9, starting transfers between devices, move(): return lax.ppermute(after(value, *others) if others else value, 'gx', pairs)  19.2 us
    ppermute x9, waiting for transfers between devices, move(): return lax.ppermute(after(value, *others) if others else value, 'gx', pairs)  3.57 us
    pallas_call x1, Pallas kernels, body(): pl.pallas_call(functools.partial(sweep_kernel, tile), out_shape=base_shap...  3.52 us
    pallas_call x1, Pallas kernels, body(): pl.pallas_call(functools.partial(final_kernel, groups, tile, early), out_...  3.15 us
    pallas_call x1, Pallas kernels, body(): pl.pallas_call(functools.partial(pack_kernel, groups, count, tile), out_s...  2.62 us
    pallas_call x1, Pallas kernels, body(): pl.pallas_call(functools.partial(gather_kernel, groups, count, tile), out...  2.34 us
  transfers between devices with their start and end apart: 11, of which 4 were waited for; matrix products, arithmetic and copies ran while one was open for 0% of the time, Pallas kernels for 19%

profile of v6, /device:TPU:0, one launch (start us, length us, event | category | flops | bytes accessed | tf_op | source)
XLA Modules:
  0.0 36.6 jit_solution(9719010924550642075)
XLA Ops:
  0.0 2.3 %gather.1 = (bf16[34,16,128]{2,1,0:T(8,128)(2,1)S(1)}, bf16[40,16,128]{2,1,0:T(8,128)(2,1)S(1)}, bf16[34,16,128]{2,1,0:T(8,128)(2,1)S(1)}, bf16[40,16,128]{2,1,0...) custom-call(s32[1,16]{1,0:T(1,128)} %bitcast.4, ...), custom_call_target="tpu_custom_call" | custom-call | tf_op jit(solution)/shard_map/gather/pallas_call | solution.py:634
  2.3 5.0 %collective-permute-start.6 = (bf16[33,16,128]{2,1,0:T(8,128)(2,1)S(1)}, bf16[33,16,128]{2,1,0:T(8,128)(2,1)S(1)}, u32[]{:S(2)}, u32[]{:S(2)}) collective-permute-start(bf16[33,16,128]{2,1,0:T(8,128)(2,1)S(1)} %get-tuple-element.59), channel_id=1, source_target_pairs={{0,20},{4,16},{8,28},{12,24},{16,4},{20,0},{24,12},{28,8},{1,21},{... | collective-permute-start | bytes 405512 | tf_op jit(solution)/shard_map/ppermute | solution.py:627
  7.4 0.3 collective-permute-start.3
  7.7 2.6 %pack.1 = (f32[48,256]{1,0:T(8,128)S(1)}, f32[48,256]{1,0:T(8,128)S(1)}, f32[2,16,256]{2,1,0:T(8,128)S(1)}) custom-call(s32[1,16]{1,0:T(1,128)} %bitcast.5, s32[1,16]{1,0:T(1,128)} %refs_1_.3, bf16[1,16]{1,0:T(2,128)(2,1)} %refs_2_.3, s32[2,2]{1,0:T(2,128)} %ice.1, bf16[16,16,16,128]{3,2,1,0:T(8,128)(2,1)} %bitcast.3, bf16[2,256,256]{2,1,0:T(8,128)(2,1)} %vel.1, ...), custom_call_target="tpu_custom_call" | custom-call | tf_op jit(solution)/shard_map/pack/pallas_call | solution.py:649
  10.3 0.1 collective-permute-start
  10.4 0.7 %collective-permute-start.1 = (f32[48,256]{1,0:T(8,128)S(1)}, f32[48,256]{1,0:T(8,128)S(1)}, u32[]{:S(2)}, u32[]{:S(2)}) collective-permute-start(f32[48,256]{1,0:T(8,128)S(1)} %get-tuple-element.46), channel_id=1, source_target_pairs={{1,2},{2,1},{5,6},{6,5},{9,10},{10,9},{13,14},{14,13},{17,18},{18,... | collective-permute-start | bytes 147464 | tf_op jit(solution)/shard_map/ppermute | solution.py:43
  11.1 0.5 %collective-permute-done.refs_0_.first = f32[48,256]{1,0:T(8,128)S(1)} collective-permute-done((f32[48,256]{1,0:T(8,128)S(1)}, f32[48,256]{1,0:T(8,128)S(1)}, u32[]{:S(2)}, u32[]{:S(2)}) %collective-permute-start) | collective-permute-done | bytes 49184 | tf_op jit(solution)/shard_map/ppermute | solution.py:43
  11.6 0.0 collective-permute-done.1.refs_1_.then
  11.6 0.0 copy-start
  11.6 0.0 copy-start.1
  11.6 0.0 copy-start.2
  11.7 0.0 copy-start.3
  11.7 0.2 widen.1
  11.9 0.4 %collective-permute-start.2 = (bf16[40,16,128]{2,1,0:T(8,128)(2,1)S(1)}, bf16[40,16,128]{2,1,0:T(8,128)(2,1)S(1)}, u32[]{:S(2)}, u32[]{:S(2)}) collective-permute-start(bf16[40,16,128]{2,1,0:T(8,128)(2,1)S(1)} %get-tuple-element.55), channel_id=1, source_target_pairs={{0,4},{4,0},{8,12},{12,8},{16,20},{20,16},{24,28},{28,24},{1,5},{5... | collective-permute-start | bytes 491528 | tf_op jit(solution)/shard_map/ppermute | solution.py:627
  12.3 2.7 %collective-permute-start.5 = (bf16[40,16,128]{2,1,0:T(8,128)(2,1)S(1)}, bf16[40,16,128]{2,1,0:T(8,128)(2,1)S(1)}, u32[]{:S(2)}, u32[]{:S(2)}) collective-permute-start(bf16[40,16,128]{2,1,0:T(8,128)(2,1)S(1)} %get-tuple-element.58), channel_id=1, source_target_pairs={{0,12},{4,8},{8,4},{12,0},{16,28},{20,24},{24,20},{28,16},{1,13},{... | collective-permute-start | bytes 491528 | tf_op jit(solution)/shard_map/ppermute | solution.py:627
  15.0 2.4 %collective-permute-start.8 = (bf16[40,16,128]{2,1,0:T(8,128)(2,1)S(1)}, bf16[40,16,128]{2,1,0:T(8,128)(2,1)S(1)}, u32[]{:S(2)}, u32[]{:S(2)}) collective-permute-start(bf16[40,16,128]{2,1,0:T(8,128)(2,1)S(1)} %get-tuple-element.62), channel_id=1, source_target_pairs={{0,28},{4,24},{8,20},{12,16},{16,12},{20,8},{24,4},{28,0},{1,29},{... | collective-permute-start | bytes 491528 | tf_op jit(solution)/shard_map/ppermute | solution.py:627
  17.4 0.2 collective-permute-done.6.refs_5_
  17.7 2.1 %collective-permute-done.3.refs_4_ = bf16[33,16,128]{2,1,0:T(8,128)(2,1)S(1)} collective-permute-done((bf16[33,16,128]{2,1,0:T(8,128)(2,1)S(1)}, bf16[33,16,128]{2,1,0:T(8,128)(2,1)S(1)}, u32[]{:S(2)}, u32[]{:S(2)}) %collective-permute-start.3) | collective-permute-done | bytes 135200 | tf_op jit(solution)/shard_map/ppermute | solution.py:627
  19.8 2.2 %collective-permute-start.4 = (bf16[34,16,128]{2,1,0:T(8,128)(2,1)S(1)}, bf16[34,16,128]{2,1,0:T(8,128)(2,1)S(1)}, u32[]{:S(2)}, u32[]{:S(2)}) collective-permute-start(bf16[34,16,128]{2,1,0:T(8,128)(2,1)S(1)} %get-tuple-element.57), channel_id=1, source_target_pairs={{0,8},{4,12},{8,0},{12,4},{16,24},{20,28},{24,16},{28,20},{1,9},{5... | collective-permute-start | bytes 417800 | tf_op jit(solution)/shard_map/ppermute | solution.py:627
  22.0 3.0 %collective-permute-start.7 = (bf16[34,16,128]{2,1,0:T(8,128)(2,1)S(1)}, bf16[34,16,128]{2,1,0:T(8,128)(2,1)S(1)}, u32[]{:S(2)}, u32[]{:S(2)}) collective-permute-start(bf16[34,16,128]{2,1,0:T(8,128)(2,1)S(1)} %get-tuple-element.61), channel_id=1, source_target_pairs={{0,24},{4,28},{8,16},{12,20},{16,8},{20,12},{24,0},{28,4},{1,25},{... | collective-permute-start | bytes 417800 | tf_op jit(solution)/shard_map/ppermute | solution.py:627
  25.0 0.0 copy-start.4
  25.0 0.0 collective-permute-done.2.refs_0_.refs_1_
  25.0 0.0 collective-permute-start.9
  25.0 0.0 collective-permute-done.5.refs_1_.refs_3_
  25.0 3.1 %collective-permute-start.10 = (bf16[1,16,128]{2,1,0:T(8,128)(2,1)S(1)}, bf16[1,16,128]{2,1,0:T(8,128)(2,1)S(1)}, u32[]{:S(2)}, u32[]{:S(2)}) collective-permute-start(bf16[1,16,128]{2,1,0:T(8,128)(2,1)S(1)} %get-tuple-element.66), channel_id=1, source_target_pairs={{0,16},{4,20},{8,24},{12,28},{16,0},{20,4},{24,8},{28,12},{1,17},{... | collective-permute-start | bytes 12296 | tf_op jit(solution)/shard_map/ppermute | solution.py:627
  28.1 0.0 copy-done
  28.1 0.0 copy-done.1
  28.1 0.0 copy-done.2
  28.1 0.0 copy-done.3
  28.1 0.0 copy-done.4
  28.1 3.5 %sweep.1 = (f32[2,288,384]{2,1,0:T(8,128)S(1)}, f32[2,288,384]{2,1,0:T(8,128)S(1)}, f32[2,256,256]{2,1,0:T(8,128)S(1)}, f32[2,256,256]{2,1,0:T(8,128)S(1)}, f32[...) custom-call(s32[2,2]{1,0:T(2,128)S(1)} %copy-done.4, bf16[2,256,256]{2,1,0:T(8,128)(2,1)S(1)} %copy-done, ...), custom_call_target="tpu_custom_call" | custom-call | tf_op jit(solution)/shard_map/sweep/pallas_call | solution.py:682
  31.6 0.0 collective-permute-done.8.refs_2_.refs_7_
  31.7 0.5 %trim.1 = (f32[2,288,384]{2,1,0:T(8,128)S(1)}, f32[2,288,384]{2,1,0:T(8,128)S(1)}, f32[2,256,256]{2,1,0:T(8,128)S(1)}, f32[2,256,256]{2,1,0:T(8,128)S(1)}, f32[2...) custom-call(bf16[40,16,128]{2,1,0:T(8,128)(2,1)S(1)} %collective-per, ...), custom_call_target="tpu_custom_call", output_to_operand_aliasing={{0}: (4, {}), {1}: (5, {}), {2}: (6, {}), {3}: (7, {}), {4}... | custom-call | tf_op jit(solution)/shard_map/trim/pallas_call | solution.py:692
  32.2 0.0 collective-permute-done.9.refs_8_
  32.2 1.2 %collective-permute-done.10.refs_9_ = bf16[1,16,128]{2,1,0:T(8,128)(2,1)S(1)} collective-permute-done((bf16[1,16,128]{2,1,0:T(8,128)(2,1)S(1)}, bf16[1,16,128]{2,1,0:T(8,128)(2,1)S(1)}, u32[]{:S(2)}, u32[]{:S(2)}) %collective-permute-start.10) | collective-permute-done | bytes 4128 | tf_op jit(solution)/shard_map/ppermute | solution.py:627
  33.4 0.0 collective-permute-done.4.refs_2_
  33.4 0.0 collective-permute-done.7.refs_6_
  33.4 3.1 %final.1 = f32[256,256]{1,0:T(8,128)} custom-call(bf16[34,16,128]{2,1,0:T(8,128)(2,1)S(1)} %get-tuple-element.54.refs_0_, bf16[40,16,128]{2,1,0:T(8,128)(2,1)S(1)} %collective-permute-done.2.refs_0_.refs_1_, bf16[34,16,128]{2,1,0:T(8,128)(2,1)S(1)} %collective-permute-done.4.refs_2_, bf16[40,16,128]{2,1,0:T(8,128)(2,1)S(1)} %collective-permute-done.5.refs_1_.refs_3_, ...), custom_call_target="tpu_custom_call" | custom-call | tf_op jit(solution)/shard_map/final/pallas_call | solution.py:702
Async XLA Ops:
  2.3 15.3 %collective-permute-start.6 = (bf16[33,16,128]{2,1,0:T(8,128)(2,1)S(1)}, bf16[33,16,128]{2,1,0:T(8,128)(2,1)S(1)}, u32[]{:S(2)}, u32[]{:S(2)}) collective-permute-start(bf16[33,16,128]{2,1,0:T(8,128)(2,1)S(1)} %get-tuple-element.59), channel_id=1, source_target_pairs={{0,20},{4,16},{8,28},{12,24},{16,4},{20,0},{24,12},{28,8},{1,21},{... | collective-permute-start | bytes 405512 | tf_op jit(solution)/shard_map/ppermute | solution.py:627
  7.4 12.4 %collective-permute-start.3 = (bf16[33,16,128]{2,1,0:T(8,128)(2,1)S(1)}, bf16[33,16,128]{2,1,0:T(8,128)(2,1)S(1)}, u32[]{:S(2)}, u32[]{:S(2)}) collective-permute-start(bf16[33,16,128]{2,1,0:T(8,128)(2,1)S(1)} %get-tuple-element.43), channel_id=1, source_target_pairs={{0,16},{4,20},{8,24},{12,28},{16,0},{20,4},{24,8},{28,12},{1,17},{... | collective-permute-start | bytes 405512 | tf_op jit(solution)/shard_map/ppermute | solution.py:627
  10.3 1.3 %collective-permute-start = (f32[48,256]{1,0:T(8,128)S(1)}, f32[48,256]{1,0:T(8,128)S(1)}, u32[]{:S(2)}, u32[]{:S(2)}) collective-permute-start(f32[48,256]{1,0:T(8,128)S(1)} %get-tuple-element.45), channel_id=1, source_target_pairs={{0,1},{1,0},{2,3},{3,2},{4,5},{5,4},{6,7},{7,6},{8,9},{9,8},{10,11... | collective-permute-start | bytes 147464 | tf_op jit(solution)/shard_map/ppermute | solution.py:43
  10.4 1.2 %collective-permute-start.1 = (f32[48,256]{1,0:T(8,128)S(1)}, f32[48,256]{1,0:T(8,128)S(1)}, u32[]{:S(2)}, u32[]{:S(2)}) collective-permute-start(f32[48,256]{1,0:T(8,128)S(1)} %get-tuple-element.46), channel_id=1, source_target_pairs={{1,2},{2,1},{5,6},{6,5},{9,10},{10,9},{13,14},{14,13},{17,18},{18,... | collective-permute-start | bytes 147464 | tf_op jit(solution)/shard_map/ppermute | solution.py:43
  11.6 16.5 %copy-start = (bf16[2,256,256]{2,1,0:T(8,128)(2,1)S(1)}, bf16[2,256,256]{2,1,0:T(8,128)(2,1)}, u32[]{:S(2)}) copy-start(bf16[2,256,256]{2,1,0:T(8,128)(2,1)} %vel.1) | copy-start | bytes 786436
  11.6 16.5 %copy-start.1 = (f32[256,256]{1,0:T(8,128)S(1)}, f32[256,256]{1,0:T(8,128)}, u32[]{:S(2)}) copy-start(f32[256,256]{1,0:T(8,128)} %visc.1) | copy-start | bytes 786436
  11.6 16.5 %copy-start.2 = (f32[256,256]{1,0:T(8,128)S(1)}, f32[256,256]{1,0:T(8,128)}, u32[]{:S(2)}) copy-start(f32[256,256]{1,0:T(8,128)} %fric.1) | copy-start | bytes 786436
  11.7 16.5 %copy-start.3 = (bf16[2,256,256]{2,1,0:T(8,128)(2,1)S(1)}, bf16[2,256,256]{2,1,0:T(8,128)(2,1)}, u32[]{:S(2)}) copy-start(bf16[2,256,256]{2,1,0:T(8,128)(2,1)} %drive.1) | copy-start | bytes 786436
  11.9 13.1 %collective-permute-start.2 = (bf16[40,16,128]{2,1,0:T(8,128)(2,1)S(1)}, bf16[40,16,128]{2,1,0:T(8,128)(2,1)S(1)}, u32[]{:S(2)}, u32[]{:S(2)}) collective-permute-start(bf16[40,16,128]{2,1,0:T(8,128)(2,1)S(1)} %get-tuple-element.55), channel_id=1, source_target_pairs={{0,4},{4,0},{8,12},{12,8},{16,20},{20,16},{24,28},{28,24},{1,5},{5... | collective-permute-start | bytes 491528 | tf_op jit(solution)/shard_map/ppermute | solution.py:627
  12.3 12.7 %collective-permute-start.5 = (bf16[40,16,128]{2,1,0:T(8,128)(2,1)S(1)}, bf16[40,16,128]{2,1,0:T(8,128)(2,1)S(1)}, u32[]{:S(2)}, u32[]{:S(2)}) collective-permute-start(bf16[40,16,128]{2,1,0:T(8,128)(2,1)S(1)} %get-tuple-element.58), channel_id=1, source_target_pairs={{0,12},{4,8},{8,4},{12,0},{16,28},{20,24},{24,20},{28,16},{1,13},{... | collective-permute-start | bytes 491528 | tf_op jit(solution)/shard_map/ppermute | solution.py:627
  15.0 16.6 %collective-permute-start.8 = (bf16[40,16,128]{2,1,0:T(8,128)(2,1)S(1)}, bf16[40,16,128]{2,1,0:T(8,128)(2,1)S(1)}, u32[]{:S(2)}, u32[]{:S(2)}) collective-permute-start(bf16[40,16,128]{2,1,0:T(8,128)(2,1)S(1)} %get-tuple-element.62), channel_id=1, source_target_pairs={{0,28},{4,24},{8,20},{12,16},{16,12},{20,8},{24,4},{28,0},{1,29},{... | collective-permute-start | bytes 491528 | tf_op jit(solution)/shard_map/ppermute | solution.py:627
  19.8 13.6 %collective-permute-start.4 = (bf16[34,16,128]{2,1,0:T(8,128)(2,1)S(1)}, bf16[34,16,128]{2,1,0:T(8,128)(2,1)S(1)}, u32[]{:S(2)}, u32[]{:S(2)}) collective-permute-start(bf16[34,16,128]{2,1,0:T(8,128)(2,1)S(1)} %get-tuple-element.57), channel_id=1, source_target_pairs={{0,8},{4,12},{8,0},{12,4},{16,24},{20,28},{24,16},{28,20},{1,9},{5... | collective-permute-start | bytes 417800 | tf_op jit(solution)/shard_map/ppermute | solution.py:627
  22.0 11.5 %collective-permute-start.7 = (bf16[34,16,128]{2,1,0:T(8,128)(2,1)S(1)}, bf16[34,16,128]{2,1,0:T(8,128)(2,1)S(1)}, u32[]{:S(2)}, u32[]{:S(2)}) collective-permute-start(bf16[34,16,128]{2,1,0:T(8,128)(2,1)S(1)} %get-tuple-element.61), channel_id=1, source_target_pairs={{0,24},{4,28},{8,16},{12,20},{16,8},{20,12},{24,0},{28,4},{1,25},{... | collective-permute-start | bytes 417800 | tf_op jit(solution)/shard_map/ppermute | solution.py:627
  25.0 3.1 %copy-start.4 = (s32[2,2]{1,0:T(2,128)S(1)}, s32[2,2]{1,0:T(2,128)}, u32[]{:S(2)}) copy-start(s32[2,2]{1,0:T(2,128)} %ice.1) | copy-start | bytes 52
  25.0 7.2 %collective-permute-start.9 = (bf16[1,16,128]{2,1,0:T(8,128)(2,1)S(1)}, bf16[1,16,128]{2,1,0:T(8,128)(2,1)S(1)}, u32[]{:S(2)}, u32[]{:S(2)}) collective-permute-start(bf16[1,16,128]{2,1,0:T(8,128)(2,1)S(1)} %get-tuple-element.64), channel_id=1, source_target_pairs={{0,20},{4,16},{8,28},{12,24},{16,4},{20,0},{24,12},{28,8},{1,21},{... | collective-permute-start | bytes 12296 | tf_op jit(solution)/shard_map/ppermute | solution.py:627
  25.0 8.4 %collective-permute-start.10 = (bf16[1,16,128]{2,1,0:T(8,128)(2,1)S(1)}, bf16[1,16,128]{2,1,0:T(8,128)(2,1)S(1)}, u32[]{:S(2)}, u32[]{:S(2)}) collective-permute-start(bf16[1,16,128]{2,1,0:T(8,128)(2,1)S(1)} %get-tuple-element.66), channel_id=1, source_target_pairs={{0,16},{4,20},{8,24},{12,28},{16,0},{20,4},{24,8},{28,12},{1,17},{... | collective-permute-start | bytes 12296 | tf_op jit(solution)/shard_map/ppermute | solution.py:627

commit v7 on v6

--- a/solution.py
+++ b/solution.py
@@ -464,12 +464,37 @@
         )
 
 
-def final_kernel(groups, tile, early, *refs):
+def part_kernel(slots, tile, *refs):
+    pays, (sums, table) = refs[:-2], refs[-2:]
+    blocks = tile // PACK
+    for number, pay in enumerate(pays):
+        meta = pay[CAP * 2 * blocks].astype(F32)[8:9]
+        for index in range(CAP * slots):
+            at = number * CAP * slots + index
+            table[at : at + 1, :] = jnp.broadcast_to(meta[:, index : index + 1], (1, LANE))
+
+    def step(index, carry):
+        total = [jnp.zeros((PACK, LANE), F32) for _ in range(slots)]
+        for number, pay in enumerate(pays):
+            for rank in range(CAP):
+                got = pay[rank * 2 * blocks + index].astype(F32)
+                for position in range(slots):
+                    at = (number * CAP + rank) * slots + position
+                    total[position] += table[at : at + 1, :] * got
+        for position in range(slots):
+            sums[index, position] = total[position]
+        return carry
+
+    lax.fori_loop(0, 2 * blocks, step, 0)
+
+
+def final_kernel(groups, tile, early, summed, *refs):
+    sums_before, refs = refs[0], refs[1:]
     pays = refs[:groups]
     apart = dict(zip(early, refs[groups:]))
     refs = refs[len(early) :]
     second, ease, lead, trail, visc, ice, grad = refs[groups : groups + 7]
-    misfit, u, v, sxx, syy, sxy, table, total, rows_x, rows_y, turned = refs[groups + 7 :]
+    misfit, u, v, sxx, syy, sxy, table, total, rows_x, rows_y, turned, result, result_sem = refs[groups + 7 :]
     rows, wide = visc.shape
     cells_y = wide - LANE
     cells = rows - 2 * PAD
@@ -549,8 +574,10 @@
 
     def step(index, carry):
         part, chunk = index // blocks, index % blocks
-        sums = [jnp.zeros((PACK, LANE), F32) for _ in range(slots)]
+        sums = [sums_before[index, position] for position in range(slots)]
         for group in range(groups):
+            if group in summed:
+                continue
             for rank in range(CAP):
                 got = pays[group][rank * 2 * blocks + index].astype(F32)
                 for position in range(slots):
@@ -579,6 +606,7 @@
         size = 32 if low >= PAD else 8
         here = pl.ds(low, size)
         sxx[here, :], syy[here, :], sxy[here, :] = stress_block(u, v, visc, low, size, wide)
+    copies, quarter = [], cells // 4
     for low in range(PAD, rows - PAD, 32):
         mine = pl.ds(low - PAD, 32)
         here = pl.ds(low, 32)
@@ -586,7 +614,12 @@
         for part, push in enumerate(image_block(sxx, syy, sxy, low, 32)):
             sums += (misfit[part, mine, :] - push[:, 0:cells_y]) * lead[part, mine, :]
             sums += lift[part][here, 0:cells_y] * trail[part, mine, :]
-        grad[mine, :] = sums
+        result[mine, :] = sums
+        done = low - PAD + 32
+        if done % quarter == 0:
+            part_rows = pl.ds(done - quarter, quarter)
+            copies += copy_all([(result.at[part_rows], grad.at[part_rows])], result_sem, done // quarter - 1)
+    wait_all(copies)
 
 
 def body(vel0, visc, fric, drive, scene_obs, scene_weight, scene_owner, scene_slot, ice_mask):
@@ -672,11 +705,9 @@
     )(first, second, edge, *(pays[step] for step in late))
     ready = dict(zip(late, outs))
     got[0] = ready[0]
-    order = [groups - 1, 1, *range(half + 2, groups - 1), half - 1, *range(2, half - 1)]
-    ties = {half + 2: [got[half + 1]], 2: [got[half]], 1: [], half - 1: [], groups - 1: []}
-    for step in order:
+    ties = {half + 2: [got[half + 1]], 1: [], half - 1: [], groups - 1: []}
+    for step in (groups - 1, 1, *range(half + 2, groups - 1), half - 1):
         got[step] = move(step, ready[step], *ties.get(step, []))
-    apart = [move(step, value, *more) for step, value, more in zip(early, outs[len(late) :], ([got[half]], [got[half]]))]
     strip = shape(len(FIELDS), 2, STRIP, wide)
     base_shapes = [shape(2, rows, wide)] * 2 + [shape(2, cells_x, cells_y)] * 2 + [shape(rows, wide)] * 2
     *base, strips = pl.pallas_call(
@@ -687,7 +718,10 @@
         scratch_shapes=[full(rows, wide)] * 12 + [full(LANE, cells_x), pltpu.SMEM(ice_mask.shape, i32), dma((1,))],
         compiler_params=limit,
         name="sweep",
-    )(ice_mask, vel0, visc, fric, drive, after(first, *[got[half]]), second)
+    )(ice_mask, vel0, visc, fric, drive, after(first, *[got[half + 1]]), second)
+    for step in range(2, half - 1):
+        got[step] = move(step, ready[step], strips)
+    apart = [move(step, value, *more) for step, value, more in zip(early, outs[len(late) :], ([strips], [strips]))]
     near = [got[step] for step in halo_steps(groups)]
     base = pl.pallas_call(
         functools.partial(trim_kernel, groups, tile),
@@ -699,19 +733,30 @@
         compiler_params=limit,
         name="trim",
     )(*near, strips, *base)
+    summed = (0, *early, *halo_steps(groups))
+    slots = cells_x // tile * (cells_y // tile)
+    partial = pl.pallas_call(
+        functools.partial(part_kernel, slots, tile),
+        out_shape=shape(2 * blocks, slots, PACK, LANE),
+        in_specs=[VMEM] * len(summed),
+        out_specs=VMEM,
+        scratch_shapes=[full(len(summed) * CAP * slots, LANE)],
+        compiler_params=limit,
+        name="part",
+    )(after(got[0], strips), *(got[step] for step in summed[1:]))
     return pl.pallas_call(
-        functools.partial(final_kernel, groups, tile, early),
+        functools.partial(final_kernel, groups, tile, early, summed),
         out_shape=shape(cells_x, cells_y),
-        in_specs=[VMEM] * (groups + len(early) + 6),
-        out_specs=VMEM,
+        in_specs=[VMEM] * (groups + len(early) + 7),
+        out_specs=HBM,
         scratch_shapes=[full(2, cells_x, cells_y)] + [full(rows, wide)] * 5
         + [
             full(groups * CAP * 4, LANE), full(8, LANE), full(PACK * groups, LANE), full(PACK * groups, LANE),
-            full(LANE, long),
+            full(LANE, long), full(cells_x, cells_y), dma((4,)),
         ],
         compiler_params=limit,
         name="final",
-    )(*got, *apart, *base)
+    )(partial, *got, *apart, *base)
 
 
 def solution(mesh):

time: 37.1 us -> 36.3 us (0.978)
  the two profiles are of different devices: /device:TPU:0 before, /device:TPU:4 now
where the time goes in v7:
time: 36.3 us; the launch traced here: 36.1 us
  starting transfers between devices  18.3 us (50%)
  Pallas kernels  12.4 us (34%)
  waiting for transfers between devices  5.25 us (14%)
    ppermute x9, starting transfers between devices, move(): return lax.ppermute(after(value, *others) if others else value, 'gx', pairs)  15.7 us
    pallas_call x1, Pallas kernels, body(): pl.pallas_call(functools.partial(sweep_kernel, tile), out_shape=base_shap...  3.43 us
    ppermute x2, waiting for transfers between devices, swap(): return (lax.ppermute(even, 'gy', near), lax.ppermute(odd, 'gy', far))  2.89 us
    pallas_call x1, Pallas kernels, body(): pl.pallas_call(functools.partial(pack_kernel, groups, count, tile), out_s...  2.67 us
    ppermute x2, starting transfers between devices, swap(): return (lax.ppermute(even, 'gy', near), lax.ppermute(odd, 'gy', far))  2.58 us
    pallas_call x1, Pallas kernels, body(): pl.pallas_call(functools.partial(final_kernel, groups, tile, early, summe...  2.51 us
    ppermute x9, waiting for transfers between devices, move(): return lax.ppermute(after(value, *others) if others else value, 'gx', pairs)  2.37 us
    pallas_call x1, Pallas kernels, body(): pl.pallas_call(functools.partial(gather_kernel, groups, count, tile), out...  2.34 us
  transfers between devices with their start and end apart: 11, of which 3 were waited for; matrix products, arithmetic and copies ran while one was open for 0% of the time, Pallas kernels for 21%

profile of v7, /device:TPU:4, one launch (start us, length us, event | category | flops | bytes accessed | tf_op | source)
XLA Modules:
  0.0 36.1 jit_solution(18431567492748541305)
XLA Ops:
  0.0 2.3 %gather.1 = (bf16[34,16,128]{2,1,0:T(8,128)(2,1)S(1)}, bf16[40,16,128]{2,1,0:T(8,128)(2,1)S(1)}, bf16[34,16,128]{2,1,0:T(8,128)(2,1)S(1)}, bf16[40,16,128]{2,1,0...) custom-call(s32[1,16]{1,0:T(1,128)} %bitcast.4, ...), custom_call_target="tpu_custom_call" | custom-call | tf_op jit(solution)/shard_map/gather/pallas_call | solution.py:667
  2.3 3.6 %collective-permute-start.2 = (bf16[33,16,128]{2,1,0:T(8,128)(2,1)S(1)}, bf16[33,16,128]{2,1,0:T(8,128)(2,1)S(1)}, u32[]{:S(2)}, u32[]{:S(2)}) collective-permute-start(bf16[33,16,128]{2,1,0:T(8,128)(2,1)S(1)} %get-tuple-element.56), channel_id=1, source_target_pairs={{0,20},{4,16},{8,28},{12,24},{16,4},{20,0},{24,12},{28,8},{1,21},{... | collective-permute-start | bytes 405512 | tf_op jit(solution)/shard_map/ppermute | solution.py:660
  5.9 0.3 collective-permute-start.3
  6.3 0.0 copy-start.3
  6.3 2.7 %pack.1 = (f32[48,256]{1,0:T(8,128)S(1)}, f32[48,256]{1,0:T(8,128)S(1)}, f32[2,16,256]{2,1,0:T(8,128)S(1)}) custom-call(s32[1,16]{1,0:T(1,128)} %bitcast.5, s32[1,16]{1,0:T(1,128)} %refs_1_.3, bf16[1,16]{1,0:T(2,128)(2,1)} %refs_2_.3, s32[2,2]{1,0:T(2,128)} %ice.1, bf16[16,16,16,128]{3,2,1,0:T(8,128)(2,1)} %bitcast.3, bf16[2,256,256]{2,1,0:T(8,128)(2,1)} %vel.1, ...), custom_call_target="tpu_custom_call" | custom-call | tf_op jit(solution)/shard_map/pack/pallas_call | solution.py:682
  8.9 0.1 collective-permute-start
  9.0 2.5 %collective-permute-start.1 = (f32[48,256]{1,0:T(8,128)S(1)}, f32[48,256]{1,0:T(8,128)S(1)}, u32[]{:S(2)}, u32[]{:S(2)}) collective-permute-start(f32[48,256]{1,0:T(8,128)S(1)} %get-tuple-element.47), channel_id=1, source_target_pairs={{1,2},{2,1},{5,6},{6,5},{9,10},{10,9},{13,14},{14,13},{17,18},{18,... | collective-permute-start | bytes 147464 | tf_op jit(solution)/shard_map/ppermute | solution.py:43
  11.5 0.0 collective-permute-done.refs_0_.first
  11.5 2.9 %collective-permute-done.1.refs_1_.then = f32[48,256]{1,0:T(8,128)S(1)} collective-permute-done((f32[48,256]{1,0:T(8,128)S(1)}, f32[48,256]{1,0:T(8,128)S(1)}, u32[]{:S(2)}, u32[]{:S(2)}) %collective-permute-start.1) | collective-permute-done | bytes 49184 | tf_op jit(solution)/shard_map/ppermute | solution.py:43
  14.4 0.0 copy-start
  14.4 0.0 copy-start.1
  14.4 0.0 copy-start.2
  14.4 0.2 widen.1
  14.7 0.6 %collective-permute-start.4 = (bf16[40,16,128]{2,1,0:T(8,128)(2,1)S(1)}, bf16[40,16,128]{2,1,0:T(8,128)(2,1)S(1)}, u32[]{:S(2)}, u32[]{:S(2)}) collective-permute-start(bf16[40,16,128]{2,1,0:T(8,128)(2,1)S(1)} %get-tuple-element.60), channel_id=1, source_target_pairs={{0,4},{4,0},{8,12},{12,8},{16,20},{20,16},{24,28},{28,24},{1,5},{5... | collective-permute-start | bytes 491528 | tf_op jit(solution)/shard_map/ppermute | solution.py:660
  15.3 2.5 %collective-permute-start.5 = (bf16[40,16,128]{2,1,0:T(8,128)(2,1)S(1)}, bf16[40,16,128]{2,1,0:T(8,128)(2,1)S(1)}, u32[]{:S(2)}, u32[]{:S(2)}) collective-permute-start(bf16[40,16,128]{2,1,0:T(8,128)(2,1)S(1)} %get-tuple-element.61), channel_id=1, source_target_pairs={{0,12},{4,8},{8,4},{12,0},{16,28},{20,24},{24,20},{28,16},{1,13},{... | collective-permute-start | bytes 491528 | tf_op jit(solution)/shard_map/ppermute | solution.py:660
  17.8 0.0 copy-start.4
  17.8 2.4 %collective-permute-start.6 = (bf16[40,16,128]{2,1,0:T(8,128)(2,1)S(1)}, bf16[40,16,128]{2,1,0:T(8,128)(2,1)S(1)}, u32[]{:S(2)}, u32[]{:S(2)}) collective-permute-start(bf16[40,16,128]{2,1,0:T(8,128)(2,1)S(1)} %get-tuple-element.62), channel_id=1, source_target_pairs={{0,28},{4,24},{8,20},{12,16},{16,12},{20,8},{24,4},{28,0},{1,29},{... | collective-permute-start | bytes 491528 | tf_op jit(solution)/shard_map/ppermute | solution.py:660
  20.2 0.0 collective-permute-done.2.refs_1_.refs_6_
  20.2 1.3 %collective-permute-start.8 = (bf16[34,16,128]{2,1,0:T(8,128)(2,1)S(1)}, bf16[34,16,128]{2,1,0:T(8,128)(2,1)S(1)}, u32[]{:S(2)}, u32[]{:S(2)}) collective-permute-start(bf16[34,16,128]{2,1,0:T(8,128)(2,1)S(1)} %get-tuple-element.66), channel_id=1, source_target_pairs={{0,24},{4,28},{8,16},{12,20},{16,8},{20,12},{24,0},{28,4},{1,25},{... | collective-permute-start | bytes 417800 | tf_op jit(solution)/shard_map/ppermute | solution.py:660
  21.6 0.0 copy-done.3
  21.6 0.0 copy-done
  21.6 0.0 copy-done.1
  21.6 0.0 copy-done.2
  21.6 0.0 copy-done.4
  21.6 3.4 %sweep.1 = (f32[2,288,384]{2,1,0:T(8,128)S(1)}, f32[2,288,384]{2,1,0:T(8,128)S(1)}, f32[2,256,256]{2,1,0:T(8,128)S(1)}, f32[2,256,256]{2,1,0:T(8,128)S(1)}, f32[...) custom-call(s32[2,2]{1,0:T(2,128)S(1)} %copy-done.4, bf16[2,256,256]{2,1,0:T(8,128)(2,1)S(1)} %copy-done, ...), custom_call_target="tpu_custom_call" | custom-call | tf_op jit(solution)/shard_map/sweep/pallas_call | solution.py:713
  25.0 0.0 collective-permute-done.3.refs_2_.refs_5_
  25.0 0.1 collective-permute-start.7
  25.1 0.0 collective-permute-done.4.refs_3_.refs_0_.refs_2_
  25.1 3.9 %collective-permute-start.9 = (bf16[1,16,128]{2,1,0:T(8,128)(2,1)S(1)}, bf16[1,16,128]{2,1,0:T(8,128)(2,1)S(1)}, u32[]{:S(2)}, u32[]{:S(2)}) collective-permute-start(bf16[1,16,128]{2,1,0:T(8,128)(2,1)S(1)} %get-tuple-element.68), channel_id=1, source_target_pairs={{0,20},{4,16},{8,28},{12,24},{16,4},{20,0},{24,12},{28,8},{1,21},{... | collective-permute-start | bytes 12296 | tf_op jit(solution)/shard_map/ppermute | solution.py:660
  29.1 0.0 collective-permute-done.5.refs_4_.refs_1_
  29.1 0.9 %collective-permute-start.10 = (bf16[1,16,128]{2,1,0:T(8,128)(2,1)S(1)}, bf16[1,16,128]{2,1,0:T(8,128)(2,1)S(1)}, u32[]{:S(2)}, u32[]{:S(2)}) collective-permute-start(bf16[1,16,128]{2,1,0:T(8,128)(2,1)S(1)} %get-tuple-element.70), channel_id=1, source_target_pairs={{0,16},{4,20},{8,24},{12,28},{16,0},{20,4},{24,8},{28,12},{1,17},{... | collective-permute-start | bytes 12296 | tf_op jit(solution)/shard_map/ppermute | solution.py:660
  30.0 0.0 collective-permute-done.6.refs_5_.refs_2_.refs_8_
  30.0 0.7 %part.1.refs_0_ = f32[16,4,16,128]{3,2,1,0:T(8,128)S(1)} custom-call(bf16[34,16,128]{2,1,0:T(8,128)(2,1)S(1)} %get-tuple-element.59.refs_0_.refs_1_, bf16[33,16,128]{2,1,0:T(8,128)(2,1)S(1)} %collective-permute-done.2.refs_1_.refs_6_, bf16[33,16,128]{2,1,0:T(8,128)(2,1)S(1)} %collective-permute-done.3.refs_2_.refs_5_, ...), custom_call_target="tpu_custom_call" | custom-call | tf_op jit(solution)/shard_map/part/pallas_call | solution.py:738
  30.7 0.5 %trim.1 = (f32[2,288,384]{2,1,0:T(8,128)S(1)}, f32[2,288,384]{2,1,0:T(8,128)S(1)}, f32[2,256,256]{2,1,0:T(8,128)S(1)}, f32[2,256,256]{2,1,0:T(8,128)S(1)}, f32[2...) custom-call(bf16[40,16,128]{2,1,0:T(8,128)(2,1)S(1)} %collective-per, ...), custom_call_target="tpu_custom_call", output_to_operand_aliasing={{0}: (4, {}), {1}: (5, {}), {2}: (6, {}), {3}: (7, {}), {4}... | custom-call | tf_op jit(solution)/shard_map/trim/pallas_call | solution.py:726
  31.2 0.3 collective-permute-done.9.refs_9_
  31.5 2.0 %collective-permute-done.10.refs_10_ = bf16[1,16,128]{2,1,0:T(8,128)(2,1)S(1)} collective-permute-done((bf16[1,16,128]{2,1,0:T(8,128)(2,1)S(1)}, bf16[1,16,128]{2,1,0:T(8,128)(2,1)S(1)}, u32[]{:S(2)}, u32[]{:S(2)}) %collective-permute-start.10) | collective-permute-done | bytes 4128 | tf_op jit(solution)/shard_map/ppermute | solution.py:660
  33.6 0.0 collective-permute-done.8.refs_7_
  33.6 0.0 collective-permute-done.7.refs_3_
  33.6 2.5 %final.1 = f32[256,256]{1,0:T(8,128)} custom-call(f32[16,4,16,128]{3,2,1,0:T(8,128)S(1)} %part.1.refs_0_, bf16[34,16,128]{2,1,0:T(8,128)(2,1)S(1)} %get-tuple-element.59.refs_0_.refs_1_, bf16[40,16,128]{2,1,0:T(8,128)(2,1)S(1)} %collective-permute-done.4.refs_3_.refs_0_.refs_2_, bf16[34,16,128]{2,1,0:T(8,128)(2,1)S(1)} %collective-permute-done.7.refs_3_, ...), custom_call_target="tpu_custom_call" | custom-call | tf_op jit(solution)/shard_map/final/pallas_call | solution.py:747
Async XLA Ops:
  2.3 17.9 %collective-permute-start.2 = (bf16[33,16,128]{2,1,0:T(8,128)(2,1)S(1)}, bf16[33,16,128]{2,1,0:T(8,128)(2,1)S(1)}, u32[]{:S(2)}, u32[]{:S(2)}) collective-permute-start(bf16[33,16,128]{2,1,0:T(8,128)(2,1)S(1)} %get-tuple-element.56), channel_id=1, source_target_pairs={{0,20},{4,16},{8,28},{12,24},{16,4},{20,0},{24,12},{28,8},{1,21},{... | collective-permute-start | bytes 405512 | tf_op jit(solution)/shard_map/ppermute | solution.py:660
  5.9 19.1 %collective-permute-start.3 = (bf16[33,16,128]{2,1,0:T(8,128)(2,1)S(1)}, bf16[33,16,128]{2,1,0:T(8,128)(2,1)S(1)}, u32[]{:S(2)}, u32[]{:S(2)}) collective-permute-start(bf16[33,16,128]{2,1,0:T(8,128)(2,1)S(1)} %get-tuple-element.44), channel_id=1, source_target_pairs={{0,16},{4,20},{8,24},{12,28},{16,0},{20,4},{24,8},{28,12},{1,17},{... | collective-permute-start | bytes 405512 | tf_op jit(solution)/shard_map/ppermute | solution.py:660
  6.3 15.3 %copy-start.3 = (bf16[2,256,256]{2,1,0:T(8,128)(2,1)S(1)}, bf16[2,256,256]{2,1,0:T(8,128)(2,1)}, u32[]{:S(2)}) copy-start(bf16[2,256,256]{2,1,0:T(8,128)(2,1)} %drive.1) | copy-start | bytes 786436
  8.9 2.6 %collective-permute-start = (f32[48,256]{1,0:T(8,128)S(1)}, f32[48,256]{1,0:T(8,128)S(1)}, u32[]{:S(2)}, u32[]{:S(2)}) collective-permute-start(f32[48,256]{1,0:T(8,128)S(1)} %get-tuple-element.46), channel_id=1, source_target_pairs={{0,1},{1,0},{2,3},{3,2},{4,5},{5,4},{6,7},{7,6},{8,9},{9,8},{10,11... | collective-permute-start | bytes 147464 | tf_op jit(solution)/shard_map/ppermute | solution.py:43
  9.0 5.4 %collective-permute-start.1 = (f32[48,256]{1,0:T(8,128)S(1)}, f32[48,256]{1,0:T(8,128)S(1)}, u32[]{:S(2)}, u32[]{:S(2)}) collective-permute-start(f32[48,256]{1,0:T(8,128)S(1)} %get-tuple-element.47), channel_id=1, source_target_pairs={{1,2},{2,1},{5,6},{6,5},{9,10},{10,9},{13,14},{14,13},{17,18},{18,... | collective-permute-start | bytes 147464 | tf_op jit(solution)/shard_map/ppermute | solution.py:43
  14.4 7.1 %copy-start = (bf16[2,256,256]{2,1,0:T(8,128)(2,1)S(1)}, bf16[2,256,256]{2,1,0:T(8,128)(2,1)}, u32[]{:S(2)}) copy-start(bf16[2,256,256]{2,1,0:T(8,128)(2,1)} %vel.1) | copy-start | bytes 786436
  14.4 7.1 %copy-start.1 = (f32[256,256]{1,0:T(8,128)S(1)}, f32[256,256]{1,0:T(8,128)}, u32[]{:S(2)}) copy-start(f32[256,256]{1,0:T(8,128)} %visc.1) | copy-start | bytes 786436
  14.4 7.1 %copy-start.2 = (f32[256,256]{1,0:T(8,128)S(1)}, f32[256,256]{1,0:T(8,128)}, u32[]{:S(2)}) copy-start(f32[256,256]{1,0:T(8,128)} %fric.1) | copy-start | bytes 786436
  14.7 10.5 %collective-permute-start.4 = (bf16[40,16,128]{2,1,0:T(8,128)(2,1)S(1)}, bf16[40,16,128]{2,1,0:T(8,128)(2,1)S(1)}, u32[]{:S(2)}, u32[]{:S(2)}) collective-permute-start(bf16[40,16,128]{2,1,0:T(8,128)(2,1)S(1)} %get-tuple-element.60), channel_id=1, source_target_pairs={{0,4},{4,0},{8,12},{12,8},{16,20},{20,16},{24,28},{28,24},{1,5},{5... | collective-permute-start | bytes 491528 | tf_op jit(solution)/shard_map/ppermute | solution.py:660
  15.3 13.8 %collective-permute-start.5 = (bf16[40,16,128]{2,1,0:T(8,128)(2,1)S(1)}, bf16[40,16,128]{2,1,0:T(8,128)(2,1)S(1)}, u32[]{:S(2)}, u32[]{:S(2)}) collective-permute-start(bf16[40,16,128]{2,1,0:T(8,128)(2,1)S(1)} %get-tuple-element.61), channel_id=1, source_target_pairs={{0,12},{4,8},{8,4},{12,0},{16,28},{20,24},{24,20},{28,16},{1,13},{... | collective-permute-start | bytes 491528 | tf_op jit(solution)/shard_map/ppermute | solution.py:660
  17.8 3.8 %copy-start.4 = (s32[2,2]{1,0:T(2,128)S(1)}, s32[2,2]{1,0:T(2,128)}, u32[]{:S(2)}) copy-start(s32[2,2]{1,0:T(2,128)} %ice.1) | copy-start | bytes 52
  17.8 12.2 %collective-permute-start.6 = (bf16[40,16,128]{2,1,0:T(8,128)(2,1)S(1)}, bf16[40,16,128]{2,1,0:T(8,128)(2,1)S(1)}, u32[]{:S(2)}, u32[]{:S(2)}) collective-permute-start(bf16[40,16,128]{2,1,0:T(8,128)(2,1)S(1)} %get-tuple-element.62), channel_id=1, source_target_pairs={{0,28},{4,24},{8,20},{12,16},{16,12},{20,8},{24,4},{28,0},{1,29},{... | collective-permute-start | bytes 491528 | tf_op jit(solution)/shard_map/ppermute | solution.py:660
  20.2 13.4 %collective-permute-start.8 = (bf16[34,16,128]{2,1,0:T(8,128)(2,1)S(1)}, bf16[34,16,128]{2,1,0:T(8,128)(2,1)S(1)}, u32[]{:S(2)}, u32[]{:S(2)}) collective-permute-start(bf16[34,16,128]{2,1,0:T(8,128)(2,1)S(1)} %get-tuple-element.66), channel_id=1, source_target_pairs={{0,24},{4,28},{8,16},{12,20},{16,8},{20,12},{24,0},{28,4},{1,25},{... | collective-permute-start | bytes 417800 | tf_op jit(solution)/shard_map/ppermute | solution.py:660
  25.0 8.6 %collective-permute-start.7 = (bf16[34,16,128]{2,1,0:T(8,128)(2,1)S(1)}, bf16[34,16,128]{2,1,0:T(8,128)(2,1)S(1)}, u32[]{:S(2)}, u32[]{:S(2)}) collective-permute-start(bf16[34,16,128]{2,1,0:T(8,128)(2,1)S(1)} %get-tuple-element.64), channel_id=1, source_target_pairs={{0,8},{4,12},{8,0},{12,4},{16,24},{20,28},{24,16},{28,20},{1,9},{5... | collective-permute-start | bytes 417800 | tf_op jit(solution)/shard_map/ppermute | solution.py:660
  25.1 6.4 %collective-permute-start.9 = (bf16[1,16,128]{2,1,0:T(8,128)(2,1)S(1)}, bf16[1,16,128]{2,1,0:T(8,128)(2,1)S(1)}, u32[]{:S(2)}, u32[]{:S(2)}) collective-permute-start(bf16[1,16,128]{2,1,0:T(8,128)(2,1)S(1)} %get-tuple-element.68), channel_id=1, source_target_pairs={{0,20},{4,16},{8,28},{12,24},{16,4},{20,0},{24,12},{28,8},{1,21},{... | collective-permute-start | bytes 12296 | tf_op jit(solution)/shard_map/ppermute | solution.py:660
  29.1 4.5 %collective-permute-start.10 = (bf16[1,16,128]{2,1,0:T(8,128)(2,1)S(1)}, bf16[1,16,128]{2,1,0:T(8,128)(2,1)S(1)}, u32[]{:S(2)}, u32[]{:S(2)}) collective-permute-start(bf16[1,16,128]{2,1,0:T(8,128)(2,1)S(1)} %get-tuple-element.70), channel_id=1, source_target_pairs={{0,16},{4,20},{8,24},{12,28},{16,0},{20,4},{24,8},{28,12},{1,17},{... | collective-permute-start | bytes 12296 | tf_op jit(solution)/shard_map/ppermute | solution.py:660

commit v8 on v7

--- a/solution.py
+++ b/solution.py
@@ -733,7 +733,7 @@
         compiler_params=limit,
         name="trim",
     )(*near, strips, *base)
-    summed = (0, *early, *halo_steps(groups))
+    summed = (0, *early, *halo_steps(groups), 2)
     slots = cells_x // tile * (cells_y // tile)
     partial = pl.pallas_call(
         functools.partial(part_kernel, slots, tile),

time: 36.3 us -> 43.1 us (1.19)
  the two profiles are of different devices: /device:TPU:4 before, /device:TPU:1 now
where the time goes in v8:
time: 43.1 us; the launch traced here: 42.8 us
  starting transfers between devices  17.8 us (41%)
  Pallas kernels  12.5 us (29%)
  waiting for transfers between devices  12.4 us (29%)
    ppermute x9, starting transfers between devices, move(): return lax.ppermute(after(value, *others) if others else value, 'gx', pairs)  13.2 us
    ppermute x9, waiting for transfers between devices, move(): return lax.ppermute(after(value, *others) if others else value, 'gx', pairs)  10.3 us
    ppermute x2, starting transfers between devices, swap(): return (lax.ppermute(even, 'gy', near), lax.ppermute(odd, 'gy', far))  4.62 us
    pallas_call x1, Pallas kernels, body(): pl.pallas_call(functools.partial(sweep_kernel, tile), out_shape=base_shap...  3.49 us
    pallas_call x1, Pallas kernels, body(): pl.pallas_call(functools.partial(pack_kernel, groups, count, tile), out_s...  2.67 us
    pallas_call x1, Pallas kernels, body(): pl.pallas_call(functools.partial(final_kernel, groups, tile, early, summe...  2.47 us
    pallas_call x1, Pallas kernels, body(): pl.pallas_call(functools.partial(gather_kernel, groups, count, tile), out...  2.34 us
    ppermute x2, waiting for transfers between devices, swap(): return (lax.ppermute(even, 'gy', near), lax.ppermute(odd, 'gy', far))  2.05 us
  transfers between devices with their start and end apart: 11, of which 3 were waited for; matrix products, arithmetic and copies ran while one was open for 0% of the time, Pallas kernels for 11%

profile of v8, /device:TPU:1, one launch (start us, length us, event | category | flops | bytes accessed | tf_op | source)
XLA Modules:
  0.0 42.8 jit_solution(13616308983912669695)
XLA Ops:
  0.0 2.3 %gather.1 = (bf16[34,16,128]{2,1,0:T(8,128)(2,1)S(1)}, bf16[40,16,128]{2,1,0:T(8,128)(2,1)S(1)}, bf16[34,16,128]{2,1,0:T(8,128)(2,1)S(1)}, bf16[40,16,128]{2,1,0...) custom-call(s32[1,16]{1,0:T(1,128)} %bitcast.4, ...), custom_call_target="tpu_custom_call" | custom-call | tf_op jit(solution)/shard_map/gather/pallas_call | solution.py:667
  2.3 0.0 copy-start.3
  2.4 2.7 %pack.1 = (f32[48,256]{1,0:T(8,128)S(1)}, f32[48,256]{1,0:T(8,128)S(1)}, f32[2,16,256]{2,1,0:T(8,128)S(1)}) custom-call(s32[1,16]{1,0:T(1,128)} %bitcast.5, s32[1,16]{1,0:T(1,128)} %refs_1_.3, bf16[1,16]{1,0:T(2,128)(2,1)} %refs_2_.3, s32[2,2]{1,0:T(2,128)} %ice.1, bf16[16,16,16,128]{3,2,1,0:T(8,128)(2,1)} %bitcast.3, bf16[2,256,256]{2,1,0:T(8,128)(2,1)} %vel.1, ...), custom_call_target="tpu_custom_call" | custom-call | tf_op jit(solution)/shard_map/pack/pallas_call | solution.py:682
  5.0 0.1 collective-permute-start
  5.2 4.5 %collective-permute-start.1 = (f32[48,256]{1,0:T(8,128)S(1)}, f32[48,256]{1,0:T(8,128)S(1)}, u32[]{:S(2)}, u32[]{:S(2)}) collective-permute-start(f32[48,256]{1,0:T(8,128)S(1)} %get-tuple-element.47), channel_id=1, source_target_pairs={{1,2},{2,1},{5,6},{6,5},{9,10},{10,9},{13,14},{14,13},{17,18},{18,... | collective-permute-start | bytes 147464 | tf_op jit(solution)/shard_map/ppermute | solution.py:43
  9.7 0.0 collective-permute-done.refs_0_.first
  9.7 2.0 %collective-permute-done.1.refs_1_.then = f32[48,256]{1,0:T(8,128)S(1)} collective-permute-done((f32[48,256]{1,0:T(8,128)S(1)}, f32[48,256]{1,0:T(8,128)S(1)}, u32[]{:S(2)}, u32[]{:S(2)}) %collective-permute-start.1) | collective-permute-done | bytes 49184 | tf_op jit(solution)/shard_map/ppermute | solution.py:43
  11.7 0.0 copy-start
  11.7 0.0 copy-start.1
  11.7 0.0 copy-start.2
  11.7 0.2 widen.1
  11.9 1.9 %collective-permute-start.4 = (bf16[40,16,128]{2,1,0:T(8,128)(2,1)S(1)}, bf16[40,16,128]{2,1,0:T(8,128)(2,1)S(1)}, u32[]{:S(2)}, u32[]{:S(2)}) collective-permute-start(bf16[40,16,128]{2,1,0:T(8,128)(2,1)S(1)} %get-tuple-element.60), channel_id=1, source_target_pairs={{0,4},{4,0},{8,12},{12,8},{16,20},{20,16},{24,28},{28,24},{1,5},{5... | collective-permute-start | bytes 491528 | tf_op jit(solution)/shard_map/ppermute | solution.py:660
  13.8 2.3 %collective-permute-start.2 = (bf16[33,16,128]{2,1,0:T(8,128)(2,1)S(1)}, bf16[33,16,128]{2,1,0:T(8,128)(2,1)S(1)}, u32[]{:S(2)}, u32[]{:S(2)}) collective-permute-start(bf16[33,16,128]{2,1,0:T(8,128)(2,1)S(1)} %get-tuple-element.56), channel_id=1, source_target_pairs={{0,20},{4,16},{8,28},{12,24},{16,4},{20,0},{24,12},{28,8},{1,21},{... | collective-permute-start | bytes 405512 | tf_op jit(solution)/shard_map/ppermute | solution.py:660
  16.1 0.0 copy-start.4
  16.1 2.2 %collective-permute-start.5 = (bf16[40,16,128]{2,1,0:T(8,128)(2,1)S(1)}, bf16[40,16,128]{2,1,0:T(8,128)(2,1)S(1)}, u32[]{:S(2)}, u32[]{:S(2)}) collective-permute-start(bf16[40,16,128]{2,1,0:T(8,128)(2,1)S(1)} %get-tuple-element.61), channel_id=1, source_target_pairs={{0,12},{4,8},{8,4},{12,0},{16,28},{20,24},{24,20},{28,16},{1,13},{... | collective-permute-start | bytes 491528 | tf_op jit(solution)/shard_map/ppermute | solution.py:660
  18.3 0.0 collective-permute-start.6
  18.3 5.8 %collective-permute-done.2.refs_1_.refs_6_ = bf16[33,16,128]{2,1,0:T(8,128)(2,1)S(1)} collective-permute-done((bf16[33,16,128]{2,1,0:T(8,128)(2,1)S(1)}, bf16[33,16,128]{2,1,0:T(8,128)(2,1)S(1)}, u32[]{:S(2)}, u32[]{:S(2)}) %collective-permute-start.2) | collective-permute-done | bytes 135200 | tf_op jit(solution)/shard_map/ppermute | solution.py:660
  24.1 0.0 copy-done.3
  24.1 0.0 copy-done
  24.1 0.0 copy-done.1
  24.1 0.0 copy-done.2
  24.2 0.0 copy-done.4
  24.2 3.5 %sweep.1 = (f32[2,288,384]{2,1,0:T(8,128)S(1)}, f32[2,288,384]{2,1,0:T(8,128)S(1)}, f32[2,256,256]{2,1,0:T(8,128)S(1)}, f32[2,256,256]{2,1,0:T(8,128)S(1)}, f32[...) custom-call(s32[2,2]{1,0:T(2,128)S(1)} %copy-done.4, bf16[2,256,256]{2,1,0:T(8,128)(2,1)S(1)} %copy-done, ...), custom_call_target="tpu_custom_call" | custom-call | tf_op jit(solution)/shard_map/sweep/pallas_call | solution.py:713
  27.7 0.3 collective-permute-start.7
  28.0 4.0 %collective-permute-start.8 = (bf16[34,16,128]{2,1,0:T(8,128)(2,1)S(1)}, bf16[34,16,128]{2,1,0:T(8,128)(2,1)S(1)}, u32[]{:S(2)}, u32[]{:S(2)}) collective-permute-start(bf16[34,16,128]{2,1,0:T(8,128)(2,1)S(1)} %get-tuple-element.66), channel_id=1, source_target_pairs={{0,24},{4,28},{8,16},{12,20},{16,8},{20,12},{24,0},{28,4},{1,25},{... | collective-permute-start | bytes 417800 | tf_op jit(solution)/shard_map/ppermute | solution.py:660
  32.0 0.0 collective-permute-done.4.refs_3_.refs_0_.refs_2_
  32.0 0.2 collective-permute-start.3
  32.2 0.0 collective-permute-done.5.refs_4_.refs_1_
  32.2 1.8 %collective-permute-start.9 = (bf16[1,16,128]{2,1,0:T(8,128)(2,1)S(1)}, bf16[1,16,128]{2,1,0:T(8,128)(2,1)S(1)}, u32[]{:S(2)}, u32[]{:S(2)}) collective-permute-start(bf16[1,16,128]{2,1,0:T(8,128)(2,1)S(1)} %get-tuple-element.68), channel_id=1, source_target_pairs={{0,20},{4,16},{8,28},{12,24},{16,4},{20,0},{24,12},{28,8},{1,21},{... | collective-permute-start | bytes 12296 | tf_op jit(solution)/shard_map/ppermute | solution.py:660
  34.1 0.0 collective-permute-done.6.refs_5_.refs_2_.refs_8_
  34.1 0.4 collective-permute-start.10
  34.5 0.5 %trim.1 = (f32[2,288,384]{2,1,0:T(8,128)S(1)}, f32[2,288,384]{2,1,0:T(8,128)S(1)}, f32[2,256,256]{2,1,0:T(8,128)S(1)}, f32[2,256,256]{2,1,0:T(8,128)S(1)}, f32[2...) custom-call(bf16[40,16,128]{2,1,0:T(8,128)(2,1)S(1)} %collective-per, ...), custom_call_target="tpu_custom_call", output_to_operand_aliasing={{0}: (4, {}), {1}: (5, {}), {2}: (6, {}), {3}: (7, {}), {4}... | custom-call | tf_op jit(solution)/shard_map/trim/pallas_call | solution.py:726
  35.0 4.5 %collective-permute-done.3.refs_2_.refs_5_ = bf16[33,16,128]{2,1,0:T(8,128)(2,1)S(1)} collective-permute-done((bf16[33,16,128]{2,1,0:T(8,128)(2,1)S(1)}, bf16[33,16,128]{2,1,0:T(8,128)(2,1)S(1)}, u32[]{:S(2)}, u32[]{:S(2)}) %collective-permute-start.3) | collective-permute-done | bytes 135200 | tf_op jit(solution)/shard_map/ppermute | solution.py:660
  39.5 0.0 collective-permute-done.7.refs_6_.refs_3_
  39.5 0.8 %part.1.refs_0_ = f32[16,4,16,128]{3,2,1,0:T(8,128)S(1)} custom-call(bf16[34,16,128]{2,1,0:T(8,128)(2,1)S(1)} %get-tuple-element.59.refs_0_.refs_1_, bf16[33,16,128]{2,1,0:T(8,128)(2,1)S(1)} %collective-permute-done.2.refs_1_.refs_6_, bf16[33,16,128]{2,1,0:T(8,128)(2,1)S(1)} %collective-permute-done.3.refs_2_.refs_5_, ...), custom_call_target="tpu_custom_call" | custom-call | tf_op jit(solution)/shard_map/part/pallas_call | solution.py:738
  40.3 0.0 collective-permute-done.9.refs_9_
  40.3 0.0 collective-permute-done.10.refs_10_
  40.3 0.0 collective-permute-done.8.refs_7_
  40.3 2.5 %final.1 = f32[256,256]{1,0:T(8,128)} custom-call(f32[16,4,16,128]{3,2,1,0:T(8,128)S(1)} %part.1.refs_0_, bf16[34,16,128]{2,1,0:T(8,128)(2,1)S(1)} %get-tuple-element.59.refs_0_.refs_1_, bf16[40,16,128]{2,1,0:T(8,128)(2,1)S(1)} %collective-permute-done.4.refs_3_.refs_0_.refs_2_, bf16[34,16,128]{2,1,0:T(8,128)(2,1)S(1)} %collective-permute-done.7.refs_6_.refs_3_, ...), custom_call_target="tpu_custom_call" | custom-call | tf_op jit(solution)/shard_map/final/pallas_call | solution.py:747
Async XLA Ops:
  2.3 21.8 %copy-start.3 = (bf16[2,256,256]{2,1,0:T(8,128)(2,1)S(1)}, bf16[2,256,256]{2,1,0:T(8,128)(2,1)}, u32[]{:S(2)}) copy-start(bf16[2,256,256]{2,1,0:T(8,128)(2,1)} %drive.1) | copy-start | bytes 786436
  5.0 4.6 %collective-permute-start = (f32[48,256]{1,0:T(8,128)S(1)}, f32[48,256]{1,0:T(8,128)S(1)}, u32[]{:S(2)}, u32[]{:S(2)}) collective-permute-start(f32[48,256]{1,0:T(8,128)S(1)} %get-tuple-element.46), channel_id=1, source_target_pairs={{0,1},{1,0},{2,3},{3,2},{4,5},{5,4},{6,7},{7,6},{8,9},{9,8},{10,11... | collective-permute-start | bytes 147464 | tf_op jit(solution)/shard_map/ppermute | solution.py:43
  5.2 6.6 %collective-permute-start.1 = (f32[48,256]{1,0:T(8,128)S(1)}, f32[48,256]{1,0:T(8,128)S(1)}, u32[]{:S(2)}, u32[]{:S(2)}) collective-permute-start(f32[48,256]{1,0:T(8,128)S(1)} %get-tuple-element.47), channel_id=1, source_target_pairs={{1,2},{2,1},{5,6},{6,5},{9,10},{10,9},{13,14},{14,13},{17,18},{18,... | collective-permute-start | bytes 147464 | tf_op jit(solution)/shard_map/ppermute | solution.py:43
  11.7 12.4 %copy-start = (bf16[2,256,256]{2,1,0:T(8,128)(2,1)S(1)}, bf16[2,256,256]{2,1,0:T(8,128)(2,1)}, u32[]{:S(2)}) copy-start(bf16[2,256,256]{2,1,0:T(8,128)(2,1)} %vel.1) | copy-start | bytes 786436
  11.7 12.4 %copy-start.1 = (f32[256,256]{1,0:T(8,128)S(1)}, f32[256,256]{1,0:T(8,128)}, u32[]{:S(2)}) copy-start(f32[256,256]{1,0:T(8,128)} %visc.1) | copy-start | bytes 786436
  11.7 12.4 %copy-start.2 = (f32[256,256]{1,0:T(8,128)S(1)}, f32[256,256]{1,0:T(8,128)}, u32[]{:S(2)}) copy-start(f32[256,256]{1,0:T(8,128)} %fric.1) | copy-start | bytes 786436
  11.9 20.1 %collective-permute-start.4 = (bf16[40,16,128]{2,1,0:T(8,128)(2,1)S(1)}, bf16[40,16,128]{2,1,0:T(8,128)(2,1)S(1)}, u32[]{:S(2)}, u32[]{:S(2)}) collective-permute-start(bf16[40,16,128]{2,1,0:T(8,128)(2,1)S(1)} %get-tuple-element.60), channel_id=1, source_target_pairs={{0,4},{4,0},{8,12},{12,8},{16,20},{20,16},{24,28},{28,24},{1,5},{5... | collective-permute-start | bytes 491528 | tf_op jit(solution)/shard_map/ppermute | solution.py:660
  13.8 10.3 %collective-permute-start.2 = (bf16[33,16,128]{2,1,0:T(8,128)(2,1)S(1)}, bf16[33,16,128]{2,1,0:T(8,128)(2,1)S(1)}, u32[]{:S(2)}, u32[]{:S(2)}) collective-permute-start(bf16[33,16,128]{2,1,0:T(8,128)(2,1)S(1)} %get-tuple-element.56), channel_id=1, source_target_pairs={{0,20},{4,16},{8,28},{12,24},{16,4},{20,0},{24,12},{28,8},{1,21},{... | collective-permute-start | bytes 405512 | tf_op jit(solution)/shard_map/ppermute | solution.py:660
  16.1 8.1 %copy-start.4 = (s32[2,2]{1,0:T(2,128)S(1)}, s32[2,2]{1,0:T(2,128)}, u32[]{:S(2)}) copy-start(s32[2,2]{1,0:T(2,128)} %ice.1) | copy-start | bytes 52
  16.1 16.1 %collective-permute-start.5 = (bf16[40,16,128]{2,1,0:T(8,128)(2,1)S(1)}, bf16[40,16,128]{2,1,0:T(8,128)(2,1)S(1)}, u32[]{:S(2)}, u32[]{:S(2)}) collective-permute-start(bf16[40,16,128]{2,1,0:T(8,128)(2,1)S(1)} %get-tuple-element.61), channel_id=1, source_target_pairs={{0,12},{4,8},{8,4},{12,0},{16,28},{20,24},{24,20},{28,16},{1,13},{... | collective-permute-start | bytes 491528 | tf_op jit(solution)/shard_map/ppermute | solution.py:660
  18.3 15.8 %collective-permute-start.6 = (bf16[40,16,128]{2,1,0:T(8,128)(2,1)S(1)}, bf16[40,16,128]{2,1,0:T(8,128)(2,1)S(1)}, u32[]{:S(2)}, u32[]{:S(2)}) collective-permute-start(bf16[40,16,128]{2,1,0:T(8,128)(2,1)S(1)} %get-tuple-element.62), channel_id=1, source_target_pairs={{0,28},{4,24},{8,20},{12,16},{16,12},{20,8},{24,4},{28,0},{1,29},{... | collective-permute-start | bytes 491528 | tf_op jit(solution)/shard_map/ppermute | solution.py:660
  27.7 11.8 %collective-permute-start.7 = (bf16[34,16,128]{2,1,0:T(8,128)(2,1)S(1)}, bf16[34,16,128]{2,1,0:T(8,128)(2,1)S(1)}, u32[]{:S(2)}, u32[]{:S(2)}) collective-permute-start(bf16[34,16,128]{2,1,0:T(8,128)(2,1)S(1)} %get-tuple-element.64), channel_id=1, source_target_pairs={{0,8},{4,12},{8,0},{12,4},{16,24},{20,28},{24,16},{28,20},{1,9},{5... | collective-permute-start | bytes 417800 | tf_op jit(solution)/shard_map/ppermute | solution.py:660
  28.0 12.3 %collective-permute-start.8 = (bf16[34,16,128]{2,1,0:T(8,128)(2,1)S(1)}, bf16[34,16,128]{2,1,0:T(8,128)(2,1)S(1)}, u32[]{:S(2)}, u32[]{:S(2)}) collective-permute-start(bf16[34,16,128]{2,1,0:T(8,128)(2,1)S(1)} %get-tuple-element.66), channel_id=1, source_target_pairs={{0,24},{4,28},{8,16},{12,20},{16,8},{20,12},{24,0},{28,4},{1,25},{... | collective-permute-start | bytes 417800 | tf_op jit(solution)/shard_map/ppermute | solution.py:660
  32.0 7.5 %collective-permute-start.3 = (bf16[33,16,128]{2,1,0:T(8,128)(2,1)S(1)}, bf16[33,16,128]{2,1,0:T(8,128)(2,1)S(1)}, u32[]{:S(2)}, u32[]{:S(2)}) collective-permute-start(bf16[33,16,128]{2,1,0:T(8,128)(2,1)S(1)} %get-tuple-element.44), channel_id=1, source_target_pairs={{0,16},{4,20},{8,24},{12,28},{16,0},{20,4},{24,8},{28,12},{1,17},{... | collective-permute-start | bytes 405512 | tf_op jit(solution)/shard_map/ppermute | solution.py:660
  32.2 8.1 %collective-permute-start.9 = (bf16[1,16,128]{2,1,0:T(8,128)(2,1)S(1)}, bf16[1,16,128]{2,1,0:T(8,128)(2,1)S(1)}, u32[]{:S(2)}, u32[]{:S(2)}) collective-permute-start(bf16[1,16,128]{2,1,0:T(8,128)(2,1)S(1)} %get-tuple-element.68), channel_id=1, source_target_pairs={{0,20},{4,16},{8,28},{12,24},{16,4},{20,0},{24,12},{28,8},{1,21},{... | collective-permute-start | bytes 12296 | tf_op jit(solution)/shard_map/ppermute | solution.py:660
  34.1 6.3 %collective-permute-start.10 = (bf16[1,16,128]{2,1,0:T(8,128)(2,1)S(1)}, bf16[1,16,128]{2,1,0:T(8,128)(2,1)S(1)}, u32[]{:S(2)}, u32[]{:S(2)}) collective-permute-start(bf16[1,16,128]{2,1,0:T(8,128)(2,1)S(1)} %get-tuple-element.70), channel_id=1, source_target_pairs={{0,16},{4,20},{8,24},{12,28},{16,0},{20,4},{24,8},{28,12},{1,17},{... | collective-permute-start | bytes 12296 | tf_op jit(solution)/shard_map/ppermute | solution.py:660
